TPU v7x, 32 devices: a whole 2x2x4 slice. The times are simulated.
32 devices in a mesh: group: 2 (over y), dom: 4 (over z), tm: 4 (over x, core).
Axes of the slice: x: 2, y: 2, z: 4, core: 2. Of those that a mesh axis runs over, the one named last changes fastest.
Arguments:
- state: float32 [192, 2, 4096], P(('group', 'tm'), None, 'dom'), parts along dimension 0, may hold values from 0 to 1
- dir_one: float32 [192, 2, 4096], P(('group', 'tm'), None, 'dom'), parts along dimension 0, may hold values from -6 to 6
- dir_two: float32 [192, 2, 4096], P(('group', 'tm'), None, 'dom'), parts along dimension 0, may hold values from -6 to 6
- feed: float32 [4096], P('dom'), may hold values from 0.02 to 0.5
- kill: float32 [4096], P('dom'), may hold values from 0.02 to 0.5
- tiles: float32 [32, 3, 128, 128], P('dom'), may hold values from -0.3125 to 0.3125
- tile_cols: int32 [32, 3], P('dom'), may hold values from 0 to 15, as said below
- send_rows: int32 [4, 4, 256], P('dom'), may hold values from 0 to 1023, as said below
- send_count: int32 [4, 4], P('dom'), may hold values from 171 to 256, as said below
Outputs:
- residual: float32 [192, 2, 4096], P(('group', 'tm'), None, 'dom'), parts along dimension 0
- jvp_one: float32 [192, 2, 4096], P(('group', 'tm'), None, 'dom'), parts along dimension 0
- jvp_two: float32 [192, 2, 4096], P(('group', 'tm'), None, 'dom'), parts along dimension 0
There are 2 independent parts, one for each index of `group`. A program takes and returns all parts, laid end to end along the dimension named above; an argument that names none is the same for every part. Nothing has to cross between parts.
Inputs may be any that keep to these rules, and one draw needn't show every extreme that they name: `tile_cols`: column blocks below 8 are the partition's own blocks; 8 + j * 2 + b is block b of received slot j. Every received block is named by some tile of its partition. `send_rows`: entries are local cells of the sending partition; entries at or past the list's count are not read. `send_count`: some list is full in every draw.
All inputs are finite; a program needn't handle non-finite values.
Results may differ from a plain program's by a relative error of at most 0.0003.
Values sent between devices are 32-bit elements; how exact they have to be, the bound alone decides.
No kernel may reach another device: no remote copies, remote signals or barrier semaphores. Data moves between devices by JAX's collectives and lax.ppermute only.
A program may use at most 64 MiB of HBM per device.

v0:
```python
import jax
import jax.numpy as jnp
from jax import lax
from jax.sharding import PartitionSpec as P

OFFSETS = (1, -1, 2, -2)
time_step = 0.5
spread_u = 1.0
spread_v = 0.5


def from_behind(block, axis, distance):
    devices = range(lax.axis_size(axis))
    route = [((i - distance) % len(devices), i) for i in devices]
    return lax.ppermute(block, axis, route)


def laplace(flat, tiles, tile_cols, send_rows, send_count):
    channels, cell_count = flat.shape
    blocks = tiles.shape[0]
    row_slots = send_rows.shape[2]
    pieces = [flat]
    for slot, offset in enumerate(OFFSETS):
        values = jnp.take(flat, send_rows[0, slot], axis=1)
        live = jnp.arange(row_slots) < send_count[0, slot]
        outgoing = jnp.where(live[None, :], values, jnp.zeros_like(values))
        pieces.append(from_behind(outgoing, "dom", offset))
    extended = jnp.concatenate(pieces, axis=1).reshape(channels, -1, 128)
    chosen = extended[:, tile_cols]
    result = jnp.einsum("rkij,crkj->cri", tiles, chosen, precision=lax.Precision.HIGHEST)
    return result.reshape(channels, blocks * 128)


def tendency(stacked, lap, feed, kill):
    conc_u = stacked[:, 0]
    conc_v = stacked[:, 1]
    square_v = conc_v * conc_v
    product_uv = conc_u * square_v
    outs = [
        spread_u * lap[:, 0] - product_uv + feed * (1.0 - conc_u),
        spread_v * lap[:, 1] + product_uv - (feed + kill) * conc_v,
    ]
    for first in (2, 4):
        delta_u = stacked[:, first]
        delta_v = stacked[:, first + 1]
        react = square_v * delta_u + 2.0 * conc_u * conc_v * delta_v
        outs.append(spread_u * lap[:, first] - react - feed * delta_u)
        outs.append(spread_v * lap[:, first + 1] + react - (feed + kill) * delta_v)
    return jnp.stack(outs, axis=1)


def per_device(state, dir_one, dir_two, feed, kill, tiles, tile_cols, send_rows, send_count):
    stacked = jnp.concatenate([state, dir_one, dir_two], axis=1)
    cell_count = stacked.shape[2]
    lap = laplace(stacked.reshape(-1, cell_count), tiles, tile_cols, send_rows, send_count)
    tendencies = tendency(stacked, lap.reshape(stacked.shape), feed, kill)
    boundary_state, boundary_rate = from_behind((stacked[-1], tendencies[-1]), "tm", 1)
    earlier = jnp.concatenate([boundary_state[None], stacked[:-1]], axis=0)
    rate_earlier = jnp.concatenate([boundary_rate[None], tendencies[:-1]], axis=0)
    result = (stacked - earlier) / time_step - 0.5 * (tendencies + rate_earlier)
    return (result[:, 0:2], result[:, 2:4], result[:, 4:6])


def solution(mesh):
    in_specs = (
        P(("group", "tm"), None, "dom"),
        P(("group", "tm"), None, "dom"),
        P(("group", "tm"), None, "dom"),
        P("dom"),
        P("dom"),
        P("dom", None, None, None),
        P("dom", None),
        P("dom", None, None),
        P("dom", None),
    )
    out_specs = (
        P(("group", "tm"), None, "dom"),
        P(("group", "tm"), None, "dom"),
        P(("group", "tm"), None, "dom"),
    )
    return jax.shard_map(
        per_device, mesh=mesh, in_specs=in_specs, out_specs=out_specs, check_vma=False
    )
```

profile of v0, /device:TPU:0, one launch (start us, length us, event | category | flops | bytes accessed | tf_op | source)
XLA Modules:
  0.0 72.7 jit_solution(14746991395514813381)
XLA Ops:
  0.7 1.1 %fusion.22 = (f32[24,2,1024]{2,0,1:T(8,128)S(1)}, f32[24,6,1024]{2,0,1:T(8,128)S(1)}) fusion(f32[24,2,1024]{2,1,0:T(2,128)} %param.11), kind=kLoop, calls=%fused_computation.74 | loop fusion | bytes 589824 | tf_op args[0]
  1.8 1.7 %fusion.21 = (f32[24,2,1024]{2,0,1:T(8,128)}, f32[24,6,1024]{2,0,1:T(8,128)S(1)}) fusion(f32[24,2,1024]{2,1,0:T(2,128)} %param.12, f32[24,6,1024]{2,0,1:T(8,128)S(1)} %get-tuple-element.25), kind=kLoop, calls=%fused_computation.73 | loop fusion | bytes 589824 | tf_op args[1]
  3.5 0.7 %fusion.20 = (f32[24,2,1024]{2,0,1:T(8,128)}, f32[24,6,1024]{2,0,1:T(8,128)S(1)}) fusion(f32[24,2,1024]{2,1,0:T(2,128)S(1)} %copy-done.3, f32[24,6,1024]{2,0,1:T(8,128)S(1)} %get-tuple-element.23), kind=kLoop, calls=%fused_computation.72 | loop fusion | bytes 589824 | tf_op args[2]
  7.0 0.9 %reshape.61 = f32[144,1024]{1,0:T(8,128)} reshape(f32[24,6,1024]{2,1,0:T(8,128)S(1)} %copy.51) | data formatting | bytes 1179648 | tf_op jit(solution)/shard_map/reshape | solution.py:55
  7.9 1.4 %copy.52 = f32[144,1024]{0,1:T(8,128)S(1)} copy(f32[144,1024]{1,0:T(8,128)} %reshape.61) | data formatting | bytes 1179648 | tf_op jit(solution)/shard_map/reshape | solution.py:55
  9.3 1.7 %gather_fusion.2 = f32[256,144]{1,0:T(8,128)} fusion(f32[144,1024]{0,1:T(8,128)S(1)} %copy.52, s32[1024]{0:T(1024)S(1)} %get-tuple-element.37), kind=kCustom, calls=%fused_computation.1.clone | custom fusion | bytes 295936 | tf_op jit(solution)/shard_map/jit(_take)/gather | solution.py:24
  11.0 1.8 %bitcast_select_fusion.2 = f32[144,256]{0,1:T(8,128)} fusion(f32[256,144]{1,0:T(8,128)} %gather_fusion.2, pred[256]{0:T(512)(128)(4,1)S(1)} %get-tuple-element.40, pred[256]{0:T(512)(128)(4,1)S(1)} %get-tuple-element.41), kind=kLoop, calls=%fused_computation.14 | loop fusion | flops 73728 | bytes 295424 | tf_op jit(solution)/shard_map/jit(_where)/select_n | solution.py:26
  12.7 4.6 %collective-permute-start.2 = (f32[144,256]{0,1:T(8,128)}, f32[144,256]{0,1:T(8,128)}, u32[]{:S(2)}, u32[]{:S(2)}) collective-permute-start(f32[144,256]{0,1:T(8,128)} %bitcast_select_fusion.2), channel_id=1, source_target_pairs={{4,0},{8,4},{12,8},{0,12},{5,1},{9,5},{13,9},{1,13},{6,2},{10,6},{... | collective-permute-start | bytes 442376 | tf_op jit(solution)/shard_map/ppermute | solution.py:15
  17.9 1.7 %gather_fusion.1 = f32[256,144]{1,0:T(8,128)} fusion(f32[144,1024]{0,1:T(8,128)S(1)} %copy.52, s32[1024]{0:T(1024)S(1)} %pad_clamp_fusion.4), kind=kCustom, calls=%fused_computation.clone | custom fusion | bytes 295936 | tf_op jit(solution)/shard_map/jit(_take)/gather | solution.py:24
  19.6 1.8 %bitcast_select_fusion.3 = f32[144,256]{0,1:T(8,128)} fusion(f32[256,144]{1,0:T(8,128)} %gather_fusion.1, pred[256]{0:T(512)(128)(4,1)S(1)} %get-tuple-element.38, pred[256]{0:T(512)(128)(4,1)S(1)} %get-tuple-element.39), kind=kLoop, calls=%fused_computation.15 | loop fusion | flops 73728 | bytes 295424 | tf_op jit(solution)/shard_map/jit(_where)/select_n | solution.py:26
  22.1 1.7 %gather_fusion.3 = f32[256,144]{1,0:T(8,128)} fusion(f32[144,1024]{0,1:T(8,128)S(1)} %copy.52, s32[1024]{0:T(1024)S(1)} %get-tuple-element.36), kind=kCustom, calls=%fused_computation.2.clone | custom fusion | bytes 295936 | tf_op jit(solution)/shard_map/jit(_take)/gather | solution.py:24
  23.7 1.8 %bitcast_select_fusion.1 = f32[144,256]{0,1:T(8,128)} fusion(f32[256,144]{1,0:T(8,128)} %gather_fusion.3, pred[256]{0:T(512)(128)(4,1)S(1)} %get-tuple-element.42, pred[256]{0:T(512)(128)(4,1)S(1)} %get-tuple-element.43), kind=kLoop, calls=%fused_computation.13 | loop fusion | flops 73728 | bytes 295424 | tf_op jit(solution)/shard_map/jit(_where)/select_n | solution.py:26
  25.5 1.0 %collective-permute-start.3 = (f32[144,256]{0,1:T(8,128)}, f32[144,256]{0,1:T(8,128)}, u32[]{:S(2)}, u32[]{:S(2)}) collective-permute-start(f32[144,256]{0,1:T(8,128)} %bitcast_select_fusion.1), channel_id=1, source_target_pairs={{8,0},{12,4},{0,8},{4,12},{9,1},{13,5},{1,9},{5,13},{10,2},{14,6},... | collective-permute-start | bytes 442376 | tf_op jit(solution)/shard_map/ppermute | solution.py:15
  27.3 1.7 %gather_fusion.4 = f32[256,144]{1,0:T(8,128)} fusion(f32[144,1024]{0,1:T(8,128)S(1)} %copy.52, s32[1024]{0:T(1024)S(1)} %get-tuple-element.35), kind=kCustom, calls=%fused_computation.3.clone | custom fusion | bytes 295936 | tf_op jit(solution)/shard_map/jit(_take)/gather | solution.py:24
  29.0 1.1 %bitcast_select_fusion = f32[144,256]{0,1:T(8,128)S(1)} fusion(f32[256,144]{1,0:T(8,128)} %gather_fusion.4, pred[256]{0:T(512)(128)(4,1)S(1)} %get-tuple-element.44, pred[256]{0:T(512)(128)(4,1)S(1)} %get-tuple-element.45), kind=kLoop, calls=%fused_computation.12 | loop fusion | flops 73728 | bytes 295424 | tf_op jit(solution)/shard_map/jit(_where)/select_n | solution.py:26
  30.1 2.0 %collective-permute-start.4 = (f32[144,256]{0,1:T(8,128)S(1)}, f32[144,256]{0,1:T(8,128)S(1)}, u32[]{:S(2)}, u32[]{:S(2)}) collective-permute-start(f32[144,256]{0,1:T(8,128)S(1)} %bitcast_select_fusion), channel_id=1, source_target_pairs={{8,0},{12,4},{0,8},{4,12},{9,1},{13,5},{1,9},{5,13},{10,2},{14,6},... | collective-permute-start | bytes 442376 | tf_op jit(solution)/shard_map/ppermute | solution.py:15
  32.1 2.0 %constant_dynamic-update-slice_fusion.7 = f32[144,2048]{1,0:T(8,128)} fusion(f32[144,1024]{1,0:T(8,128)} %reshape.61), kind=kLoop, calls=%fused_computation.51 | loop fusion | bytes 1179648
  34.1 1.0 %copy.56 = f32[144,256]{1,0:T(8,128)S(1)} copy(f32[144,256]{0,1:T(8,128)} %collective-permute-done.1) | data formatting | bytes 294912 | tf_op jit(solution)/shard_map/ppermute | solution.py:15
  35.9 1.0 %copy.57 = f32[144,256]{1,0:T(8,128)S(1)} copy(f32[144,256]{0,1:T(8,128)} %collective-permute-done.2) | data formatting | bytes 294912 | tf_op jit(solution)/shard_map/ppermute | solution.py:15
  37.7 11.9 %collective-permute-done.3 = f32[144,256]{0,1:T(8,128)} collective-permute-done((f32[144,256]{0,1:T(8,128)}, f32[144,256]{0,1:T(8,128)}, u32[]{:S(2)}, u32[]{:S(2)}) %collective-permute-start.3) | collective-permute-done | bytes 147488 | tf_op jit(solution)/shard_map/ppermute | solution.py:15
  49.5 1.0 %copy.58 = f32[144,256]{1,0:T(8,128)S(1)} copy(f32[144,256]{0,1:T(8,128)} %collective-permute-done.3) | data formatting | bytes 294912 | tf_op jit(solution)/shard_map/ppermute | solution.py:15
  51.3 3.8 %collective-permute-done.4 = f32[144,256]{0,1:T(8,128)S(1)} collective-permute-done((f32[144,256]{0,1:T(8,128)S(1)}, f32[144,256]{0,1:T(8,128)S(1)}, u32[]{:S(2)}, u32[]{:S(2)}) %collective-permute-start.4) | collective-permute-done | bytes 147488 | tf_op jit(solution)/shard_map/ppermute | solution.py:15
  55.9 1.3 %copy_bitcast_fusion = f32[144,16,128]{2,0,1:T(8,128)S(1)} fusion(f32[144,2048]{1,0:T(8,128)} %constant_dynamic-update-slice_fusion.3), kind=kLoop, calls=%fused_computation.6 | loop fusion | bytes 2359296 | tf_op jit(solution)/shard_map/reshape | solution.py:28
  57.2 1.9 %gather_fusion = f32[24,144,128]{2,1,0:T(8,128)} fusion(f32[144,16,128]{2,0,1:T(8,128)S(1)} %copy_bitcast_fusion, s32[1024]{0:T(1024)S(1)} %get-tuple-element.34), kind=kCustom, calls=%fused_computation.4 | custom fusion | bytes 3539040 | tf_op jit(solution)/shard_map/gather | solution.py:29
  59.1 3.7 %convolution_bitcast_fusion = f32[144,8,128]{2,0,1:T(8,128)S(1)} fusion(f32[144,8,3,128]{3,0,2,1:T(8,128)} %bitcast.40, f32[8,3,128,128]{3,2,1,0:T(8,128)S(1)} %copy-done), kind=kOutput, calls=%fused_computation.5 | convolution fusion | flops 679477248 | bytes 3932160 | tf_op jit(solution)/shard_map/rkij,crkj->cri/dot_general | solution.py:30
  62.8 1.0 %copy.62 = f32[144,8,128]{2,1,0:T(8,128)} copy(f32[144,8,128]{2,0,1:T(8,128)S(1)} %convolution_bitcast_fusion) | data formatting | bytes 1179648 | tf_op jit(solution)/shard_map/rkij,crkj->cri/transpose | solution.py:30
  63.8 1.2 %reshape_reshape.3 = f32[24,6,1024]{2,1,0:T(8,128)S(1)} reshape(f32[144,8,128]{2,1,0:T(8,128)} %copy.62) | data formatting | bytes 1179648 | tf_op jit(solution)/shard_map/reshape;reshape | solution.py:56
  66.6 0.8 %copy.50 = f32[1,6,1024]{2,0,1:T(1,128)S(1)} copy(f32[1,6,1024]{2,1,0:T(8,128)} %bitcast) | data formatting | bytes 49152 | tf_op jit(solution)/shard_map/broadcast_in_dim | solution.py:58
  67.4 2.4 %collective-permute-done.5 = f32[6,1024]{1,0:T(8,128)S(1)} collective-permute-done((f32[6,1024]{1,0:T(8,128)S(1)}, f32[6,1024]{1,0:T(8,128)S(1)}, u32[]{:S(2)}, u32[]{:S(2)}) %collective-permute-start.5) | collective-permute-done | bytes 24608 | tf_op jit(solution)/shard_map/ppermute | solution.py:15
  70.2 0.8 %copy.78 = f32[24,2,1024]{2,1,0:T(2,128)} copy(f32[24,2,1024]{2,0,1:T(8,128)S(1)} %get-tuple-element.17) | data formatting | bytes 393216
  71.1 0.8 %copy.77 = f32[24,2,1024]{2,1,0:T(2,128)} copy(f32[24,2,1024]{2,0,1:T(8,128)S(1)} %get-tuple-element.18) | data formatting | bytes 393216
  71.9 0.8 %copy.76 = f32[24,2,1024]{2,1,0:T(2,128)} copy(f32[24,2,1024]{2,0,1:T(8,128)S(1)} %get-tuple-element.19) | data formatting | bytes 393216
  (61 shorter events, 9.7 us)
Async XLA Ops:
  0.6 58.5 %copy-start = (f32[8,3,128,128]{3,2,1,0:T(8,128)S(1)}, f32[8,3,128,128]{3,2,1,0:T(8,128)}, u32[]{:S(2)}) copy-start(f32[8,3,128,128]{3,2,1,0:T(8,128)} %param.16) | copy-start | bytes 4718596
  0.6 2.8 %copy-start.3 = (f32[24,2,1024]{2,1,0:T(2,128)S(1)}, f32[24,2,1024]{2,1,0:T(2,128)}, u32[]{:S(2)}) copy-start(f32[24,2,1024]{2,1,0:T(2,128)} %param.13) | copy-start | bytes 589828
  3.5 2.2 %copy-start.5 = (s32[1,4]{1,0:T(1,128)S(1)}, s32[1,4]{1,0:T(1,128)}, u32[]{:S(2)}) copy-start(s32[1,4]{1,0:T(1,128)} %param.19) | copy-start | bytes 52
  3.5 2.8 %copy-start.7 = (s32[1,4,256]{2,1,0:T(4,128)S(1)}, s32[1,4,256]{2,1,0:T(4,128)}, u32[]{:S(2)}) copy-start(s32[1,4,256]{2,1,0:T(4,128)} %param.18) | copy-start | bytes 12292
  4.9 61.8 %collective-permute-start = (f32[6,1024]{1,0:T(8,128)}, f32[6,1024]{1,0:T(8,128)}, u32[]{:S(2)}, u32[]{:S(2)}) collective-permute-start(f32[6,1024]{1,0:T(8,128)} %bitcast.37), channel_id=1, source_target_pairs={{3,0},{0,1},{1,2},{2,3},{7,4},{4,5},{5,6},{6,7},{11,8},{8,9},{9,10... | collective-permute-start | bytes 73736 | tf_op jit(solution)/shard_map/ppermute | solution.py:15
  12.7 23.1 %collective-permute-start.2 = (f32[144,256]{0,1:T(8,128)}, f32[144,256]{0,1:T(8,128)}, u32[]{:S(2)}, u32[]{:S(2)}) collective-permute-start(f32[144,256]{0,1:T(8,128)} %bitcast_select_fusion.2), channel_id=1, source_target_pairs={{4,0},{8,4},{12,8},{0,12},{5,1},{9,5},{13,9},{1,13},{6,2},{10,6},{... | collective-permute-start | bytes 442376 | tf_op jit(solution)/shard_map/ppermute | solution.py:15
  19.6 6.9 %copy-start.8 = (s32[8,3]{0,1:T(4,128)S(1)}, s32[8,3]{0,1:T(4,128)}, u32[]{:S(2)}) copy-start(s32[8,3]{0,1:T(4,128)} %param.17) | copy-start | bytes 292
  21.4 12.7 %collective-permute-start.1 = (f32[144,256]{0,1:T(8,128)}, f32[144,256]{0,1:T(8,128)}, u32[]{:S(2)}, u32[]{:S(2)}) collective-permute-start(f32[144,256]{0,1:T(8,128)} %bitcast_select_fusion.3), channel_id=1, source_target_pairs={{12,0},{0,4},{4,8},{8,12},{13,1},{1,5},{5,9},{9,13},{14,2},{2,6},{... | collective-permute-start | bytes 442376 | tf_op jit(solution)/shard_map/ppermute | solution.py:15
  25.5 24.0 %collective-permute-start.3 = (f32[144,256]{0,1:T(8,128)}, f32[144,256]{0,1:T(8,128)}, u32[]{:S(2)}, u32[]{:S(2)}) collective-permute-start(f32[144,256]{0,1:T(8,128)} %bitcast_select_fusion.1), channel_id=1, source_target_pairs={{8,0},{12,4},{0,8},{4,12},{9,1},{13,5},{1,9},{5,13},{10,2},{14,6},... | collective-permute-start | bytes 442376 | tf_op jit(solution)/shard_map/ppermute | solution.py:15
  29.0 5.1 %copy-start.4 = (f32[1024]{0:T(1024)S(1)}, f32[1024]{0:T(1024)}, u32[]{:S(2)}) copy-start(f32[1024]{0:T(1024)} %param.14) | copy-start | bytes 12292
  29.0 5.1 %copy-start.6 = (f32[1024]{0:T(1024)S(1)}, f32[1024]{0:T(1024)}, u32[]{:S(2)}) copy-start(f32[1024]{0:T(1024)} %param.15) | copy-start | bytes 12292
  30.1 24.9 %collective-permute-start.4 = (f32[144,256]{0,1:T(8,128)S(1)}, f32[144,256]{0,1:T(8,128)S(1)}, u32[]{:S(2)}, u32[]{:S(2)}) collective-permute-start(f32[144,256]{0,1:T(8,128)S(1)} %bitcast_select_fusion), channel_id=1, source_target_pairs={{8,0},{12,4},{0,8},{4,12},{9,1},{13,5},{1,9},{5,13},{10,2},{14,6},... | collective-permute-start | bytes 442376 | tf_op jit(solution)/shard_map/ppermute | solution.py:15
  64.9 0.9 %copy-start.2 = (f32[24,2,1024]{2,0,1:T(8,128)S(1)}, f32[24,2,1024]{2,0,1:T(8,128)}, u32[]{:S(2)}) copy-start(f32[24,2,1024]{2,0,1:T(8,128)} %get-tuple-element.22) | copy-start | bytes 589828
  65.4 1.0 %copy-start.1 = (f32[24,2,1024]{2,0,1:T(8,128)S(1)}, f32[24,2,1024]{2,0,1:T(8,128)}, u32[]{:S(2)}) copy-start(f32[24,2,1024]{2,0,1:T(8,128)} %get-tuple-element.20) | copy-start | bytes 589828
  66.5 3.4 %collective-permute-start.5 = (f32[6,1024]{1,0:T(8,128)S(1)}, f32[6,1024]{1,0:T(8,128)S(1)}, u32[]{:S(2)}, u32[]{:S(2)}) collective-permute-start(f32[6,1024]{1,0:T(8,128)S(1)} %bitcast.43), channel_id=1, source_target_pairs={{3,0},{0,1},{1,2},{2,3},{7,4},{4,5},{5,6},{6,7},{11,8},{8,9},{9,10... | collective-permute-start | bytes 73736 | tf_op jit(solution)/shard_map/ppermute | solution.py:15
where the time goes:
time: 73.4 us; the launch traced here: 72.7 us
  local copies, waits for them, and re-layouts  32.3 us (44%)
  waiting for transfers between devices  18.1 us (25%)
  other arithmetic  9.53 us (13%)
  starting transfers between devices  8.21 us (11%)
  matrix products  3.65 us (5%)
  between operations  0.91 us (1%)
    ppermute x6, waiting for transfers between devices, from_behind(): return lax.ppermute(block, axis, route)  18.1 us
    unnamed x30, local copies, waits for them, and re-layouts  11.6 us
    ppermute x6, starting transfers between devices, from_behind(): return lax.ppermute(block, axis, route)  8.21 us
    gather x4, local copies, waits for them, and re-layouts, laplace(): values = jnp.take(flat, send_rows[0, slot], axis=1)  6.66 us
    select_n x4, other arithmetic, laplace(): outgoing = jnp.where(live[None, :], values, jnp.zeros_like(values))  6.49 us
    dot_general x1, matrix products, laplace(): jnp.einsum('rkij,crkj->cri', tiles, chosen, precision=lax.Precision.HIGHEST)  3.65 us
    ppermute x4, local copies, waits for them, and re-layouts, from_behind(): return lax.ppermute(block, axis, route)  3.24 us
    and x4, other arithmetic, laplace(): values = jnp.take(flat, send_rows[0, slot], axis=1)  2.46 us
  transfers between devices with their start and end apart: 6, of which 3 were waited for; matrix products, arithmetic and copies ran while one was open for 52% of the time, Pallas kernels for 0%

commit v1 on v0

v1 whole, which is shorter than its diff:
```python
import functools

import jax
import jax.numpy as jnp
from jax import lax
from jax.experimental import pallas as pl
from jax.experimental.pallas import tpu as pltpu
from jax.sharding import PartitionSpec as P

OFFSETS = (1, -1, 2, -2)
time_step = 0.5
spread_u = 1.0
spread_v = 0.5
LANES = 128
STEPS = 8
FIELDS = 3
CHUNKS = ((1, 2), (0,))
VMEM = pltpu.VMEM
SMEM = pltpu.SMEM
F32 = jnp.float32
BF16 = jnp.bfloat16


def shift_along(block, axis, distance):
    size = lax.axis_size(axis)
    return lax.ppermute(block, axis, [((i - distance) % size, i) for i in range(size)])


def steps_at(ref, group, cell_block, species, stride):
    return ref[pl.ds(group * STEPS * stride + cell_block * 2 + species, STEPS, stride=stride), :]


def steps_before(ref, prev_ref, field, group, cell_block, species, stride):
    offset = cell_block * 2 + species
    if group > 0:
        return ref[pl.ds((group * STEPS - 1) * stride + offset, STEPS, stride=stride), :]
    now = steps_at(ref, 0, cell_block, species, stride)
    row = field * stride + offset
    first = jnp.broadcast_to(prev_ref[row : row + 1, :], now.shape)
    index = lax.broadcasted_iota(jnp.int32, now.shape, 0)
    return jnp.where(index == 0, first, pltpu.roll(now, 1, 0))


def split(values):
    high = values.astype(BF16)
    return high, (values - high.astype(F32)).astype(BF16)


def gather_kernel(chunk, slot_groups, cell_blocks, *refs):
    refs = list(refs)
    fields = [refs.pop(0) for _ in range(FIELDS)]
    prev = refs.pop(0) if 0 in chunk else None
    rows_ref, count_ref = refs.pop(0), refs.pop(0)
    sends = [refs.pop(0) for _ in slot_groups]
    parts_ref = refs.pop(0)
    last = None if 0 in chunk else refs.pop(0)
    (choose,) = refs
    stride = 2 * cell_blocks
    size = len(chunk) * FIELDS * 2 * STEPS
    if last is not None:
        for field in range(FIELDS):
            last[field * stride : (field + 1) * stride, :] = fields[field][-stride:, :]
    for place, group in enumerate(chunk):
        for field in range(FIELDS):
            row = (place * FIELDS + field) * 2 * STEPS
            for block in range(cell_blocks):
                both = []
                for species, scale in enumerate((-0.5 * spread_u, -0.5 * spread_v)):
                    now = steps_at(fields[field], group, block, species, stride)
                    before = steps_before(fields[field], prev, field, group, block, species, stride)
                    both.append((now + before) * scale)
                high, low = split(jnp.concatenate(both, axis=0))
                parts_ref[block, row : row + 2 * STEPS, :] = high
                parts_ref[block, size + row : size + row + 2 * STEPS, :] = low
    slot_rows = rows_ref.shape[1]
    parts = jnp.concatenate([parts_ref[b] for b in range(cell_blocks)], axis=1)
    lane = lax.broadcasted_iota(jnp.int32, (1, slot_rows), 1)
    cell = lax.broadcasted_iota(jnp.int32, (LANES, slot_rows), 0)
    for send, slots in zip(sends, slot_groups):
        for place, slot in enumerate(slots):
            listed = jnp.where(lane < count_ref[slot], rows_ref[slot : slot + 1, :], -1)
            for block in range(cell_blocks):
                hit = cell == listed - block * LANES
                choose[block * LANES : (block + 1) * LANES, :] = jnp.where(hit, 1.0, 0.0).astype(BF16)
            taken = jnp.dot(parts, choose[...], preferred_element_type=F32)
            send[:, place * slot_rows : (place + 1) * slot_rows] = taken[:size] + taken[size:]


def pointwise(u, v, du, dv, ddu, ddv, feed, total):
    square = v * v
    product = u * square
    twice = 2.0 * u * v
    outs = [feed * (1.0 - u) - product, product - total * v]
    for first, second in ((du, dv), (ddu, ddv)):
        react = square * first + twice * second
        outs += [-react - feed * first, react - total * second]
    return outs


def local_kernel(chunks, cell_blocks, *refs):
    refs = list(refs)
    fields = [refs.pop(0) for _ in range(FIELDS)]
    prev, feed_ref, kill_ref, tiles = [refs.pop(0) for _ in range(4)]
    bases = [refs.pop(0) for _ in chunks]
    (split_tiles,) = refs
    stride = 2 * cell_blocks
    for base, chunk in zip(bases, chunks):
        for place, group in enumerate(chunk):
            for block in range(cell_blocks):
                feed = feed_ref[block : block + 1, :]
                total = feed + kill_ref[block : block + 1, :]
                now = [steps_at(fields[f], group, block, s, stride) for f in range(FIELDS) for s in range(2)]
                before = [
                    steps_before(fields[f], prev, f, group, block, s, stride)
                    for f in range(FIELDS)
                    for s in range(2)
                ]
                rate_now = pointwise(*now, feed, total)
                rate_before = pointwise(*before, feed, total)
                for index in range(2 * FIELDS):
                    row = (place * FIELDS * 2 + index) * STEPS
                    base[block, row : row + STEPS, :] = (now[index] - before[index]) * (1.0 / time_step) - 0.5 * (
                        rate_now[index] + rate_before[index]
                    )
    blocks, per_row = tiles.shape[:2]
    for block in range(blocks):
        for k in range(per_row):
            high, low = split(jnp.transpose(tiles[block, k]))
            split_tiles[block, k * LANES : (k + 1) * LANES, :LANES] = high
            split_tiles[block, k * LANES : (k + 1) * LANES, LANES:] = low


def apply_kernel(chunk, slot_groups, cell_blocks, blocks, per_row, first, *refs):
    refs = list(refs)
    cols, split_tiles, base, parts_ref = [refs.pop(0) for _ in range(4)]
    arrived = [refs.pop(0) for _ in slot_groups]
    if not first:
        refs = refs[FIELDS:]
    outs = [refs.pop(0) for _ in range(FIELDS)]
    extended, made, sems = refs
    stride = 2 * cell_blocks
    size = base.shape[1]
    extended[:cell_blocks] = parts_ref[...]
    for ref, slots in zip(arrived, slot_groups):
        per_slot = ref.shape[1] // len(slots) // LANES
        for place, slot in enumerate(slots):
            for b in range(per_slot):
                lane = (place * per_slot + b) * LANES
                high, low = split(ref[:, lane : lane + LANES])
                extended[cell_blocks + slot * per_slot + b, :size, :] = high
                extended[cell_blocks + slot * per_slot + b, size:, :] = low
    for block in range(blocks):
        chosen = jnp.concatenate([extended[cols[k, block]] for k in range(per_row)], axis=1)
        product = jnp.dot(chosen, split_tiles[block], preferred_element_type=F32)
        product = product[:, :LANES] + product[:, LANES:]
        result = base[block] + (product[:size] + product[size:])
        for place in range(len(chunk)):
            for index in range(2 * FIELDS):
                row = (place * FIELDS * 2 + index) * STEPS
                at = place * STEPS * stride + block * 2 + index % 2
                made[index // 2, pl.ds(at, STEPS, stride=stride), :] = result[row : row + STEPS, :]
    span = len(chunk) * STEPS * stride
    copies = [
        pltpu.make_async_copy(made.at[f], outs[f].at[pl.ds(chunk[0] * STEPS * stride, span), :], sems.at[f])
        for f in range(FIELDS)
    ]
    for copy in copies:
        copy.start()
    for copy in copies:
        copy.wait()


def per_device(state, dir_one, dir_two, feed, kill, tiles, tile_cols, send_rows, send_count):
    steps, _, cells = state.shape
    cell_blocks = cells // LANES
    stride = 2 * cell_blocks
    blocks, per_row = tiles.shape[:2]
    slot_rows = send_rows.shape[2]
    size_dom = lax.axis_size("dom")

    by_route = {}
    for slot, offset in enumerate(OFFSETS):
        by_route.setdefault(offset % size_dom, []).append(slot)
    slot_groups = sorted(by_route.values(), key=lambda slots: -len(slots))

    def view(array):
        array = array.reshape(steps, 2, cell_blocks, LANES).transpose(0, 2, 1, 3)
        return array.reshape(steps * stride, LANES)

    def unview(array):
        array = array.reshape(steps, cell_blocks, 2, LANES).transpose(0, 2, 1, 3)
        return array.reshape(steps, 2, cells)

    fields = [view(state), view(dir_one), view(dir_two)]
    rows = send_rows.reshape(send_rows.shape[1:])
    counts = send_count.reshape(send_count.shape[1:])
    cols = tile_cols.T
    feed = feed.reshape(cell_blocks, LANES)
    kill = kill.reshape(cell_blocks, LANES)

    vmem = pl.BlockSpec(memory_space=VMEM)
    smem = pl.BlockSpec(memory_space=SMEM)
    anywhere = pl.BlockSpec(memory_space=pl.ANY)
    params = pltpu.CompilerParams(vmem_limit_bytes=16 * 1024 * 1024)

    prev = None
    parts, arrived = [], []
    for chunk in CHUNKS:
        size = len(chunk) * FIELDS * 2 * STEPS
        widths = [len(slots) * slot_rows for slots in slot_groups]
        shapes = [jax.ShapeDtypeStruct((size, width), F32) for width in widths]
        shapes.append(jax.ShapeDtypeStruct((cell_blocks, 2 * size, LANES), BF16))
        inputs = list(fields)
        if 0 in chunk:
            inputs.append(prev)
        else:
            shapes.append(jax.ShapeDtypeStruct((FIELDS * stride, LANES), F32))
        results = pl.pallas_call(
            functools.partial(gather_kernel, chunk, slot_groups, cell_blocks),
            out_shape=shapes,
            in_specs=[vmem] * len(inputs) + [vmem, smem],
            out_specs=[vmem] * len(shapes),
            scratch_shapes=[VMEM((cells, slot_rows), BF16)],
            compiler_params=params,
            cost_estimate=pl.CostEstimate(
                flops=4 * size * cells * sum(widths), bytes_accessed=4 * size * (cells + sum(widths)), transcendentals=0
            ),
            name="gather_rows",
        )(*inputs, rows, counts)
        if 0 not in chunk and prev is None:
            prev = shift_along(results[-1], "tm", 1)
        arrived.append(
            [shift_along(send, "dom", OFFSETS[slots[0]]) for send, slots in zip(results, slot_groups)]
        )
        parts.append(results[len(slot_groups)])

    *bases, split_tiles = pl.pallas_call(
        functools.partial(local_kernel, CHUNKS, cell_blocks),
        out_shape=[jax.ShapeDtypeStruct((cell_blocks, p.shape[1] // 2, LANES), F32) for p in parts]
        + [jax.ShapeDtypeStruct((blocks, per_row * LANES, 2 * LANES), BF16)],
        in_specs=[vmem] * 7,
        out_specs=[vmem] * (len(parts) + 1),
        compiler_params=params,
        cost_estimate=pl.CostEstimate(flops=60 * steps * 6 * cells, bytes_accessed=4 * tiles.size, transcendentals=0),
        name="local_terms",
    )(*fields, prev, feed, kill, tiles)

    outs = []
    for number, chunk in enumerate(CHUNKS):
        size = len(chunk) * FIELDS * 2 * STEPS
        inputs = [cols, split_tiles, bases[number], parts[number], *arrived[number]]
        specs = [smem] + [vmem] * (len(inputs) - 1)
        aliases = {len(inputs) + f: f for f in range(FIELDS)} if outs else {}
        outs = pl.pallas_call(
            functools.partial(apply_kernel, chunk, slot_groups, cell_blocks, blocks, per_row, not outs),
            out_shape=[jax.ShapeDtypeStruct((steps * stride, LANES), F32)] * FIELDS,
            in_specs=specs + [anywhere] * len(outs),
            out_specs=[anywhere] * FIELDS,
            input_output_aliases=aliases,
            scratch_shapes=[
                VMEM((cell_blocks + len(OFFSETS) * slot_rows // LANES, 2 * size, LANES), BF16),
                VMEM((FIELDS, len(chunk) * STEPS * stride, LANES), F32),
                pltpu.SemaphoreType.DMA((FIELDS,)),
            ],
            compiler_params=params,
            cost_estimate=pl.CostEstimate(
                flops=8 * size * blocks * per_row * LANES * LANES, bytes_accessed=8 * size * cells, transcendentals=0
            ),
            name="apply_tiles",
        )(*inputs, *outs)
    return tuple(unview(out) for out in outs)


def solution(mesh):
    fields = P(("group", "tm"), None, "dom")
    in_specs = (
        fields,
        fields,
        fields,
        P("dom"),
        P("dom"),
        P("dom", None, None, None),
        P("dom", None),
        P("dom", None, None),
        P("dom", None),
    )
    return jax.shard_map(
        per_device, mesh=mesh, in_specs=in_specs, out_specs=(fields, fields, fields), check_vma=False
    )
```

time: 73.4 us -> 32 us (0.44)
  local copies, waits for them, and re-layouts: 32.3 us -> 4.25 us
  waiting for transfers between devices: 18.1 us -> 8.02 us
  other arithmetic: 9.53 us -> 0 us
  Pallas kernels: 0 us -> 7.05 us
  matrix products: 3.65 us -> 0 us
  starting transfers between devices: 8.21 us -> 11.8 us
    ppermute x6 -> x7, waiting for transfers between devices: 18.1 us -> 8.02 us  [shift_along(): lax.ppermute(block, axis, [((i - distance) % size, i) for i in range(size)])]
    gather x5 -> x0, local copies, waits for them, and re-layouts: 8.57 us -> none  [the longest x4 6.66 us: laplace(): values = jnp.take(flat, send_rows[0, slot], axis=1)]
    unnamed x30 -> x18, local copies, waits for them, and re-layouts: 11.6 us -> 4.25 us
    pallas_call x0 -> x5, Pallas kernels: none -> 7.05 us  [the longest x2 3.71 us: per_device(): pl.pallas_call(functools.partial(apply_kernel, chunk, slot_groups, cell_b...]
    select_n x9 -> x0, other arithmetic: 6.51 us -> none  [the longest x4 6.49 us: laplace(): outgoing = jnp.where(live[None, :], values, jnp.zeros_like(values))]
    dot_general x1 -> x0, matrix products: 3.65 us -> none  [laplace(): jnp.einsum('rkij,crkj->cri', tiles, chosen, precision=lax.Precision.HIGHEST)]
    reshape x3 -> x0, local copies, waits for them, and re-layouts: 3.64 us -> none  [the longest x2 2.29 us: per_device(): stacked.reshape(-1, cell_count)]
    ppermute x6 -> x7, starting transfers between devices: 8.21 us -> 11.8 us  [shift_along(): lax.ppermute(block, axis, [((i - distance) % size, i) for i in range(size)])]
  transfers between devices with their start and end apart: 6 -> 7, of which waited for: 3 -> 4; matrix products, arithmetic and copies ran while one was open for 52% -> 0% of each run, Pallas kernels for 0% -> 12%
where the time goes in v1:
time: 32 us; the launch traced here: 31.8 us
  starting transfers between devices  11.8 us (37%)
  waiting for transfers between devices  8.02 us (25%)
  Pallas kernels  7.05 us (22%)
  local copies, waits for them, and re-layouts  4.25 us (13%)
  between operations  0.72 us (2%)
    ppermute x7, starting transfers between devices, shift_along(): lax.ppermute(block, axis, [((i - distance) % size, i) for i in range(size)])  11.8 us
    ppermute x7, waiting for transfers between devices, shift_along(): lax.ppermute(block, axis, [((i - distance) % size, i) for i in range(size)])  8.02 us
    unnamed x18, local copies, waits for them, and re-layouts  4.25 us
    pallas_call x2, Pallas kernels, per_device(): pl.pallas_call(functools.partial(apply_kernel, chunk, slot_groups, cell_b...  3.71 us
    pallas_call x2, Pallas kernels, per_device(): pl.pallas_call(functools.partial(gather_kernel, chunk, slot_groups, cell_...  2.51 us
    pallas_call x1, Pallas kernels, per_device(): pl.pallas_call(functools.partial(local_kernel, CHUNKS, cell_blocks), out_...  0.83 us
  transfers between devices with their start and end apart: 7, of which 4 were waited for; matrix products, arithmetic and copies ran while one was open for 0% of the time, Pallas kernels for 12%

profile of v1, /device:TPU:0, one launch (start us, length us, event | category | flops | bytes accessed | tf_op | source)
XLA Modules:
  0.0 31.8 jit_solution(14854306006975022993)
XLA Ops:
  0.6 0.0 copy-start
  0.6 0.0 copy-start.1
  0.7 1.0 %copy-done.1 = f32[24,2,1024]{2,1,0:T(2,128)S(1)} copy-done((f32[24,2,1024]{2,1,0:T(2,128)S(1)}, f32[24,2,1024]{2,1,0:T(2,128)}, u32[]{:S(2)}) %copy-start.1) | copy-done | bytes 196632
  1.7 0.0 copy-start.2
  1.7 0.9 %copy-done.2 = f32[24,2,1024]{2,1,0:T(2,128)S(1)} copy-done((f32[24,2,1024]{2,1,0:T(2,128)S(1)}, f32[24,2,1024]{2,1,0:T(2,128)}, u32[]{:S(2)}) %copy-start.2) | copy-done | bytes 196632
  2.6 0.9 %copy-done.3 = f32[24,2,1024]{2,1,0:T(2,128)S(1)} copy-done((f32[24,2,1024]{2,1,0:T(2,128)S(1)}, f32[24,2,1024]{2,1,0:T(2,128)}, u32[]{:S(2)}) %copy-start.3) | copy-done | bytes 196632
  3.5 0.7 %copy-done.7 = s32[1,4,256]{2,1,0:T(4,128)S(1)} copy-done((s32[1,4,256]{2,1,0:T(4,128)S(1)}, s32[1,4,256]{2,1,0:T(4,128)}, u32[]{:S(2)}) %copy-start.7) | copy-done | bytes 4120
  4.2 0.7 %copy-done.8 = s32[1,4]{1,0:T(1,128)S(1)} copy-done((s32[1,4]{1,0:T(1,128)S(1)}, s32[1,4]{1,0:T(1,128)}, u32[]{:S(2)}) %copy-start.8) | copy-done | bytes 40
  4.9 1.4 %gather_rows.2 = (f32[96,512]{1,0:T(8,128)S(1)}, f32[96,256]{1,0:T(8,128)S(1)}, f32[96,256]{1,0:T(8,128)S(1)}, bf16[8,192,128]{2,1,0:T(8,128)(2,1)S(1)}, f32[48,128]{1,0:T(8,128)S(1)}) custom-call(f32[384,128]{1,0:T(8,128)S(1)} %bitcast.35, f32[384,128]{1,0:T(8,128)S(1)} %bitcast.38, f32[384,128]{1,0:T(8,128)S(1)} %bitcast.41, s32[4,256]{1,0:T(4,128)S(1)} %bitcast.48, ...), custom_call_target="tpu_custom_call" | custom-call | flops 402653184 | bytes 786432 | tf_op jit(solution)/shard_map/gather_rows/pallas_call | solution.py:218
  6.3 0.0 copy-start.4
  6.3 4.1 %collective-permute-start.4 = (f32[96,512]{1,0:T(8,128)S(1)}, f32[96,512]{1,0:T(8,128)S(1)}, u32[]{:S(2)}, u32[]{:S(2)}) collective-permute-start(f32[96,512]{1,0:T(8,128)S(1)} %get-tuple-element.30), channel_id=1, source_target_pairs={{8,0},{12,4},{0,8},{4,12},{9,1},{13,5},{1,9},{5,13},{10,2},{14,6},... | collective-permute-start | bytes 589832 | tf_op jit(solution)/shard_map/ppermute | solution.py:26
  10.4 1.6 %collective-permute-start.5 = (f32[96,256]{1,0:T(8,128)S(1)}, f32[96,256]{1,0:T(8,128)S(1)}, u32[]{:S(2)}, u32[]{:S(2)}) collective-permute-start(f32[96,256]{1,0:T(8,128)S(1)} %get-tuple-element.31), channel_id=1, source_target_pairs={{12,0},{0,4},{4,8},{8,12},{13,1},{1,5},{5,9},{9,13},{14,2},{2,6},{... | collective-permute-start | bytes 294920 | tf_op jit(solution)/shard_map/ppermute | solution.py:26
  12.0 0.0 collective-permute-start
  12.0 2.2 %collective-permute-start.6 = (f32[96,256]{1,0:T(8,128)S(1)}, f32[96,256]{1,0:T(8,128)S(1)}, u32[]{:S(2)}, u32[]{:S(2)}) collective-permute-start(f32[96,256]{1,0:T(8,128)S(1)} %get-tuple-element.32), channel_id=1, source_target_pairs={{4,0},{8,4},{12,8},{0,12},{5,1},{9,5},{13,9},{1,13},{6,2},{10,6},{... | collective-permute-start | bytes 294920 | tf_op jit(solution)/shard_map/ppermute | solution.py:26
  14.2 1.0 %collective-permute-done.refs_3_ = f32[48,128]{1,0:T(8,128)S(1)} collective-permute-done((f32[48,128]{1,0:T(8,128)S(1)}, f32[48,128]{1,0:T(8,128)S(1)}, u32[]{:S(2)}, u32[]{:S(2)}) %collective-permute-start) | collective-permute-done | bytes 24608 | tf_op jit(solution)/shard_map/ppermute | solution.py:26
  15.2 1.1 %gather_rows.3 = (f32[48,512]{1,0:T(8,128)S(1)}, f32[48,256]{1,0:T(8,128)S(1)}, f32[48,256]{1,0:T(8,128)S(1)}, bf16[8,96,128]{2,1,0:T(8,128)(2,1)S(1)}) custom-call(f32[384,128]{1,0:T(8,128)S(1)} %bitcast.36, f32[384,128]{1,0:T(8,128)S(1)} %bitcast.39, f32[384,128]{1,0:T(8,128)S(1)} %bitcast.42, f32[48,128]{1,0:T(8,128)S(1)} %collective-permute-done.refs_3_, ...), custom_call_target="tpu_custom_call" | custom-call | flops 201326592 | bytes 393216 | tf_op jit(solution)/shard_map/gather_rows/pallas_call | solution.py:218
  16.4 0.4 %collective-permute-start.1 = (f32[48,512]{1,0:T(8,128)S(1)}, f32[48,512]{1,0:T(8,128)S(1)}, u32[]{:S(2)}, u32[]{:S(2)}) collective-permute-start(f32[48,512]{1,0:T(8,128)S(1)} %get-tuple-element.25), channel_id=1, source_target_pairs={{8,0},{12,4},{0,8},{4,12},{9,1},{13,5},{1,9},{5,13},{10,2},{14,6},... | collective-permute-start | bytes 294920 | tf_op jit(solution)/shard_map/ppermute | solution.py:26
  16.8 2.5 %collective-permute-start.2 = (f32[48,256]{1,0:T(8,128)S(1)}, f32[48,256]{1,0:T(8,128)S(1)}, u32[]{:S(2)}, u32[]{:S(2)}) collective-permute-start(f32[48,256]{1,0:T(8,128)S(1)} %get-tuple-element.26), channel_id=1, source_target_pairs={{12,0},{0,4},{4,8},{8,12},{13,1},{1,5},{5,9},{9,13},{14,2},{2,6},{... | collective-permute-start | bytes 147464 | tf_op jit(solution)/shard_map/ppermute | solution.py:26
  19.2 0.4 %collective-permute-done.5.refs_5_ = f32[96,256]{1,0:T(8,128)S(1)} collective-permute-done((f32[96,256]{1,0:T(8,128)S(1)}, f32[96,256]{1,0:T(8,128)S(1)}, u32[]{:S(2)}, u32[]{:S(2)}) %collective-permute-start.5) | collective-permute-done | bytes 98336 | tf_op jit(solution)/shard_map/ppermute | solution.py:26
  19.6 1.0 %collective-permute-start.3 = (f32[48,256]{1,0:T(8,128)S(1)}, f32[48,256]{1,0:T(8,128)S(1)}, u32[]{:S(2)}, u32[]{:S(2)}) collective-permute-start(f32[48,256]{1,0:T(8,128)S(1)} %get-tuple-element.27), channel_id=1, source_target_pairs={{4,0},{8,4},{12,8},{0,12},{5,1},{9,5},{13,9},{1,13},{6,2},{10,6},{... | collective-permute-start | bytes 147464 | tf_op jit(solution)/shard_map/ppermute | solution.py:26
  20.6 0.0 copy-done
  20.6 0.0 copy-done.5
  20.6 0.0 copy-done.6
  20.6 0.8 %local_terms.1 = (f32[8,96,128]{2,1,0:T(8,128)S(1)}, f32[8,48,128]{2,1,0:T(8,128)S(1)}, bf16[8,384,256]{2,1,0:T(8,128)(2,1)S(1)}) custom-call(f32[384,128]{1,0:T(8,128)S(1)} %bitcast.37, f32[384,128]{1,0:T(8,128)S(1)} %bitcast.40, f32[384,128]{1,0:T(8,128)S(1)} %bitcast.43, f32[48,128]{1,0:T(8,128)S(1)} %collective-permute-done.refs_3_, ...), custom_call_target="tpu_custom_call" | custom-call | flops 8847360 | bytes 1572864 | tf_op jit(solution)/shard_map/local_terms/pallas_call | solution.py:237
  21.4 0.0 collective-permute-done.6.refs_6_
  21.4 4.2 %collective-permute-done.4.refs_4_ = f32[96,512]{1,0:T(8,128)S(1)} collective-permute-done((f32[96,512]{1,0:T(8,128)S(1)}, f32[96,512]{1,0:T(8,128)S(1)}, u32[]{:S(2)}, u32[]{:S(2)}) %collective-permute-start.4) | collective-permute-done | bytes 196640 | tf_op jit(solution)/shard_map/ppermute | solution.py:26
  25.6 0.0 copy-done.4
  25.6 2.0 %apply_tiles.2 = (f32[384,128]{1,0:T(8,128)}, f32[384,128]{1,0:T(8,128)}, f32[384,128]{1,0:T(8,128)}) custom-call(s32[3,8]{1,0:T(4,128)S(1)} %bitcast.44, bf16[8,384,256]{2,1,0:T(8,128)(2,1)S(1)} %get-tuple-element.22.refs_1_, f32[8,96,128]{2,1,0:T(8,128)S(1)} %get-tuple-element.28.refs_2_, bf16[8,192,128]{2,1,0:T(8,128)(2,1)S(1)} %get-tuple-element.29.refs_3_, ...), custom_call_target="tpu_custom_call" | custom-call | flops 301989888 | bytes 786432 | tf_op jit(solution)/shard_map/apply_tiles/pallas_call | solution.py:254
  27.6 0.0 collective-permute-done.2.refs_5_
  27.7 2.4 %collective-permute-done.3.refs_6_ = f32[48,256]{1,0:T(8,128)S(1)} collective-permute-done((f32[48,256]{1,0:T(8,128)S(1)}, f32[48,256]{1,0:T(8,128)S(1)}, u32[]{:S(2)}, u32[]{:S(2)}) %collective-permute-start.3) | collective-permute-done | bytes 49184 | tf_op jit(solution)/shard_map/ppermute | solution.py:26
  30.1 0.0 collective-permute-done.1.refs_4_
  30.1 1.7 %apply_tiles.3 = (f32[384,128]{1,0:T(8,128)}, f32[384,128]{1,0:T(8,128)}, f32[384,128]{1,0:T(8,128)}) custom-call(s32[3,8]{1,0:T(4,128)S(1)} %bitcast.45, bf16[8,384,256]{2,1,0:T(8,128)(2,1)S(1)} %get-tuple-element.22.refs_1_, f32[8,48,128]{2,1,0:T(8,128)S(1)} %get-tuple-element.23.refs_2_, ...), custom_call_target="tpu_custom_call", output_to_operand_aliasing={{0}: (7, {}), {1}: (8, {}), {2}: (9, {})} | custom-call | flops 150994944 | bytes 393216 | tf_op jit(solution)/shard_map/apply_tiles/pallas_call | solution.py:254
  (5 shorter events, 0.0 us)
Async XLA Ops:
  0.6 20.0 %copy-start = (f32[8,3,128,128]{3,2,1,0:T(8,128)S(1)}, f32[8,3,128,128]{3,2,1,0:T(8,128)}, u32[]{:S(2)}) copy-start(f32[8,3,128,128]{3,2,1,0:T(8,128)} %refs_6_.1) | copy-start | bytes 4718596
  0.6 1.0 %copy-start.1 = (f32[24,2,1024]{2,1,0:T(2,128)S(1)}, f32[24,2,1024]{2,1,0:T(2,128)}, u32[]{:S(2)}) copy-start(f32[24,2,1024]{2,1,0:T(2,128)} %param.9) | copy-start | bytes 589828
  1.7 0.9 %copy-start.2 = (f32[24,2,1024]{2,1,0:T(2,128)S(1)}, f32[24,2,1024]{2,1,0:T(2,128)}, u32[]{:S(2)}) copy-start(f32[24,2,1024]{2,1,0:T(2,128)} %param.10) | copy-start | bytes 589828
  2.6 0.9 %copy-start.3 = (f32[24,2,1024]{2,1,0:T(2,128)S(1)}, f32[24,2,1024]{2,1,0:T(2,128)}, u32[]{:S(2)}) copy-start(f32[24,2,1024]{2,1,0:T(2,128)} %param.11) | copy-start | bytes 589828
  3.5 0.7 %copy-start.7 = (s32[1,4,256]{2,1,0:T(4,128)S(1)}, s32[1,4,256]{2,1,0:T(4,128)}, u32[]{:S(2)}) copy-start(s32[1,4,256]{2,1,0:T(4,128)} %param.16) | copy-start | bytes 12292
  4.2 0.7 %copy-start.8 = (s32[1,4]{1,0:T(1,128)S(1)}, s32[1,4]{1,0:T(1,128)}, u32[]{:S(2)}) copy-start(s32[1,4]{1,0:T(1,128)} %param.17) | copy-start | bytes 52
  4.9 15.7 %copy-start.5 = (f32[1024]{0:T(1024)S(1)}, f32[1024]{0:T(1024)}, u32[]{:S(2)}) copy-start(f32[1024]{0:T(1024)} %param.12) | copy-start | bytes 12292
  4.9 15.7 %copy-start.6 = (f32[1024]{0:T(1024)S(1)}, f32[1024]{0:T(1024)}, u32[]{:S(2)}) copy-start(f32[1024]{0:T(1024)} %param.13) | copy-start | bytes 12292
  6.3 19.4 %copy-start.4 = (s32[8,3]{0,1:T(4,128)S(1)}, s32[8,3]{0,1:T(4,128)}, u32[]{:S(2)}) copy-start(s32[8,3]{0,1:T(4,128)} %param.15) | copy-start | bytes 292
  6.3 19.4 %collective-permute-start.4 = (f32[96,512]{1,0:T(8,128)S(1)}, f32[96,512]{1,0:T(8,128)S(1)}, u32[]{:S(2)}, u32[]{:S(2)}) collective-permute-start(f32[96,512]{1,0:T(8,128)S(1)} %get-tuple-element.30), channel_id=1, source_target_pairs={{8,0},{12,4},{0,8},{4,12},{9,1},{13,5},{1,9},{5,13},{10,2},{14,6},... | collective-permute-start | bytes 589832 | tf_op jit(solution)/shard_map/ppermute | solution.py:26
  10.4 9.2 %collective-permute-start.5 = (f32[96,256]{1,0:T(8,128)S(1)}, f32[96,256]{1,0:T(8,128)S(1)}, u32[]{:S(2)}, u32[]{:S(2)}) collective-permute-start(f32[96,256]{1,0:T(8,128)S(1)} %get-tuple-element.31), channel_id=1, source_target_pairs={{12,0},{0,4},{4,8},{8,12},{13,1},{1,5},{5,9},{9,13},{14,2},{2,6},{... | collective-permute-start | bytes 294920 | tf_op jit(solution)/shard_map/ppermute | solution.py:26
  12.0 3.3 %collective-permute-start = (f32[48,128]{1,0:T(8,128)S(1)}, f32[48,128]{1,0:T(8,128)S(1)}, u32[]{:S(2)}, u32[]{:S(2)}) collective-permute-start(f32[48,128]{1,0:T(8,128)S(1)} %get-tuple-element.21), channel_id=1, source_target_pairs={{3,0},{0,1},{1,2},{2,3},{7,4},{4,5},{5,6},{6,7},{11,8},{8,9},{9,10... | collective-permute-start | bytes 73736 | tf_op jit(solution)/shard_map/ppermute | solution.py:26
  12.0 9.5 %collective-permute-start.6 = (f32[96,256]{1,0:T(8,128)S(1)}, f32[96,256]{1,0:T(8,128)S(1)}, u32[]{:S(2)}, u32[]{:S(2)}) collective-permute-start(f32[96,256]{1,0:T(8,128)S(1)} %get-tuple-element.32), channel_id=1, source_target_pairs={{4,0},{8,4},{12,8},{0,12},{5,1},{9,5},{13,9},{1,13},{6,2},{10,6},{... | collective-permute-start | bytes 294920 | tf_op jit(solution)/shard_map/ppermute | solution.py:26
  16.4 13.7 %collective-permute-start.1 = (f32[48,512]{1,0:T(8,128)S(1)}, f32[48,512]{1,0:T(8,128)S(1)}, u32[]{:S(2)}, u32[]{:S(2)}) collective-permute-start(f32[48,512]{1,0:T(8,128)S(1)} %get-tuple-element.25), channel_id=1, source_target_pairs={{8,0},{12,4},{0,8},{4,12},{9,1},{13,5},{1,9},{5,13},{10,2},{14,6},... | collective-permute-start | bytes 294920 | tf_op jit(solution)/shard_map/ppermute | solution.py:26
  16.8 10.9 %collective-permute-start.2 = (f32[48,256]{1,0:T(8,128)S(1)}, f32[48,256]{1,0:T(8,128)S(1)}, u32[]{:S(2)}, u32[]{:S(2)}) collective-permute-start(f32[48,256]{1,0:T(8,128)S(1)} %get-tuple-element.26), channel_id=1, source_target_pairs={{12,0},{0,4},{4,8},{8,12},{13,1},{1,5},{5,9},{9,13},{14,2},{2,6},{... | collective-permute-start | bytes 147464 | tf_op jit(solution)/shard_map/ppermute | solution.py:26
  19.6 10.5 %collective-permute-start.3 = (f32[48,256]{1,0:T(8,128)S(1)}, f32[48,256]{1,0:T(8,128)S(1)}, u32[]{:S(2)}, u32[]{:S(2)}) collective-permute-start(f32[48,256]{1,0:T(8,128)S(1)} %get-tuple-element.27), channel_id=1, source_target_pairs={{4,0},{8,4},{12,8},{0,12},{5,1},{9,5},{13,9},{1,13},{6,2},{10,6},{... | collective-permute-start | bytes 147464 | tf_op jit(solution)/shard_map/ppermute | solution.py:26

commit v2 on v1

--- a/solution.py
+++ b/solution.py
@@ -46,44 +46,97 @@
     return high, (values - high.astype(F32)).astype(BF16)
 
 
-def gather_kernel(chunk, slot_groups, cell_blocks, *refs):
-    refs = list(refs)
-    fields = [refs.pop(0) for _ in range(FIELDS)]
-    prev = refs.pop(0) if 0 in chunk else None
-    rows_ref, count_ref = refs.pop(0), refs.pop(0)
-    sends = [refs.pop(0) for _ in slot_groups]
-    parts_ref = refs.pop(0)
-    last = None if 0 in chunk else refs.pop(0)
-    (choose,) = refs
-    stride = 2 * cell_blocks
-    size = len(chunk) * FIELDS * 2 * STEPS
-    if last is not None:
-        for field in range(FIELDS):
-            last[field * stride : (field + 1) * stride, :] = fields[field][-stride:, :]
+def summed_parts(chunk, cell_blocks, field_at, prev, parts_ref):
+    stride = 2 * cell_blocks
+    size = parts_ref.shape[1] // 2
     for place, group in enumerate(chunk):
         for field in range(FIELDS):
             row = (place * FIELDS + field) * 2 * STEPS
             for block in range(cell_blocks):
                 both = []
                 for species, scale in enumerate((-0.5 * spread_u, -0.5 * spread_v)):
-                    now = steps_at(fields[field], group, block, species, stride)
-                    before = steps_before(fields[field], prev, field, group, block, species, stride)
+                    now = steps_at(field_at[field], group, block, species, stride)
+                    before = steps_before(field_at[field], prev, field, group, block, species, stride)
                     both.append((now + before) * scale)
                 high, low = split(jnp.concatenate(both, axis=0))
                 parts_ref[block, row : row + 2 * STEPS, :] = high
                 parts_ref[block, size + row : size + row + 2 * STEPS, :] = low
-    slot_rows = rows_ref.shape[1]
-    parts = jnp.concatenate([parts_ref[b] for b in range(cell_blocks)], axis=1)
-    lane = lax.broadcasted_iota(jnp.int32, (1, slot_rows), 1)
+
+
+def choose_rows(slots, listed_ref, choose):
+    cells = choose.shape[0]
+    slot_rows = listed_ref.shape[1]
     cell = lax.broadcasted_iota(jnp.int32, (LANES, slot_rows), 0)
-    for send, slots in zip(sends, slot_groups):
-        for place, slot in enumerate(slots):
-            listed = jnp.where(lane < count_ref[slot], rows_ref[slot : slot + 1, :], -1)
-            for block in range(cell_blocks):
-                hit = cell == listed - block * LANES
-                choose[block * LANES : (block + 1) * LANES, :] = jnp.where(hit, 1.0, 0.0).astype(BF16)
-            taken = jnp.dot(parts, choose[...], preferred_element_type=F32)
-            send[:, place * slot_rows : (place + 1) * slot_rows] = taken[:size] + taken[size:]
+    for place, slot in enumerate(slots):
+        listed = listed_ref[slot : slot + 1, :]
+        for start in range(0, cells, LANES):
+            hit = cell == listed - start
+            choose[start : start + LANES, place * slot_rows : (place + 1) * slot_rows] = jnp.where(
+                hit, 1.0, 0.0
+            ).astype(BF16)
+
+
+def take_rows(parts_ref, choose, sends):
+    size = parts_ref.shape[1] // 2
+    parts = jnp.concatenate([parts_ref[b] for b in range(parts_ref.shape[0])], axis=1)
+    start = 0
+    for send in sends:
+        width = send.shape[1]
+        taken = jnp.dot(parts, choose[:, start : start + width], preferred_element_type=F32)
+        send[...] = taken[:size] + taken[size:]
+        start += width
+
+
+def first_kernel(chunk, slots, cell_blocks, *refs):
+    refs = list(refs)
+    sources = [refs.pop(0) for _ in range(FIELDS)]
+    rows_hbm, count_hbm, send, parts_ref, held, listed, last, choose, rows_ref, count_ref, sems = refs
+    stride = 2 * cell_blocks
+    early = (chunk[0] * STEPS - 1) * stride
+    late = held.shape[1] - early
+    small = [
+        pltpu.make_async_copy(rows_hbm, rows_ref, sems.at[2 * FIELDS]),
+        pltpu.make_async_copy(count_hbm, count_ref, sems.at[2 * FIELDS + 1]),
+    ]
+    needed = [
+        pltpu.make_async_copy(sources[f].at[pl.ds(early, late), :], held.at[f, pl.ds(early, late), :], sems.at[f])
+        for f in range(FIELDS)
+    ]
+    others = [
+        pltpu.make_async_copy(sources[f].at[pl.ds(0, early), :], held.at[f, pl.ds(0, early), :], sems.at[FIELDS + f])
+        for f in range(FIELDS)
+    ]
+    for copy in small + needed + others:
+        copy.start()
+    for copy in small:
+        copy.wait()
+    lane = lax.broadcasted_iota(jnp.int32, rows_ref.shape, 1)
+    for slot in range(rows_ref.shape[0]):
+        listed[slot : slot + 1, :] = jnp.where(
+            lane[slot : slot + 1] < count_ref[:, slot : slot + 1], rows_ref[slot : slot + 1, :], -1
+        )
+    choose_rows(slots, listed, choose)
+    for copy in needed:
+        copy.wait()
+    summed_parts(chunk, cell_blocks, [held.at[f] for f in range(FIELDS)], None, parts_ref)
+    take_rows(parts_ref, choose, [send])
+    for field in range(FIELDS):
+        last[field * stride : (field + 1) * stride, :] = held[field, -stride:, :]
+    for copy in others:
+        copy.wait()
+
+
+def rest_kernel(slots, parts_ref, listed, *refs):
+    *sends, choose = refs
+    choose_rows(slots, listed, choose)
+    take_rows(parts_ref, choose, sends)
+
+
+def gather_kernel(chunk, slots, cell_blocks, held, prev, listed, *refs):
+    *sends, parts_ref, choose = refs
+    choose_rows(slots, listed, choose)
+    summed_parts(chunk, cell_blocks, [held.at[f] for f in range(FIELDS)], prev, parts_ref)
+    take_rows(parts_ref, choose, sends)
 
 
 def pointwise(u, v, du, dv, ddu, ddv, feed, total):
@@ -99,8 +152,8 @@
 
 def local_kernel(chunks, cell_blocks, *refs):
     refs = list(refs)
-    fields = [refs.pop(0) for _ in range(FIELDS)]
-    prev, feed_ref, kill_ref, tiles = [refs.pop(0) for _ in range(4)]
+    held, prev, feed_ref, kill_ref, tiles = [refs.pop(0) for _ in range(5)]
+    fields = [held.at[f] for f in range(FIELDS)]
     bases = [refs.pop(0) for _ in chunks]
     (split_tiles,) = refs
     stride = 2 * cell_blocks
@@ -193,7 +246,7 @@
 
     fields = [view(state), view(dir_one), view(dir_two)]
     rows = send_rows.reshape(send_rows.shape[1:])
-    counts = send_count.reshape(send_count.shape[1:])
+    counts = send_count
     cols = tile_cols.T
     feed = feed.reshape(cell_blocks, LANES)
     kill = kill.reshape(cell_blocks, LANES)
@@ -203,47 +256,88 @@
     anywhere = pl.BlockSpec(memory_space=pl.ANY)
     params = pltpu.CompilerParams(vmem_limit_bytes=16 * 1024 * 1024)
 
-    prev = None
-    parts, arrived = [], []
-    for chunk in CHUNKS:
-        size = len(chunk) * FIELDS * 2 * STEPS
-        widths = [len(slots) * slot_rows for slots in slot_groups]
-        shapes = [jax.ShapeDtypeStruct((size, width), F32) for width in widths]
-        shapes.append(jax.ShapeDtypeStruct((cell_blocks, 2 * size, LANES), BF16))
-        inputs = list(fields)
-        if 0 in chunk:
-            inputs.append(prev)
-        else:
-            shapes.append(jax.ShapeDtypeStruct((FIELDS * stride, LANES), F32))
-        results = pl.pallas_call(
-            functools.partial(gather_kernel, chunk, slot_groups, cell_blocks),
-            out_shape=shapes,
-            in_specs=[vmem] * len(inputs) + [vmem, smem],
-            out_specs=[vmem] * len(shapes),
-            scratch_shapes=[VMEM((cells, slot_rows), BF16)],
-            compiler_params=params,
-            cost_estimate=pl.CostEstimate(
-                flops=4 * size * cells * sum(widths), bytes_accessed=4 * size * (cells + sum(widths)), transcendentals=0
-            ),
-            name="gather_rows",
-        )(*inputs, rows, counts)
-        if 0 not in chunk and prev is None:
-            prev = shift_along(results[-1], "tm", 1)
-        arrived.append(
-            [shift_along(send, "dom", OFFSETS[slots[0]]) for send, slots in zip(results, slot_groups)]
+    def rows_of(chunk):
+        return len(chunk) * FIELDS * 2 * STEPS
+
+    def f32(*shape):
+        return jax.ShapeDtypeStruct(shape, F32)
+
+    def parts_of(chunk):
+        return jax.ShapeDtypeStruct((cell_blocks, 2 * rows_of(chunk), LANES), BF16)
+
+    def gather_cost(chunk, slots):
+        width = len(slots) * slot_rows
+        size = rows_of(chunk)
+        return pl.CostEstimate(
+            flops=4 * size * cells * width, bytes_accessed=4 * size * (cells + width), transcendentals=0
         )
-        parts.append(results[len(slot_groups)])
+
+    def send_all(sends, groups):
+        return [shift_along(send, "dom", OFFSETS[slots[0]]) for send, slots in zip(sends, groups)]
+
+    hbm = pl.BlockSpec(memory_space=pltpu.HBM)
+    lead, later = CHUNKS
+    wide, *narrow = slot_groups
+    others = [slot for slots in narrow for slot in slots]
+    every = wide + others
+    send, lead_parts, held, listed, last = pl.pallas_call(
+        functools.partial(first_kernel, lead, wide, cell_blocks),
+        out_shape=[
+            f32(rows_of(lead), len(wide) * slot_rows),
+            parts_of(lead),
+            f32(FIELDS, steps * stride, LANES),
+            jax.ShapeDtypeStruct(rows.shape, jnp.int32),
+            f32(FIELDS * stride, LANES),
+        ],
+        in_specs=[hbm] * (FIELDS + 2),
+        out_specs=[vmem] * 5,
+        scratch_shapes=[
+            VMEM((cells, len(wide) * slot_rows), BF16),
+            VMEM(rows.shape, jnp.int32),
+            VMEM(counts.shape, jnp.int32),
+            pltpu.SemaphoreType.DMA((2 * FIELDS + 2,)),
+        ],
+        compiler_params=params,
+        cost_estimate=gather_cost(lead, wide),
+        name="gather_first",
+    )(*[pltpu.with_memory_space_constraint(x, pltpu.HBM) for x in (*fields, rows, counts)])
+    lead_arrived = send_all([send], [wide])
+    prev = shift_along(last, "tm", 1)
+    sends = pl.pallas_call(
+        functools.partial(rest_kernel, others),
+        out_shape=[f32(rows_of(lead), len(slots) * slot_rows) for slots in narrow],
+        in_specs=[vmem] * 2,
+        out_specs=[vmem] * len(narrow),
+        scratch_shapes=[VMEM((cells, len(others) * slot_rows), BF16)],
+        compiler_params=params,
+        cost_estimate=gather_cost(lead, others),
+        name="gather_rest",
+    )(lead_parts, listed)
+    lead_arrived += send_all(sends, narrow)
+    *sends, later_parts = pl.pallas_call(
+        functools.partial(gather_kernel, later, every, cell_blocks),
+        out_shape=[f32(rows_of(later), len(slots) * slot_rows) for slots in slot_groups] + [parts_of(later)],
+        in_specs=[vmem] * 3,
+        out_specs=[vmem] * (len(slot_groups) + 1),
+        scratch_shapes=[VMEM((cells, len(every) * slot_rows), BF16)],
+        compiler_params=params,
+        cost_estimate=gather_cost(later, every),
+        name="gather_later",
+    )(held, prev, listed)
+    later_arrived = send_all(sends, slot_groups)
+    arrived = [lead_arrived, later_arrived]
+    parts = [lead_parts, later_parts]
 
     *bases, split_tiles = pl.pallas_call(
         functools.partial(local_kernel, CHUNKS, cell_blocks),
         out_shape=[jax.ShapeDtypeStruct((cell_blocks, p.shape[1] // 2, LANES), F32) for p in parts]
         + [jax.ShapeDtypeStruct((blocks, per_row * LANES, 2 * LANES), BF16)],
-        in_specs=[vmem] * 7,
+        in_specs=[vmem] * 5,
         out_specs=[vmem] * (len(parts) + 1),
         compiler_params=params,
         cost_estimate=pl.CostEstimate(flops=60 * steps * 6 * cells, bytes_accessed=4 * tiles.size, transcendentals=0),
         name="local_terms",
-    )(*fields, prev, feed, kill, tiles)
+    )(held, prev, feed, kill, tiles)
 
     outs = []
     for number, chunk in enumerate(CHUNKS):

time: 32 us -> 28.2 us (0.88)
  local copies, waits for them, and re-layouts: 4.25 us -> 0.02 us
  Pallas kernels: 7.05 us -> 7.38 us
    unnamed x18 -> x8, local copies, waits for them, and re-layouts: 4.25 us -> 0.02 us
    pallas_call x2 -> x3, Pallas kernels: 2.51 us -> 2.83 us  [the longest x1 1.88 us: per_device(): pl.pallas_call(functools.partial(first_kernel, lead, wide, cell_blocks),...]
  transfers between devices with their start and end apart: 7 -> 7, of which waited for: 4 -> 5; matrix products, arithmetic and copies ran while one was open for 0% -> 0% of each run, Pallas kernels for 12% -> 13%
where the time goes in v2:
time: 28.2 us; the launch traced here: 28.1 us
  starting transfers between devices  11.7 us (41%)
  waiting for transfers between devices  8.24 us (29%)
  Pallas kernels  7.38 us (26%)
  between operations  0.72 us (3%)
    ppermute x7, starting transfers between devices, shift_along(): lax.ppermute(block, axis, [((i - distance) % size, i) for i in range(size)])  11.7 us
    ppermute x7, waiting for transfers between devices, shift_along(): lax.ppermute(block, axis, [((i - distance) % size, i) for i in range(size)])  8.24 us
    pallas_call x2, Pallas kernels, per_device(): pl.pallas_call(functools.partial(apply_kernel, chunk, slot_groups, cell_b...  3.72 us
    pallas_call x1, Pallas kernels, per_device(): pl.pallas_call(functools.partial(first_kernel, lead, wide, cell_blocks),...  1.88 us
    pallas_call x1, Pallas kernels, per_device(): pl.pallas_call(functools.partial(local_kernel, CHUNKS, cell_blocks), out_...  0.84 us
    pallas_call x1, Pallas kernels, per_device(): pl.pallas_call(functools.partial(gather_kernel, later, every, cell_blocks...  0.57 us
  transfers between devices with their start and end apart: 7, of which 5 were waited for; matrix products, arithmetic and copies ran while one was open for 0% of the time, Pallas kernels for 13%

profile of v2, /device:TPU:0, one launch (start us, length us, event | category | flops | bytes accessed | tf_op | source)
XLA Modules:
  0.0 28.1 jit_solution(14143273197497249035)
XLA Ops:
  0.6 0.0 copy-start.2
  0.6 0.0 copy-start.3
  0.7 0.0 copy-start
  0.7 1.9 %gather_first.1 = (f32[96,512]{1,0:T(8,128)S(1)}, bf16[8,192,128]{2,1,0:T(8,128)(2,1)S(1)}, f32[3,384,128]{2,1,0:T(8,128)S(1)}, s32[4,256]{1,0:T(4,128)S(1)}, f32[48,128]{1,0:T(8,128)S(1)}) custom-call(f32[384,128]{1,0:T(8,128)} %bitcast.41, f32[384,128]{1,0:T(8,128)} %bitcast.42, f32[384,128]{1,0:T(8,128)} %bitcast.43, s32[4,256]{1,0:T(4,128)} %bitcast.44, ...), custom_call_target="tpu_custom_call" | custom-call | flops 201326592 | bytes 589824 | tf_op jit(solution)/shard_map/gather_first/pallas_call | solution.py:283
  2.6 4.1 %collective-permute-start.4 = (f32[96,512]{1,0:T(8,128)S(1)}, f32[96,512]{1,0:T(8,128)S(1)}, u32[]{:S(2)}, u32[]{:S(2)}) collective-permute-start(f32[96,512]{1,0:T(8,128)S(1)} %get-tuple-element.34), channel_id=1, source_target_pairs={{8,0},{12,4},{0,8},{4,12},{9,1},{13,5},{1,9},{5,13},{10,2},{14,6},... | collective-permute-start | bytes 589832 | tf_op jit(solution)/shard_map/ppermute | solution.py:26
  6.7 0.4 %gather_rest.1 = (f32[96,256]{1,0:T(8,128)S(1)}, f32[96,256]{1,0:T(8,128)S(1)}) custom-call(bf16[8,192,128]{2,1,0:T(8,128)(2,1)S(1)} %get-tuple-element.33.parts_ref.refs_3_, s32[4,256]{1,0:T(4,128)S(1)} %get-tuple-element.27.listed), custom_call_target="tpu_custom_call" | custom-call | flops 201326592 | bytes 589824 | tf_op jit(solution)/shard_map/gather_rest/pallas_call | solution.py:306
  7.0 0.0 copy-start.1
  7.0 1.6 %collective-permute-start.5 = (f32[96,256]{1,0:T(8,128)S(1)}, f32[96,256]{1,0:T(8,128)S(1)}, u32[]{:S(2)}, u32[]{:S(2)}) collective-permute-start(f32[96,256]{1,0:T(8,128)S(1)} %get-tuple-element.35), channel_id=1, source_target_pairs={{12,0},{0,4},{4,8},{8,12},{13,1},{1,5},{5,9},{9,13},{14,2},{2,6},{... | collective-permute-start | bytes 294920 | tf_op jit(solution)/shard_map/ppermute | solution.py:26
  8.7 0.0 collective-permute-start
  8.7 2.2 %collective-permute-start.6 = (f32[96,256]{1,0:T(8,128)S(1)}, f32[96,256]{1,0:T(8,128)S(1)}, u32[]{:S(2)}, u32[]{:S(2)}) collective-permute-start(f32[96,256]{1,0:T(8,128)S(1)} %get-tuple-element.36), channel_id=1, source_target_pairs={{4,0},{8,4},{12,8},{0,12},{5,1},{9,5},{13,9},{1,13},{6,2},{10,6},{... | collective-permute-start | bytes 294920 | tf_op jit(solution)/shard_map/ppermute | solution.py:26
  10.9 1.0 %collective-permute-done.refs_1_.prev = f32[48,128]{1,0:T(8,128)S(1)} collective-permute-done((f32[48,128]{1,0:T(8,128)S(1)}, f32[48,128]{1,0:T(8,128)S(1)}, u32[]{:S(2)}, u32[]{:S(2)}) %collective-permute-start) | collective-permute-done | bytes 24608 | tf_op jit(solution)/shard_map/ppermute | solution.py:26
  11.9 0.6 %gather_later.1 = (f32[48,512]{1,0:T(8,128)S(1)}, f32[48,256]{1,0:T(8,128)S(1)}, f32[48,256]{1,0:T(8,128)S(1)}, bf16[8,96,128]{2,1,0:T(8,128)(2,1)S(1)}) custom-call(f32[3,384,128]{2,1,0:T(8,128)S(1)} %get-tuple-element.23.refs_0_.held, f32[48,128]{1,0:T(8,128)S(1)} %collective-permute-done.refs_1_.prev, s32[4,256]{1,0:T(4,128)S(1)} %get-tuple-element.27.listed), custom_call_target="tpu_custom_call" | custom-call | flops 201326592 | bytes 393216 | tf_op jit(solution)/shard_map/gather_later/pallas_call | solution.py:317
  12.5 0.4 %collective-permute-start.1 = (f32[48,512]{1,0:T(8,128)S(1)}, f32[48,512]{1,0:T(8,128)S(1)}, u32[]{:S(2)}, u32[]{:S(2)}) collective-permute-start(f32[48,512]{1,0:T(8,128)S(1)} %get-tuple-element.29), channel_id=1, source_target_pairs={{8,0},{12,4},{0,8},{4,12},{9,1},{13,5},{1,9},{5,13},{10,2},{14,6},... | collective-permute-start | bytes 294920 | tf_op jit(solution)/shard_map/ppermute | solution.py:26
  12.9 2.5 %collective-permute-start.2 = (f32[48,256]{1,0:T(8,128)S(1)}, f32[48,256]{1,0:T(8,128)S(1)}, u32[]{:S(2)}, u32[]{:S(2)}) collective-permute-start(f32[48,256]{1,0:T(8,128)S(1)} %get-tuple-element.30), channel_id=1, source_target_pairs={{12,0},{0,4},{4,8},{8,12},{13,1},{1,5},{5,9},{9,13},{14,2},{2,6},{... | collective-permute-start | bytes 147464 | tf_op jit(solution)/shard_map/ppermute | solution.py:26
  15.4 0.5 %collective-permute-done.5.refs_5_ = f32[96,256]{1,0:T(8,128)S(1)} collective-permute-done((f32[96,256]{1,0:T(8,128)S(1)}, f32[96,256]{1,0:T(8,128)S(1)}, u32[]{:S(2)}, u32[]{:S(2)}) %collective-permute-start.5) | collective-permute-done | bytes 98336 | tf_op jit(solution)/shard_map/ppermute | solution.py:26
  15.9 0.9 %collective-permute-start.3 = (f32[48,256]{1,0:T(8,128)S(1)}, f32[48,256]{1,0:T(8,128)S(1)}, u32[]{:S(2)}, u32[]{:S(2)}) collective-permute-start(f32[48,256]{1,0:T(8,128)S(1)} %get-tuple-element.31), channel_id=1, source_target_pairs={{4,0},{8,4},{12,8},{0,12},{5,1},{9,5},{13,9},{1,13},{6,2},{10,6},{... | collective-permute-start | bytes 147464 | tf_op jit(solution)/shard_map/ppermute | solution.py:26
  16.7 0.0 copy-done.2
  16.7 0.0 copy-done.3
  16.7 0.0 copy-done
  16.8 0.8 %local_terms.1 = (f32[8,96,128]{2,1,0:T(8,128)S(1)}, f32[8,48,128]{2,1,0:T(8,128)S(1)}, bf16[8,384,256]{2,1,0:T(8,128)(2,1)S(1)}) custom-call(f32[3,384,128]{2,1,0:T(8,128)S(1)} %get-tuple-element.23.refs_0_.held, f32[48,128]{1,0:T(8,128)S(1)} %collective-permute-done.refs_1_.prev, f32[8,128]{1,0:T(8,128)S(1)} %bitcast.36, f32[8,128]{1,0:T(8,128)S(1)} %bitcast.37, ...), custom_call_target="tpu_custom_call" | custom-call | flops 8847360 | bytes 1572864 | tf_op jit(solution)/shard_map/local_terms/pallas_call | solution.py:331
  17.6 0.1 collective-permute-done.6.refs_6_
  17.7 4.2 %collective-permute-done.4.refs_4_ = f32[96,512]{1,0:T(8,128)S(1)} collective-permute-done((f32[96,512]{1,0:T(8,128)S(1)}, f32[96,512]{1,0:T(8,128)S(1)}, u32[]{:S(2)}, u32[]{:S(2)}) %collective-permute-start.4) | collective-permute-done | bytes 196640 | tf_op jit(solution)/shard_map/ppermute | solution.py:26
  21.9 0.0 copy-done.1
  21.9 2.0 %apply_tiles.2 = (f32[384,128]{1,0:T(8,128)}, f32[384,128]{1,0:T(8,128)}, f32[384,128]{1,0:T(8,128)}) custom-call(s32[3,8]{1,0:T(4,128)S(1)} %bitcast.34, bf16[8,384,256]{2,1,0:T(8,128)(2,1)S(1)} %get-tuple-element.25.refs_1_, f32[8,96,128]{2,1,0:T(8,128)S(1)} %get-tuple-element.32.refs_2_, bf16[8,192,128]{2,1,0:T(8,128)(2,1)S(1)} %get-tuple-element.33.parts_ref.refs_3_, ...), custom_call_target="tpu_custom_call" | custom-call | flops 301989888 | bytes 786432 | tf_op jit(solution)/shard_map/apply_tiles/pallas_call | solution.py:348
  23.9 0.0 collective-permute-done.2.refs_5_
  23.9 2.4 %collective-permute-done.3.refs_6_ = f32[48,256]{1,0:T(8,128)S(1)} collective-permute-done((f32[48,256]{1,0:T(8,128)S(1)}, f32[48,256]{1,0:T(8,128)S(1)}, u32[]{:S(2)}, u32[]{:S(2)}) %collective-permute-start.3) | collective-permute-done | bytes 49184 | tf_op jit(solution)/shard_map/ppermute | solution.py:26
  26.3 0.0 collective-permute-done.1.refs_4_
  26.4 1.7 %apply_tiles.3 = (f32[384,128]{1,0:T(8,128)}, f32[384,128]{1,0:T(8,128)}, f32[384,128]{1,0:T(8,128)}) custom-call(s32[3,8]{1,0:T(4,128)S(1)} %bitcast.35, bf16[8,384,256]{2,1,0:T(8,128)(2,1)S(1)} %get-tuple-element.25.refs_1_, f32[8,48,128]{2,1,0:T(8,128)S(1)} %get-tuple-element.26.refs_2_, ...), custom_call_target="tpu_custom_call", output_to_operand_aliasing={{0}: (7, {}), {1}: (8, {}), {2}: (9, {})} | custom-call | flops 150994944 | bytes 393216 | tf_op jit(solution)/shard_map/apply_tiles/pallas_call | solution.py:348
Async XLA Ops:
  0.6 16.1 %copy-start.2 = (f32[1024]{0:T(1024)S(1)}, f32[1024]{0:T(1024)}, u32[]{:S(2)}) copy-start(f32[1024]{0:T(1024)} %param.12) | copy-start | bytes 12292
  0.6 16.1 %copy-start.3 = (f32[1024]{0:T(1024)S(1)}, f32[1024]{0:T(1024)}, u32[]{:S(2)}) copy-start(f32[1024]{0:T(1024)} %param.13) | copy-start | bytes 12292
  0.7 16.1 %copy-start = (f32[8,3,128,128]{3,2,1,0:T(8,128)S(1)}, f32[8,3,128,128]{3,2,1,0:T(8,128)}, u32[]{:S(2)}) copy-start(f32[8,3,128,128]{3,2,1,0:T(8,128)} %refs_4_.3) | copy-start | bytes 4718596
  2.6 19.4 %collective-permute-start.4 = (f32[96,512]{1,0:T(8,128)S(1)}, f32[96,512]{1,0:T(8,128)S(1)}, u32[]{:S(2)}, u32[]{:S(2)}) collective-permute-start(f32[96,512]{1,0:T(8,128)S(1)} %get-tuple-element.34), channel_id=1, source_target_pairs={{8,0},{12,4},{0,8},{4,12},{9,1},{13,5},{1,9},{5,13},{10,2},{14,6},... | collective-permute-start | bytes 589832 | tf_op jit(solution)/shard_map/ppermute | solution.py:26
  7.0 14.9 %copy-start.1 = (s32[8,3]{0,1:T(4,128)S(1)}, s32[8,3]{0,1:T(4,128)}, u32[]{:S(2)}) copy-start(s32[8,3]{0,1:T(4,128)} %param.15) | copy-start | bytes 292
  7.0 8.8 %collective-permute-start.5 = (f32[96,256]{1,0:T(8,128)S(1)}, f32[96,256]{1,0:T(8,128)S(1)}, u32[]{:S(2)}, u32[]{:S(2)}) collective-permute-start(f32[96,256]{1,0:T(8,128)S(1)} %get-tuple-element.35), channel_id=1, source_target_pairs={{12,0},{0,4},{4,8},{8,12},{13,1},{1,5},{5,9},{9,13},{14,2},{2,6},{... | collective-permute-start | bytes 294920 | tf_op jit(solution)/shard_map/ppermute | solution.py:26
  8.7 3.3 %collective-permute-start = (f32[48,128]{1,0:T(8,128)S(1)}, f32[48,128]{1,0:T(8,128)S(1)}, u32[]{:S(2)}, u32[]{:S(2)}) collective-permute-start(f32[48,128]{1,0:T(8,128)S(1)} %get-tuple-element.24), channel_id=1, source_target_pairs={{3,0},{0,1},{1,2},{2,3},{7,4},{4,5},{5,6},{6,7},{11,8},{8,9},{9,10... | collective-permute-start | bytes 73736 | tf_op jit(solution)/shard_map/ppermute | solution.py:26
  8.7 9.0 %collective-permute-start.6 = (f32[96,256]{1,0:T(8,128)S(1)}, f32[96,256]{1,0:T(8,128)S(1)}, u32[]{:S(2)}, u32[]{:S(2)}) collective-permute-start(f32[96,256]{1,0:T(8,128)S(1)} %get-tuple-element.36), channel_id=1, source_target_pairs={{4,0},{8,4},{12,8},{0,12},{5,1},{9,5},{13,9},{1,13},{6,2},{10,6},{... | collective-permute-start | bytes 294920 | tf_op jit(solution)/shard_map/ppermute | solution.py:26
  12.5 13.8 %collective-permute-start.1 = (f32[48,512]{1,0:T(8,128)S(1)}, f32[48,512]{1,0:T(8,128)S(1)}, u32[]{:S(2)}, u32[]{:S(2)}) collective-permute-start(f32[48,512]{1,0:T(8,128)S(1)} %get-tuple-element.29), channel_id=1, source_target_pairs={{8,0},{12,4},{0,8},{4,12},{9,1},{13,5},{1,9},{5,13},{10,2},{14,6},... | collective-permute-start | bytes 294920 | tf_op jit(solution)/shard_map/ppermute | solution.py:26
  12.9 11.0 %collective-permute-start.2 = (f32[48,256]{1,0:T(8,128)S(1)}, f32[48,256]{1,0:T(8,128)S(1)}, u32[]{:S(2)}, u32[]{:S(2)}) collective-permute-start(f32[48,256]{1,0:T(8,128)S(1)} %get-tuple-element.30), channel_id=1, source_target_pairs={{12,0},{0,4},{4,8},{8,12},{13,1},{1,5},{5,9},{9,13},{14,2},{2,6},{... | collective-permute-start | bytes 147464 | tf_op jit(solution)/shard_map/ppermute | solution.py:26
  15.9 10.5 %collective-permute-start.3 = (f32[48,256]{1,0:T(8,128)S(1)}, f32[48,256]{1,0:T(8,128)S(1)}, u32[]{:S(2)}, u32[]{:S(2)}) collective-permute-start(f32[48,256]{1,0:T(8,128)S(1)} %get-tuple-element.31), channel_id=1, source_target_pairs={{4,0},{8,4},{12,8},{0,12},{5,1},{9,5},{13,9},{1,13},{6,2},{10,6},{... | collective-permute-start | bytes 147464 | tf_op jit(solution)/shard_map/ppermute | solution.py:26

commit v3 on v2

v3 whole, which is shorter than its diff:
```python
import functools

import jax
import jax.numpy as jnp
from jax import lax
from jax.experimental import pallas as pl
from jax.experimental.pallas import tpu as pltpu
from jax.sharding import PartitionSpec as P

OFFSETS = (1, -1, 2, -2)
time_step = 0.5
spread_u = 1.0
spread_v = 0.5
LANES = 128
STEPS = 8
FIELDS = 3
VMEM = pltpu.VMEM
SMEM = pltpu.SMEM
F32 = jnp.float32
BF16 = jnp.bfloat16


def shift_along(block, axis, distance):
    size = lax.axis_size(axis)
    return lax.ppermute(block, axis, [((i - distance) % size, i) for i in range(size)])


def steps_at(ref, group, cell_block, species, stride):
    return ref[pl.ds(group * STEPS * stride + cell_block * 2 + species, STEPS, stride=stride), :]


def steps_before(ref, prev_ref, field, group, cell_block, species, stride):
    offset = cell_block * 2 + species
    if group > 0:
        return ref[pl.ds((group * STEPS - 1) * stride + offset, STEPS, stride=stride), :]
    now = steps_at(ref, 0, cell_block, species, stride)
    row = field * stride + offset
    first = jnp.broadcast_to(prev_ref[row : row + 1, :], now.shape)
    index = lax.broadcasted_iota(jnp.int32, now.shape, 0)
    return jnp.where(index == 0, first, pltpu.roll(now, 1, 0))


def split(values):
    high = values.astype(BF16)
    return high, (values - high.astype(F32)).astype(BF16)


def summed_parts(groups, cell_blocks, fields, prev, parts_ref, high_row, low_row):
    stride = 2 * cell_blocks
    for place, group in enumerate(groups):
        for field in range(FIELDS):
            row = (place * FIELDS + field) * 2 * STEPS
            for block in range(cell_blocks):
                both = []
                for species, scale in enumerate((-0.5 * spread_u, -0.5 * spread_v)):
                    now = steps_at(fields[field], group, block, species, stride)
                    before = steps_before(fields[field], prev, field, group, block, species, stride)
                    both.append((now + before) * scale)
                high, low = split(jnp.concatenate(both, axis=0))
                parts_ref[block, high_row + row : high_row + row + 2 * STEPS, :] = high
                parts_ref[block, low_row + row : low_row + row + 2 * STEPS, :] = low


def choose_rows(slots, listed_ref, choose):
    cells = choose.shape[0]
    slot_rows = listed_ref.shape[1]
    cell = lax.broadcasted_iota(jnp.int32, (LANES, slot_rows), 0)
    for place, slot in enumerate(slots):
        listed = listed_ref[slot : slot + 1, :]
        for start in range(0, cells, LANES):
            hit = cell == listed - start
            choose[start : start + LANES, place * slot_rows : (place + 1) * slot_rows] = jnp.where(
                hit, 1.0, 0.0
            ).astype(BF16)


def take_rows(parts, choose, sends):
    size = parts.shape[0] // 2
    start = 0
    for send in sends:
        width = send.shape[1]
        taken = jnp.dot(parts, choose[:, start : start + width], preferred_element_type=F32)
        send[...] = taken[:size] + taken[size:]
        start += width


def side_by_side(parts_ref, rows):
    blocks = [
        jnp.concatenate([parts_ref[b, start : start + count, :] for start, count in rows], axis=0)
        for b in range(parts_ref.shape[0])
    ]
    return jnp.concatenate(blocks, axis=1)


def first_kernel(lead, slots, cell_blocks, *refs):
    refs = list(refs)
    sources = [refs.pop(0) for _ in range(FIELDS)]
    rows_hbm, count_hbm, send, parts_ref, held, listed, last, choose, rows_ref, count_ref, sems = refs
    stride = 2 * cell_blocks
    early = (lead[0] * STEPS - 1) * stride
    late = held.shape[1] - early
    small = [
        pltpu.make_async_copy(rows_hbm, rows_ref, sems.at[2 * FIELDS]),
        pltpu.make_async_copy(count_hbm, count_ref, sems.at[2 * FIELDS + 1]),
    ]
    needed = [
        pltpu.make_async_copy(sources[f].at[pl.ds(early, late), :], held.at[f, pl.ds(early, late), :], sems.at[f])
        for f in range(FIELDS)
    ]
    others = [
        pltpu.make_async_copy(sources[f].at[pl.ds(0, early), :], held.at[f, pl.ds(0, early), :], sems.at[FIELDS + f])
        for f in range(FIELDS)
    ]
    for copy in small + needed + others:
        copy.start()
    for copy in small:
        copy.wait()
    lane = lax.broadcasted_iota(jnp.int32, rows_ref.shape, 1)
    for slot in range(rows_ref.shape[0]):
        listed[slot : slot + 1, :] = jnp.where(
            lane[slot : slot + 1] < count_ref[:, slot : slot + 1], rows_ref[slot : slot + 1, :], -1
        )
    choose_rows(slots, listed, choose)
    for copy in needed:
        copy.wait()
    size = parts_ref.shape[1] // 2
    summed_parts(lead, cell_blocks, [held.at[f] for f in range(FIELDS)], None, parts_ref, 0, size)
    take_rows(side_by_side(parts_ref, [(0, 2 * size)]), choose, [send])
    for field in range(FIELDS):
        last[field * stride : (field + 1) * stride, :] = held[field, -stride:, :]
    for copy in others:
        copy.wait()


def rest_kernel(late, wide, others, cell_blocks, held, prev, listed, lead_parts, send, *refs):
    *sends, parts_ref, choose = refs
    size = parts_ref.shape[1] // 2
    lead_size = lead_parts.shape[1] // 2
    late_size = size - lead_size
    choose_rows(others + wide, listed, choose)
    parts_ref[:, late_size:size, :] = lead_parts[:, :lead_size, :]
    parts_ref[:, size + late_size :, :] = lead_parts[:, lead_size:, :]
    summed_parts(late, cell_blocks, [held.at[f] for f in range(FIELDS)], prev, parts_ref, 0, size)
    take_rows(side_by_side(parts_ref, [(0, 2 * size)]), choose, sends)
    narrow_width = choose.shape[1] - send.shape[1]
    late_parts = side_by_side(parts_ref, [(0, late_size), (size, late_size)])
    take_rows(late_parts, choose.at[:, narrow_width:], [send])


def pointwise(u, v, du, dv, ddu, ddv, feed, total):
    square = v * v
    product = u * square
    twice = 2.0 * u * v
    outs = [feed * (1.0 - u) - product, product - total * v]
    for first, second in ((du, dv), (ddu, ddv)):
        react = square * first + twice * second
        outs += [-react - feed * first, react - total * second]
    return outs


def local_kernel(groups, cell_blocks, held, prev, feed_ref, kill_ref, tiles, base, split_tiles):
    fields = [held.at[f] for f in range(FIELDS)]
    stride = 2 * cell_blocks
    pairs = [(f, s) for f in range(FIELDS) for s in range(2)]
    for place, group in enumerate(groups):
        for block in range(cell_blocks):
            feed = feed_ref[block : block + 1, :]
            total = feed + kill_ref[block : block + 1, :]
            now = [steps_at(fields[f], group, block, s, stride) for f, s in pairs]
            before = [steps_before(fields[f], prev, f, group, block, s, stride) for f, s in pairs]
            rate_now = pointwise(*now, feed, total)
            rate_before = pointwise(*before, feed, total)
            for index in range(2 * FIELDS):
                row = (place * FIELDS * 2 + index) * STEPS
                base[block, row : row + STEPS, :] = (now[index] - before[index]) * (1.0 / time_step) - 0.5 * (
                    rate_now[index] + rate_before[index]
                )
    blocks, per_row = tiles.shape[:2]
    for block in range(blocks):
        for k in range(per_row):
            high, low = split(jnp.transpose(tiles[block, k]))
            split_tiles[block, k * LANES : (k + 1) * LANES, :LANES] = high
            split_tiles[block, k * LANES : (k + 1) * LANES, LANES:] = low


def apply_kernel(wide, narrow, cell_blocks, blocks, per_row, *refs):
    refs = list(refs)
    cols, split_tiles, base, parts_ref, wide_lead, wide_late = [refs.pop(0) for _ in range(6)]
    arrived = [refs.pop(0) for _ in narrow]
    outs = [refs.pop(0) for _ in range(FIELDS)]
    extended, made, sems = refs
    stride = 2 * cell_blocks
    size = base.shape[1]
    late_size = wide_late.shape[0]
    extended[:cell_blocks] = parts_ref[...]
    received = [(wide_late, wide, 0), (wide_lead, wide, late_size)]
    received += [(ref, slots, 0) for ref, slots in zip(arrived, narrow)]
    for ref, slots, row in received:
        count, width = ref.shape
        per_slot = width // len(slots) // LANES
        for place, slot in enumerate(slots):
            for b in range(per_slot):
                lane = (place * per_slot + b) * LANES
                high, low = split(ref[:, lane : lane + LANES])
                extended[cell_blocks + slot * per_slot + b, row : row + count, :] = high
                extended[cell_blocks + slot * per_slot + b, size + row : size + row + count, :] = low
    for block in range(blocks):
        chosen = jnp.concatenate([extended[cols[k, block]] for k in range(per_row)], axis=1)
        product = jnp.dot(chosen, split_tiles[block], preferred_element_type=F32)
        product = product[:, :LANES] + product[:, LANES:]
        result = base[block] + (product[:size] + product[size:])
        for index in range(size // STEPS):
            group, field, species = index // (2 * FIELDS), index // 2 % FIELDS, index % 2
            at = group * STEPS * stride + block * 2 + species
            made[field, pl.ds(at, STEPS, stride=stride), :] = result[index * STEPS : (index + 1) * STEPS, :]
    copies = [pltpu.make_async_copy(made.at[f], outs[f], sems.at[f]) for f in range(FIELDS)]
    for copy in copies:
        copy.start()
    for copy in copies:
        copy.wait()


def per_device(state, dir_one, dir_two, feed, kill, tiles, tile_cols, send_rows, send_count):
    steps, _, cells = state.shape
    cell_blocks = cells // LANES
    stride = 2 * cell_blocks
    blocks, per_row = tiles.shape[:2]
    slot_rows = send_rows.shape[2]
    size_dom = lax.axis_size("dom")

    by_route = {}
    for slot, offset in enumerate(OFFSETS):
        by_route.setdefault(offset % size_dom, []).append(slot)
    slot_groups = sorted(by_route.values(), key=lambda slots: -len(slots))

    def view(array):
        array = array.reshape(steps, 2, cell_blocks, LANES).transpose(0, 2, 1, 3)
        return array.reshape(steps * stride, LANES)

    def unview(array):
        array = array.reshape(steps, cell_blocks, 2, LANES).transpose(0, 2, 1, 3)
        return array.reshape(steps, 2, cells)

    fields = [view(state), view(dir_one), view(dir_two)]
    rows = send_rows.reshape(send_rows.shape[1:])
    counts = send_count
    cols = tile_cols.T
    feed = feed.reshape(cell_blocks, LANES)
    kill = kill.reshape(cell_blocks, LANES)

    vmem = pl.BlockSpec(memory_space=VMEM)
    smem = pl.BlockSpec(memory_space=SMEM)
    anywhere = pl.BlockSpec(memory_space=pl.ANY)
    params = pltpu.CompilerParams(vmem_limit_bytes=16 * 1024 * 1024)

    groups = tuple(range(steps // STEPS))
    late, lead = groups[:1], groups[1:]
    wide, *narrow = slot_groups
    others = [slot for slots in narrow for slot in slots]

    def rows_of(part):
        return len(part) * FIELDS * 2 * STEPS

    def f32(*shape):
        return jax.ShapeDtypeStruct(shape, F32)

    def bf16(*shape):
        return jax.ShapeDtypeStruct(shape, BF16)

    def cost(flops, moved):
        return pl.CostEstimate(flops=flops, bytes_accessed=moved, transcendentals=0)

    hbm = pl.BlockSpec(memory_space=pltpu.HBM)
    size = rows_of(groups)
    wide_width = len(wide) * slot_rows
    in_hbm = [pltpu.with_memory_space_constraint(x, pltpu.HBM) for x in (*fields, rows, counts)]
    send, lead_parts, held, listed, last = pl.pallas_call(
        functools.partial(first_kernel, lead, wide, cell_blocks),
        out_shape=[
            f32(rows_of(lead), wide_width),
            bf16(cell_blocks, 2 * rows_of(lead), LANES),
            f32(FIELDS, steps * stride, LANES),
            jax.ShapeDtypeStruct(rows.shape, jnp.int32),
            f32(FIELDS * stride, LANES),
        ],
        in_specs=[hbm] * (FIELDS + 2),
        out_specs=[vmem] * 5,
        scratch_shapes=[
            VMEM((cells, wide_width), BF16),
            VMEM(rows.shape, jnp.int32),
            VMEM(counts.shape, jnp.int32),
            pltpu.SemaphoreType.DMA((2 * FIELDS + 2,)),
        ],
        compiler_params=params,
        cost_estimate=cost(4 * rows_of(lead) * cells * wide_width, 8 * size * cells),
        name="gather_first",
    )(*in_hbm)
    wide_lead = shift_along(send, "dom", OFFSETS[wide[0]])
    prev = shift_along(last, "tm", 1)
    send, *sends, parts = pl.pallas_call(
        functools.partial(rest_kernel, late, wide, others, cell_blocks),
        out_shape=[f32(rows_of(late), wide_width)]
        + [f32(size, len(slots) * slot_rows) for slots in narrow]
        + [bf16(cell_blocks, 2 * size, LANES)],
        in_specs=[vmem] * 4,
        out_specs=[vmem] * (len(narrow) + 2),
        scratch_shapes=[VMEM((cells, len(OFFSETS) * slot_rows), BF16)],
        compiler_params=params,
        cost_estimate=cost(4 * size * cells * len(OFFSETS) * slot_rows, 8 * size * cells),
        name="gather_rest",
    )(held, prev, listed, lead_parts)
    arrived = [shift_along(part, "dom", OFFSETS[slots[0]]) for part, slots in zip(sends, narrow)]
    wide_late = shift_along(send, "dom", OFFSETS[wide[0]])

    base, split_tiles = pl.pallas_call(
        functools.partial(local_kernel, groups, cell_blocks),
        out_shape=[f32(cell_blocks, size, LANES), bf16(blocks, per_row * LANES, 2 * LANES)],
        in_specs=[vmem] * 5,
        out_specs=[vmem] * 2,
        compiler_params=params,
        cost_estimate=cost(60 * size * cells, 8 * tiles.size),
        name="local_terms",
    )(held, prev, feed, kill, tiles)

    outs = pl.pallas_call(
        functools.partial(apply_kernel, wide, narrow, cell_blocks, blocks, per_row),
        out_shape=[f32(steps * stride, LANES)] * FIELDS,
        in_specs=[smem] + [vmem] * (5 + len(narrow)),
        out_specs=[anywhere] * FIELDS,
        scratch_shapes=[
            VMEM((cell_blocks + len(OFFSETS) * slot_rows // LANES, 2 * size, LANES), BF16),
            VMEM((FIELDS, steps * stride, LANES), F32),
            pltpu.SemaphoreType.DMA((FIELDS,)),
        ],
        compiler_params=params,
        cost_estimate=cost(8 * size * blocks * per_row * LANES * LANES, 16 * size * cells),
        name="apply_tiles",
    )(cols, split_tiles, base, parts, wide_lead, wide_late, *arrived)
    return tuple(unview(out) for out in outs)


def solution(mesh):
    fields = P(("group", "tm"), None, "dom")
    in_specs = (
        fields,
        fields,
        fields,
        P("dom"),
        P("dom"),
        P("dom", None, None, None),
        P("dom", None),
        P("dom", None, None),
        P("dom", None),
    )
    return jax.shard_map(
        per_device, mesh=mesh, in_specs=in_specs, out_specs=(fields, fields, fields), check_vma=False
    )
```

time: 28.2 us -> 29.2 us (1.035); the launches traced: 28.1 us -> 28.8 us
  waiting for transfers between devices: 8.24 us -> 12.8 us
  starting transfers between devices: 11.7 us -> 9.41 us
  Pallas kernels: 7.38 us -> 5.79 us
    ppermute x7 -> x5, waiting for transfers between devices: 8.24 us -> 12.8 us  [shift_along(): lax.ppermute(block, axis, [((i - distance) % size, i) for i in range(size)])]
    ppermute x7 -> x5, starting transfers between devices: 11.7 us -> 9.41 us  [shift_along(): lax.ppermute(block, axis, [((i - distance) % size, i) for i in range(size)])]
    pallas_call x5 -> x3, Pallas kernels: 5.5 us -> 3.91 us  [the longest x1 2.34 us: per_device(): pl.pallas_call(functools.partial(apply_kernel, wide, narrow, cell_blocks,...]
  transfers between devices with their start and end apart: 7 -> 5, of which waited for: 5 -> 1; matrix products, arithmetic and copies ran while one was open for 0% -> 0% of each run, Pallas kernels for 13% -> 5%
where the time goes in v3:
time: 29.2 us; the launch traced here: 28.8 us
  waiting for transfers between devices  12.8 us (44%)
  starting transfers between devices  9.41 us (32%)
  Pallas kernels  5.79 us (20%)
  between operations  0.71 us (2%)
    ppermute x5, waiting for transfers between devices, shift_along(): lax.ppermute(block, axis, [((i - distance) % size, i) for i in range(size)])  12.8 us
    ppermute x5, starting transfers between devices, shift_along(): lax.ppermute(block, axis, [((i - distance) % size, i) for i in range(size)])  9.41 us
    pallas_call x1, Pallas kernels, per_device(): pl.pallas_call(functools.partial(apply_kernel, wide, narrow, cell_blocks,...  2.34 us
    pallas_call x1, Pallas kernels, per_device(): pl.pallas_call(functools.partial(first_kernel, lead, wide, cell_blocks),...  1.88 us
    pallas_call x1, Pallas kernels, per_device(): pl.pallas_call(functools.partial(local_kernel, groups, cell_blocks), out_...  0.83 us
    pallas_call x1, Pallas kernels, per_device(): pl.pallas_call(functools.partial(rest_kernel, late, wide, others, cell_bl...  0.73 us
  transfers between devices with their start and end apart: 5, of which 1 were waited for; matrix products, arithmetic and copies ran while one was open for 0% of the time, Pallas kernels for 5%

profile of v3, /device:TPU:0, one launch (start us, length us, event | category | flops | bytes accessed | tf_op | source)
XLA Modules:
  0.0 28.8 jit_solution(13688436812684812050)
XLA Ops:
  0.6 0.0 copy-start
  0.6 0.0 copy-start.2
  0.7 0.0 copy-start.1
  0.7 1.9 %gather_first.1 = (f32[96,512]{1,0:T(8,128)S(1)}, bf16[8,192,128]{2,1,0:T(8,128)(2,1)S(1)}, f32[3,384,128]{2,1,0:T(8,128)S(1)}, s32[4,256]{1,0:T(4,128)S(1)}, f32[48,128]{1,0:T(8,128)S(1)}) custom-call(f32[384,128]{1,0:T(8,128)} %bitcast.37, f32[384,128]{1,0:T(8,128)} %bitcast.38, f32[384,128]{1,0:T(8,128)} %bitcast.39, s32[4,256]{1,0:T(4,128)} %bitcast.43, ...), custom_call_target="tpu_custom_call" | custom-call | flops 201326592 | bytes 1179648 | tf_op jit(solution)/shard_map/gather_first/pallas_call | solution.py:277
  2.6 0.5 %collective-permute-start = (f32[48,128]{1,0:T(8,128)S(1)}, f32[48,128]{1,0:T(8,128)S(1)}, u32[]{:S(2)}, u32[]{:S(2)}) collective-permute-start(f32[48,128]{1,0:T(8,128)S(1)} %get-tuple-element.18), channel_id=1, source_target_pairs={{3,0},{0,1},{1,2},{2,3},{7,4},{4,5},{5,6},{6,7},{11,8},{8,9},{9,10... | collective-permute-start | bytes 73736 | tf_op jit(solution)/shard_map/ppermute | solution.py:25
  3.1 3.7 %collective-permute-start.1 = (f32[96,512]{1,0:T(8,128)S(1)}, f32[96,512]{1,0:T(8,128)S(1)}, u32[]{:S(2)}, u32[]{:S(2)}) collective-permute-start(f32[96,512]{1,0:T(8,128)S(1)} %get-tuple-element.24), channel_id=1, source_target_pairs={{8,0},{12,4},{0,8},{4,12},{9,1},{13,5},{1,9},{5,13},{10,2},{14,6},... | collective-permute-start | bytes 589832 | tf_op jit(solution)/shard_map/ppermute | solution.py:25
  6.7 0.0 collective-permute-done.prev
  6.7 0.7 %gather_rest.1 = (f32[48,512]{1,0:T(8,128)S(1)}, f32[144,256]{1,0:T(8,128)S(1)}, f32[144,256]{1,0:T(8,128)S(1)}, bf16[8,288,128]{2,1,0:T(8,128)(2,1)S(1)}) custom-call(f32[3,384,128]{2,1,0:T(8,128)S(1)} %get-tuple-element.17.held, f32[48,128]{1,0:T(8,128)S(1)} %collective-permute-done.prev, s32[4,256]{1,0:T(4,128)S(1)} %get-tuple-element.21.listed, ...), custom_call_target="tpu_custom_call" | custom-call | flops 603979776 | bytes 1179648 | tf_op jit(solution)/shard_map/gather_rest/pallas_call | solution.py:300
  7.5 0.0 copy-start.3
  7.5 2.2 %collective-permute-start.3 = (f32[144,256]{1,0:T(8,128)S(1)}, f32[144,256]{1,0:T(8,128)S(1)}, u32[]{:S(2)}, u32[]{:S(2)}) collective-permute-start(f32[144,256]{1,0:T(8,128)S(1)} %get-tuple-element.26), channel_id=1, source_target_pairs={{12,0},{0,4},{4,8},{8,12},{13,1},{1,5},{5,9},{9,13},{14,2},{2,6},{... | collective-permute-start | bytes 442376 | tf_op jit(solution)/shard_map/ppermute | solution.py:25
  9.7 2.1 %collective-permute-start.4 = (f32[144,256]{1,0:T(8,128)S(1)}, f32[144,256]{1,0:T(8,128)S(1)}, u32[]{:S(2)}, u32[]{:S(2)}) collective-permute-start(f32[144,256]{1,0:T(8,128)S(1)} %get-tuple-element.27), channel_id=1, source_target_pairs={{4,0},{8,4},{12,8},{0,12},{5,1},{9,5},{13,9},{1,13},{6,2},{10,6},{... | collective-permute-start | bytes 442376 | tf_op jit(solution)/shard_map/ppermute | solution.py:25
  11.8 0.9 %collective-permute-start.2 = (f32[48,512]{1,0:T(8,128)S(1)}, f32[48,512]{1,0:T(8,128)S(1)}, u32[]{:S(2)}, u32[]{:S(2)}) collective-permute-start(f32[48,512]{1,0:T(8,128)S(1)} %get-tuple-element.25), channel_id=1, source_target_pairs={{8,0},{12,4},{0,8},{4,12},{9,1},{13,5},{1,9},{5,13},{10,2},{14,6},... | collective-permute-start | bytes 294920 | tf_op jit(solution)/shard_map/ppermute | solution.py:25
  12.7 0.0 copy-done
  12.7 0.0 copy-done.2
  12.7 0.0 copy-done.1
  12.7 0.8 %local_terms.1 = (f32[8,144,128]{2,1,0:T(8,128)S(1)}, bf16[8,384,256]{2,1,0:T(8,128)(2,1)S(1)}) custom-call(f32[3,384,128]{2,1,0:T(8,128)S(1)} %get-tuple-element.17.held, f32[48,128]{1,0:T(8,128)S(1)} %collective-permute-done.prev, f32[8,128]{1,0:T(8,128)S(1)} %bitcast.34, f32[8,128]{1,0:T(8,128)S(1)} %bitcast.35, f32[8,3,128,128]{3,2,1,0:T(8,128)S(1)} %copy-done), custom_call_target="tpu_custom_call" | custom-call | flops 8847360 | bytes 3145728 | tf_op jit(solution)/shard_map/local_terms/pallas_call | solution.py:315
  13.6 12.8 %collective-permute-done.2.refs_5_ = f32[48,512]{1,0:T(8,128)S(1)} collective-permute-done((f32[48,512]{1,0:T(8,128)S(1)}, f32[48,512]{1,0:T(8,128)S(1)}, u32[]{:S(2)}, u32[]{:S(2)}) %collective-permute-start.2) | collective-permute-done | bytes 98336 | tf_op jit(solution)/shard_map/ppermute | solution.py:25
  26.4 0.0 collective-permute-done.3.refs_6_
  26.4 0.0 collective-permute-done.4.refs_7_
  26.4 0.0 collective-permute-done.1.refs_4_
  26.4 0.0 copy-done.3
  26.4 2.3 %apply_tiles.1 = (f32[384,128]{1,0:T(8,128)}, f32[384,128]{1,0:T(8,128)}, f32[384,128]{1,0:T(8,128)}) custom-call(s32[3,8]{1,0:T(4,128)S(1)} %bitcast.36, bf16[8,384,256]{2,1,0:T(8,128)(2,1)S(1)} %get-tuple-element.19.refs_1_, f32[8,144,128]{2,1,0:T(8,128)S(1)} %get-tuple-element.20.refs_2_, bf16[8,288,128]{2,1,0:T(8,128)(2,1)S(1)} %get-tuple-element.23.refs_3_, ...), custom_call_target="tpu_custom_call" | custom-call | flops 452984832 | bytes 2359296 | tf_op jit(solution)/shard_map/apply_tiles/pallas_call | solution.py:325
Async XLA Ops:
  0.6 12.1 %copy-start = (f32[8,3,128,128]{3,2,1,0:T(8,128)S(1)}, f32[8,3,128,128]{3,2,1,0:T(8,128)}, u32[]{:S(2)}) copy-start(f32[8,3,128,128]{3,2,1,0:T(8,128)} %tiles.1) | copy-start | bytes 4718596
  0.6 12.1 %copy-start.2 = (f32[1024]{0:T(1024)S(1)}, f32[1024]{0:T(1024)}, u32[]{:S(2)}) copy-start(f32[1024]{0:T(1024)} %param.13) | copy-start | bytes 12292
  0.7 12.1 %copy-start.1 = (f32[1024]{0:T(1024)S(1)}, f32[1024]{0:T(1024)}, u32[]{:S(2)}) copy-start(f32[1024]{0:T(1024)} %param.12) | copy-start | bytes 12292
  2.6 4.2 %collective-permute-start = (f32[48,128]{1,0:T(8,128)S(1)}, f32[48,128]{1,0:T(8,128)S(1)}, u32[]{:S(2)}, u32[]{:S(2)}) collective-permute-start(f32[48,128]{1,0:T(8,128)S(1)} %get-tuple-element.18), channel_id=1, source_target_pairs={{3,0},{0,1},{1,2},{2,3},{7,4},{4,5},{5,6},{6,7},{11,8},{8,9},{9,10... | collective-permute-start | bytes 73736 | tf_op jit(solution)/shard_map/ppermute | solution.py:25
  3.1 23.4 %collective-permute-start.1 = (f32[96,512]{1,0:T(8,128)S(1)}, f32[96,512]{1,0:T(8,128)S(1)}, u32[]{:S(2)}, u32[]{:S(2)}) collective-permute-start(f32[96,512]{1,0:T(8,128)S(1)} %get-tuple-element.24), channel_id=1, source_target_pairs={{8,0},{12,4},{0,8},{4,12},{9,1},{13,5},{1,9},{5,13},{10,2},{14,6},... | collective-permute-start | bytes 589832 | tf_op jit(solution)/shard_map/ppermute | solution.py:25
  7.5 19.0 %copy-start.3 = (s32[8,3]{0,1:T(4,128)S(1)}, s32[8,3]{0,1:T(4,128)}, u32[]{:S(2)}) copy-start(s32[8,3]{0,1:T(4,128)} %param.15) | copy-start | bytes 292
  7.5 18.9 %collective-permute-start.3 = (f32[144,256]{1,0:T(8,128)S(1)}, f32[144,256]{1,0:T(8,128)S(1)}, u32[]{:S(2)}, u32[]{:S(2)}) collective-permute-start(f32[144,256]{1,0:T(8,128)S(1)} %get-tuple-element.26), channel_id=1, source_target_pairs={{12,0},{0,4},{4,8},{8,12},{13,1},{1,5},{5,9},{9,13},{14,2},{2,6},{... | collective-permute-start | bytes 442376 | tf_op jit(solution)/shard_map/ppermute | solution.py:25
  9.7 16.7 %collective-permute-start.4 = (f32[144,256]{1,0:T(8,128)S(1)}, f32[144,256]{1,0:T(8,128)S(1)}, u32[]{:S(2)}, u32[]{:S(2)}) collective-permute-start(f32[144,256]{1,0:T(8,128)S(1)} %get-tuple-element.27), channel_id=1, source_target_pairs={{4,0},{8,4},{12,8},{0,12},{5,1},{9,5},{13,9},{1,13},{6,2},{10,6},{... | collective-permute-start | bytes 442376 | tf_op jit(solution)/shard_map/ppermute | solution.py:25
  11.8 14.6 %collective-permute-start.2 = (f32[48,512]{1,0:T(8,128)S(1)}, f32[48,512]{1,0:T(8,128)S(1)}, u32[]{:S(2)}, u32[]{:S(2)}) collective-permute-start(f32[48,512]{1,0:T(8,128)S(1)} %get-tuple-element.25), channel_id=1, source_target_pairs={{8,0},{12,4},{0,8},{4,12},{9,1},{13,5},{1,9},{5,13},{10,2},{14,6},... | collective-permute-start | bytes 294920 | tf_op jit(solution)/shard_map/ppermute | solution.py:25

commit v4 on v3

--- a/solution.py
+++ b/solution.py
@@ -132,19 +132,26 @@
         copy.wait()
 
 
-def rest_kernel(late, wide, others, cell_blocks, held, prev, listed, lead_parts, send, *refs):
+def second_kernel(middle, wide, others, cell_blocks, held, listed, lead_parts, send, *refs):
     *sends, parts_ref, choose = refs
     size = parts_ref.shape[1] // 2
     lead_size = lead_parts.shape[1] // 2
-    late_size = size - lead_size
-    choose_rows(others + wide, listed, choose)
-    parts_ref[:, late_size:size, :] = lead_parts[:, :lead_size, :]
-    parts_ref[:, size + late_size :, :] = lead_parts[:, lead_size:, :]
+    middle_size = size - lead_size
+    choose_rows(wide + others, listed, choose)
+    parts_ref[:, middle_size:size, :] = lead_parts[:, :lead_size, :]
+    parts_ref[:, size + middle_size :, :] = lead_parts[:, lead_size:, :]
+    summed_parts(middle, cell_blocks, [held.at[f] for f in range(FIELDS)], None, parts_ref, 0, size)
+    width = send.shape[1]
+    take_rows(side_by_side(parts_ref, [(0, middle_size), (size, middle_size)]), choose, [send])
+    take_rows(side_by_side(parts_ref, [(0, 2 * size)]), choose.at[:, width:], sends)
+
+
+def third_kernel(late, wide, others, cell_blocks, held, prev, listed, *refs):
+    *sends, parts_ref, choose = refs
+    size = parts_ref.shape[1] // 2
+    choose_rows(wide + others, listed, choose)
     summed_parts(late, cell_blocks, [held.at[f] for f in range(FIELDS)], prev, parts_ref, 0, size)
     take_rows(side_by_side(parts_ref, [(0, 2 * size)]), choose, sends)
-    narrow_width = choose.shape[1] - send.shape[1]
-    late_parts = side_by_side(parts_ref, [(0, late_size), (size, late_size)])
-    take_rows(late_parts, choose.at[:, narrow_width:], [send])
 
 
 def pointwise(u, v, du, dv, ddu, ddv, feed, total):
@@ -158,23 +165,36 @@
     return outs
 
 
-def local_kernel(groups, cell_blocks, held, prev, feed_ref, kill_ref, tiles, base, split_tiles):
+def local_kernel(
+    chunks, cell_blocks, held, prev, feed_hbm, kill_hbm, tiles_hbm, base_one, base_two, split_tiles, feed_ref, kill_ref, tiles, sems
+):
+    copies = [
+        pltpu.make_async_copy(feed_hbm, feed_ref, sems.at[0]),
+        pltpu.make_async_copy(kill_hbm, kill_ref, sems.at[1]),
+        pltpu.make_async_copy(tiles_hbm, tiles, sems.at[2]),
+    ]
+    for copy in copies:
+        copy.start()
+    for copy in copies[:2]:
+        copy.wait()
     fields = [held.at[f] for f in range(FIELDS)]
     stride = 2 * cell_blocks
     pairs = [(f, s) for f in range(FIELDS) for s in range(2)]
-    for place, group in enumerate(groups):
-        for block in range(cell_blocks):
-            feed = feed_ref[block : block + 1, :]
-            total = feed + kill_ref[block : block + 1, :]
-            now = [steps_at(fields[f], group, block, s, stride) for f, s in pairs]
-            before = [steps_before(fields[f], prev, f, group, block, s, stride) for f, s in pairs]
-            rate_now = pointwise(*now, feed, total)
-            rate_before = pointwise(*before, feed, total)
-            for index in range(2 * FIELDS):
-                row = (place * FIELDS * 2 + index) * STEPS
-                base[block, row : row + STEPS, :] = (now[index] - before[index]) * (1.0 / time_step) - 0.5 * (
-                    rate_now[index] + rate_before[index]
-                )
+    for base, groups in zip((base_one, base_two), chunks):
+        for place, group in enumerate(groups):
+            for block in range(cell_blocks):
+                feed = feed_ref[block : block + 1, :]
+                total = feed + kill_ref[block : block + 1, :]
+                now = [steps_at(fields[f], group, block, s, stride) for f, s in pairs]
+                before = [steps_before(fields[f], prev, f, group, block, s, stride) for f, s in pairs]
+                rate_now = pointwise(*now, feed, total)
+                rate_before = pointwise(*before, feed, total)
+                for index in range(2 * FIELDS):
+                    row = (place * FIELDS * 2 + index) * STEPS
+                    base[block, row : row + STEPS, :] = (now[index] - before[index]) * (1.0 / time_step) - 0.5 * (
+                        rate_now[index] + rate_before[index]
+                    )
+    copies[2].wait()
     blocks, per_row = tiles.shape[:2]
     for block in range(blocks):
         for k in range(per_row):
@@ -183,19 +203,18 @@
             split_tiles[block, k * LANES : (k + 1) * LANES, LANES:] = low
 
 
-def apply_kernel(wide, narrow, cell_blocks, blocks, per_row, *refs):
+def apply_kernel(groups, received, cell_blocks, blocks, per_row, held_back, *refs):
     refs = list(refs)
-    cols, split_tiles, base, parts_ref, wide_lead, wide_late = [refs.pop(0) for _ in range(6)]
-    arrived = [refs.pop(0) for _ in narrow]
+    cols_ref, split_tiles, base, parts_ref = [refs.pop(0) for _ in range(4)]
+    arrived = [refs.pop(0) for _ in received]
+    refs = refs[held_back:]
     outs = [refs.pop(0) for _ in range(FIELDS)]
     extended, made, sems = refs
     stride = 2 * cell_blocks
     size = base.shape[1]
-    late_size = wide_late.shape[0]
+    cols = cols_ref[...]
     extended[:cell_blocks] = parts_ref[...]
-    received = [(wide_late, wide, 0), (wide_lead, wide, late_size)]
-    received += [(ref, slots, 0) for ref, slots in zip(arrived, narrow)]
-    for ref, slots, row in received:
+    for ref, (slots, row) in zip(arrived, received):
         count, width = ref.shape
         per_slot = width // len(slots) // LANES
         for place, slot in enumerate(slots):
@@ -213,7 +232,8 @@
             group, field, species = index // (2 * FIELDS), index // 2 % FIELDS, index % 2
             at = group * STEPS * stride + block * 2 + species
             made[field, pl.ds(at, STEPS, stride=stride), :] = result[index * STEPS : (index + 1) * STEPS, :]
-    copies = [pltpu.make_async_copy(made.at[f], outs[f], sems.at[f]) for f in range(FIELDS)]
+    span = pl.ds(groups[0] * STEPS * stride, len(groups) * STEPS * stride)
+    copies = [pltpu.make_async_copy(made.at[f], outs[f].at[span, :], sems.at[f]) for f in range(FIELDS)]
     for copy in copies:
         copy.start()
     for copy in copies:
@@ -254,7 +274,8 @@
     params = pltpu.CompilerParams(vmem_limit_bytes=16 * 1024 * 1024)
 
     groups = tuple(range(steps // STEPS))
-    late, lead = groups[:1], groups[1:]
+    late, middle, lead = groups[:1], groups[1:-1], groups[-1:]
+    most = middle + lead
     wide, *narrow = slot_groups
     others = [slot for slots in narrow for slot in slots]
 
@@ -264,21 +285,30 @@
     def f32(*shape):
         return jax.ShapeDtypeStruct(shape, F32)
 
-    def bf16(*shape):
-        return jax.ShapeDtypeStruct(shape, BF16)
+    def parts_of(part):
+        return jax.ShapeDtypeStruct((cell_blocks, 2 * rows_of(part), LANES), BF16)
+
+    def sends_of(part, chosen):
+        return [f32(rows_of(part), len(slots) * slot_rows) for slots in chosen]
 
     def cost(flops, moved):
         return pl.CostEstimate(flops=flops, bytes_accessed=moved, transcendentals=0)
 
+    def in_hbm(*arrays):
+        return [pltpu.with_memory_space_constraint(array, pltpu.HBM) for array in arrays]
+
+    def send_to(send, slots):
+        return shift_along(send, "dom", OFFSETS[slots[0]])
+
     hbm = pl.BlockSpec(memory_space=pltpu.HBM)
     size = rows_of(groups)
+    every = len(OFFSETS) * slot_rows
     wide_width = len(wide) * slot_rows
-    in_hbm = [pltpu.with_memory_space_constraint(x, pltpu.HBM) for x in (*fields, rows, counts)]
     send, lead_parts, held, listed, last = pl.pallas_call(
         functools.partial(first_kernel, lead, wide, cell_blocks),
         out_shape=[
             f32(rows_of(lead), wide_width),
-            bf16(cell_blocks, 2 * rows_of(lead), LANES),
+            parts_of(lead),
             f32(FIELDS, steps * stride, LANES),
             jax.ShapeDtypeStruct(rows.shape, jnp.int32),
             f32(FIELDS * stride, LANES),
@@ -294,48 +324,82 @@
         compiler_params=params,
         cost_estimate=cost(4 * rows_of(lead) * cells * wide_width, 8 * size * cells),
         name="gather_first",
-    )(*in_hbm)
-    wide_lead = shift_along(send, "dom", OFFSETS[wide[0]])
+    )(*in_hbm(*fields, rows, counts))
+    wide_lead = send_to(send, wide)
+    send, *sends, most_parts = pl.pallas_call(
+        functools.partial(second_kernel, middle, wide, others, cell_blocks),
+        out_shape=sends_of(middle, [wide]) + sends_of(most, narrow) + [parts_of(most)],
+        in_specs=[vmem] * 3,
+        out_specs=[vmem] * (len(narrow) + 2),
+        scratch_shapes=[VMEM((cells, every), BF16)],
+        compiler_params=params,
+        cost_estimate=cost(4 * rows_of(most) * cells * every, 8 * size * cells),
+        name="gather_second",
+    )(held, listed, lead_parts)
+    wide_middle = send_to(send, wide)
     prev = shift_along(last, "tm", 1)
-    send, *sends, parts = pl.pallas_call(
-        functools.partial(rest_kernel, late, wide, others, cell_blocks),
-        out_shape=[f32(rows_of(late), wide_width)]
-        + [f32(size, len(slots) * slot_rows) for slots in narrow]
-        + [bf16(cell_blocks, 2 * size, LANES)],
-        in_specs=[vmem] * 4,
-        out_specs=[vmem] * (len(narrow) + 2),
-        scratch_shapes=[VMEM((cells, len(OFFSETS) * slot_rows), BF16)],
+    narrow_most = [send_to(part, slots) for part, slots in zip(sends, narrow)]
+    *sends, late_parts = pl.pallas_call(
+        functools.partial(third_kernel, late, wide, others, cell_blocks),
+        out_shape=sends_of(late, slot_groups) + [parts_of(late)],
+        in_specs=[vmem] * 3,
+        out_specs=[vmem] * (len(slot_groups) + 1),
+        scratch_shapes=[VMEM((cells, every), BF16)],
         compiler_params=params,
-        cost_estimate=cost(4 * size * cells * len(OFFSETS) * slot_rows, 8 * size * cells),
-        name="gather_rest",
-    )(held, prev, listed, lead_parts)
-    arrived = [shift_along(part, "dom", OFFSETS[slots[0]]) for part, slots in zip(sends, narrow)]
-    wide_late = shift_along(send, "dom", OFFSETS[wide[0]])
-
-    base, split_tiles = pl.pallas_call(
-        functools.partial(local_kernel, groups, cell_blocks),
-        out_shape=[f32(cell_blocks, size, LANES), bf16(blocks, per_row * LANES, 2 * LANES)],
-        in_specs=[vmem] * 5,
-        out_specs=[vmem] * 2,
+        cost_estimate=cost(4 * rows_of(late) * cells * every, 8 * size * cells),
+        name="gather_third",
+    )(held, prev, listed)
+    arrived_late = [send_to(sends[0], wide)]
+    sends[1], wide_lead = lax.optimization_barrier((sends[1], wide_lead))
+    arrived_late.append(send_to(sends[1], slot_groups[1]))
+    for number in range(2, len(sends)):
+        sends[number], wide_middle = lax.optimization_barrier((sends[number], wide_middle))
+        arrived_late.append(send_to(sends[number], slot_groups[number]))
+
+    base_most, base_late, split_tiles = pl.pallas_call(
+        functools.partial(local_kernel, (most, late), cell_blocks),
+        out_shape=[
+            f32(cell_blocks, rows_of(most), LANES),
+            f32(cell_blocks, rows_of(late), LANES),
+            jax.ShapeDtypeStruct((blocks, per_row * LANES, 2 * LANES), BF16),
+        ],
+        in_specs=[vmem] * 2 + [hbm] * 3,
+        out_specs=[vmem] * 3,
+        scratch_shapes=[
+            VMEM(feed.shape, F32),
+            VMEM(kill.shape, F32),
+            VMEM(tiles.shape, F32),
+            pltpu.SemaphoreType.DMA((3,)),
+        ],
         compiler_params=params,
         cost_estimate=cost(60 * size * cells, 8 * tiles.size),
         name="local_terms",
-    )(held, prev, feed, kill, tiles)
-
-    outs = pl.pallas_call(
-        functools.partial(apply_kernel, wide, narrow, cell_blocks, blocks, per_row),
-        out_shape=[f32(steps * stride, LANES)] * FIELDS,
-        in_specs=[smem] + [vmem] * (5 + len(narrow)),
-        out_specs=[anywhere] * FIELDS,
-        scratch_shapes=[
-            VMEM((cell_blocks + len(OFFSETS) * slot_rows // LANES, 2 * size, LANES), BF16),
-            VMEM((FIELDS, steps * stride, LANES), F32),
-            pltpu.SemaphoreType.DMA((FIELDS,)),
-        ],
-        compiler_params=params,
-        cost_estimate=cost(8 * size * blocks * per_row * LANES * LANES, 16 * size * cells),
-        name="apply_tiles",
-    )(cols, split_tiles, base, parts, wide_lead, wide_late, *arrived)
+    )(held, prev, *in_hbm(feed, kill, tiles))
+
+    def apply(part, base, parts, transfers, outs):
+        inputs = [cols, split_tiles, base, parts, *[array for array, _, _ in transfers]]
+        received = [(slots, row) for _, slots, row in transfers]
+        return pl.pallas_call(
+            functools.partial(apply_kernel, part, received, cell_blocks, blocks, per_row, len(outs)),
+            out_shape=[f32(steps * stride, LANES)] * FIELDS,
+            in_specs=[vmem] * len(inputs) + [anywhere] * len(outs),
+            out_specs=[anywhere] * FIELDS,
+            input_output_aliases={len(inputs) + f: f for f in range(len(outs))},
+            scratch_shapes=[
+                VMEM((cell_blocks + every // LANES, 2 * rows_of(part), LANES), BF16),
+                VMEM((FIELDS, len(part) * STEPS * stride, LANES), F32),
+                pltpu.SemaphoreType.DMA((FIELDS,)),
+            ],
+            compiler_params=params,
+            cost_estimate=cost(8 * rows_of(part) * blocks * per_row * LANES * LANES, 16 * rows_of(part) * cells),
+            name="apply_tiles",
+        )(*inputs, *outs)
+
+    transfers = [(wide_middle, wide, 0), (wide_lead, wide, rows_of(middle))]
+    transfers += [(array, slots, 0) for array, slots in zip(narrow_most, narrow)]
+    outs = apply(most, base_most, most_parts, transfers, [])
+    transfers = [(array, slots, 0) for array, slots in zip(arrived_late, slot_groups)]
+    outs = apply(late, base_late, late_parts, transfers, outs)
     return tuple(unview(out) for out in outs)
 
 

time: 29.2 us -> 28.2 us (0.966)
  waiting for transfers between devices: 12.8 us -> 7.11 us
  starting transfers between devices: 9.41 us -> 12.8 us
  Pallas kernels: 5.79 us -> 7.44 us
    ppermute x5 -> x8, waiting for transfers between devices: 12.8 us -> 7.11 us  [shift_along(): lax.ppermute(block, axis, [((i - distance) % size, i) for i in range(size)])]
    ppermute x5 -> x8, starting transfers between devices: 9.41 us -> 12.8 us  [shift_along(): lax.ppermute(block, axis, [((i - distance) % size, i) for i in range(size)])]
    pallas_call x3 -> x5, Pallas kernels: 3.91 us -> 5.88 us  [the longest x2 2.69 us: apply(): pl.pallas_call(functools.partial(apply_kernel, part, received, cell_block...]
    pallas_call x1, Pallas kernels: 1.88 us -> 1.56 us  [per_device(): pl.pallas_call(functools.partial(first_kernel, lead, wide, cell_blocks),...]
  transfers between devices with their start and end apart: 5 -> 8, of which waited for: 1 -> 2; matrix products, arithmetic and copies ran while one was open for 0% -> 0% of each run, Pallas kernels for 5% -> 17%
where the time goes in v4:
time: 28.2 us; the launch traced here: 28.1 us
  starting transfers between devices  12.8 us (45%)
  Pallas kernels  7.44 us (26%)
  waiting for transfers between devices  7.11 us (25%)
  between operations  0.74 us (3%)
    ppermute x8, starting transfers between devices, shift_along(): lax.ppermute(block, axis, [((i - distance) % size, i) for i in range(size)])  12.8 us
    ppermute x8, waiting for transfers between devices, shift_along(): lax.ppermute(block, axis, [((i - distance) % size, i) for i in range(size)])  7.11 us
    pallas_call x2, Pallas kernels, apply(): pl.pallas_call(functools.partial(apply_kernel, part, received, cell_block...  2.69 us
    pallas_call x1, Pallas kernels, per_device(): pl.pallas_call(functools.partial(local_kernel, (most, late), cell_blocks)...  1.94 us
    pallas_call x1, Pallas kernels, per_device(): pl.pallas_call(functools.partial(first_kernel, lead, wide, cell_blocks),...  1.56 us
    pallas_call x1, Pallas kernels, per_device(): pl.pallas_call(functools.partial(second_kernel, middle, wide, others, cel...  0.68 us
    pallas_call x1, Pallas kernels, per_device(): pl.pallas_call(functools.partial(third_kernel, late, wide, others, cell_b...  0.58 us
  transfers between devices with their start and end apart: 8, of which 2 were waited for; matrix products, arithmetic and copies ran while one was open for 0% of the time, Pallas kernels for 17%

profile of v4, /device:TPU:0, one launch (start us, length us, event | category | flops | bytes accessed | tf_op | source)
XLA Modules:
  0.0 28.1 jit_solution(16960628442959958291)
XLA Ops:
  0.6 1.6 %gather_first.1 = (f32[48,512]{1,0:T(8,128)S(1)}, bf16[8,96,128]{2,1,0:T(8,128)(2,1)S(1)}, f32[3,384,128]{2,1,0:T(8,128)S(1)}, s32[4,256]{1,0:T(4,128)S(1)}, f32[48,128]{1,0:T(8,128)S(1)}) custom-call(f32[384,128]{1,0:T(8,128)} %bitcast.39, f32[384,128]{1,0:T(8,128)} %bitcast.40, f32[384,128]{1,0:T(8,128)} %bitcast.41, s32[4,256]{1,0:T(4,128)} %bitcast.42, ...), custom_call_target="tpu_custom_call" | custom-call | flops 100663296 | bytes 1179648 | tf_op jit(solution)/shard_map/gather_first/pallas_call | solution.py:307
  2.2 4.1 %collective-permute-start.2 = (f32[48,512]{1,0:T(8,128)S(1)}, f32[48,512]{1,0:T(8,128)S(1)}, u32[]{:S(2)}, u32[]{:S(2)}) collective-permute-start(f32[48,512]{1,0:T(8,128)S(1)} %get-tuple-element.37), channel_id=1, source_target_pairs={{8,0},{12,4},{0,8},{4,12},{9,1},{13,5},{1,9},{5,13},{10,2},{14,6},... | collective-permute-start | bytes 294920 | tf_op jit(solution)/shard_map/ppermute | solution.py:25
  6.3 0.7 %gather_second.1 = (f32[48,512]{1,0:T(8,128)S(1)}, f32[96,256]{1,0:T(8,128)S(1)}, f32[96,256]{1,0:T(8,128)S(1)}, bf16[8,192,128]{2,1,0:T(8,128)(2,1)S(1)}) custom-call(f32[3,384,128]{2,1,0:T(8,128)S(1)} %get-tuple-element.29.held, s32[4,256]{1,0:T(4,128)S(1)} %get-tuple-element.33.listed, bf16[8,96,128]{2,1,0:T(8,128)(2,1)S(1)} %get-tuple-element.40.lead_parts), custom_call_target="tpu_custom_call" | custom-call | flops 402653184 | bytes 1179648 | tf_op jit(solution)/shard_map/gather_second/pallas_call | solution.py:329
  7.0 0.0 copy-start
  7.0 0.1 collective-permute-start.4
  7.1 0.1 collective-permute-start
  7.1 1.8 %collective-permute-start.6 = (f32[96,256]{1,0:T(8,128)S(1)}, f32[96,256]{1,0:T(8,128)S(1)}, u32[]{:S(2)}, u32[]{:S(2)}) collective-permute-start(f32[96,256]{1,0:T(8,128)S(1)} %get-tuple-element.47), channel_id=1, source_target_pairs={{12,0},{0,4},{4,8},{8,12},{13,1},{1,5},{5,9},{9,13},{14,2},{2,6},{... | collective-permute-start | bytes 294920 | tf_op jit(solution)/shard_map/ppermute | solution.py:25
  9.0 2.0 %collective-permute-start.7 = (f32[96,256]{1,0:T(8,128)S(1)}, f32[96,256]{1,0:T(8,128)S(1)}, u32[]{:S(2)}, u32[]{:S(2)}) collective-permute-start(f32[96,256]{1,0:T(8,128)S(1)} %get-tuple-element.48), channel_id=1, source_target_pairs={{4,0},{8,4},{12,8},{0,12},{5,1},{9,5},{13,9},{1,13},{6,2},{10,6},{... | collective-permute-start | bytes 294920 | tf_op jit(solution)/shard_map/ppermute | solution.py:25
  11.0 0.0 collective-permute-done.prev
  11.0 0.6 %gather_third.1 = (f32[48,512]{1,0:T(8,128)S(1)}, f32[48,256]{1,0:T(8,128)S(1)}, f32[48,256]{1,0:T(8,128)S(1)}, bf16[8,96,128]{2,1,0:T(8,128)(2,1)S(1)}) custom-call(f32[3,384,128]{2,1,0:T(8,128)S(1)} %get-tuple-element.29.held, f32[48,128]{1,0:T(8,128)S(1)} %collective-permute-done.prev, s32[4,256]{1,0:T(4,128)S(1)} %get-tuple-element.33.listed), custom_call_target="tpu_custom_call" | custom-call | flops 201326592 | bytes 1179648 | tf_op jit(solution)/shard_map/gather_third/pallas_call | solution.py:342
  11.6 2.3 %collective-permute-start.1 = (f32[48,512]{1,0:T(8,128)S(1)}, f32[48,512]{1,0:T(8,128)S(1)}, u32[]{:S(2)}, u32[]{:S(2)}) collective-permute-start(f32[48,512]{1,0:T(8,128)S(1)} %get-tuple-element.35), channel_id=1, source_target_pairs={{8,0},{12,4},{0,8},{4,12},{9,1},{13,5},{1,9},{5,13},{10,2},{14,6},... | collective-permute-start | bytes 294920 | tf_op jit(solution)/shard_map/ppermute | solution.py:25
  13.9 2.4 %collective-permute-done.2.refs_5_ = f32[48,512]{1,0:T(8,128)S(1)} collective-permute-done((f32[48,512]{1,0:T(8,128)S(1)}, f32[48,512]{1,0:T(8,128)S(1)}, u32[]{:S(2)}, u32[]{:S(2)}) %collective-permute-start.2) | collective-permute-done | bytes 98336 | tf_op jit(solution)/shard_map/ppermute | solution.py:25
  16.3 0.0 collective-permute-start.3
  16.3 4.7 %collective-permute-done.4.refs_4_ = f32[48,512]{1,0:T(8,128)S(1)} collective-permute-done((f32[48,512]{1,0:T(8,128)S(1)}, f32[48,512]{1,0:T(8,128)S(1)}, u32[]{:S(2)}, u32[]{:S(2)}) %collective-permute-start.4) | collective-permute-done | bytes 98336 | tf_op jit(solution)/shard_map/ppermute | solution.py:25
  21.0 2.4 %collective-permute-start.5 = (f32[48,256]{1,0:T(8,128)S(1)}, f32[48,256]{1,0:T(8,128)S(1)}, u32[]{:S(2)}, u32[]{:S(2)}) collective-permute-start(f32[48,256]{1,0:T(8,128)S(1)} %get-tuple-element.42), channel_id=1, source_target_pairs={{4,0},{8,4},{12,8},{0,12},{5,1},{9,5},{13,9},{1,13},{6,2},{10,6},{... | collective-permute-start | bytes 147464 | tf_op jit(solution)/shard_map/ppermute | solution.py:25
  23.4 1.9 %local_terms.1 = (f32[8,96,128]{2,1,0:T(8,128)S(1)}, f32[8,48,128]{2,1,0:T(8,128)S(1)}, bf16[8,384,256]{2,1,0:T(8,128)(2,1)S(1)}) custom-call(f32[3,384,128]{2,1,0:T(8,128)S(1)} %get-tuple-element.29.held, f32[48,128]{1,0:T(8,128)S(1)} %collective-permute-done.prev, f32[8,128]{1,0:T(8,128)} %bitcast.43, f32[8,128]{1,0:T(8,128)} %bitcast.44, ...), custom_call_target="tpu_custom_call" | custom-call | flops 8847360 | bytes 3145728 | tf_op jit(solution)/shard_map/local_terms/pallas_call | solution.py:359
  25.3 0.0 collective-permute-done.6.refs_6_
  25.3 0.0 collective-permute-done.7.refs_7_
  25.3 0.0 copy-done
  25.3 1.5 %apply_tiles.2 = (f32[384,128]{1,0:T(8,128)}, f32[384,128]{1,0:T(8,128)}, f32[384,128]{1,0:T(8,128)}) custom-call(s32[3,8]{1,0:T(4,128)S(1)} %bitcast.34, bf16[8,384,256]{2,1,0:T(8,128)(2,1)S(1)} %get-tuple-element.31.refs_1_, f32[8,96,128]{2,1,0:T(8,128)S(1)} %get-tuple-element.43.refs_2_, bf16[8,192,128]{2,1,0:T(8,128)(2,1)S(1)} %get-tuple-element.44.refs_3_, ...), custom_call_target="tpu_custom_call" | custom-call | flops 301989888 | bytes 1572864 | tf_op jit(solution)/shard_map/apply_tiles/pallas_call | solution.py:382
  26.8 0.0 collective-permute-done.1.refs_4_
  26.8 0.0 collective-permute-done.3.refs_5_
  26.8 0.0 collective-permute-done.5.refs_6_
  26.8 1.2 %apply_tiles.3 = (f32[384,128]{1,0:T(8,128)}, f32[384,128]{1,0:T(8,128)}, f32[384,128]{1,0:T(8,128)}) custom-call(s32[3,8]{1,0:T(4,128)S(1)} %bitcast.35, bf16[8,384,256]{2,1,0:T(8,128)(2,1)S(1)} %get-tuple-element.31.refs_1_, f32[8,48,128]{2,1,0:T(8,128)S(1)} %get-tuple-element.32.refs_2_, ...), custom_call_target="tpu_custom_call", output_to_operand_aliasing={{0}: (7, {}), {1}: (8, {}), {2}: (9, {})} | custom-call | flops 150994944 | bytes 786432 | tf_op jit(solution)/shard_map/apply_tiles/pallas_call | solution.py:382
Async XLA Ops:
  2.2 14.1 %collective-permute-start.2 = (f32[48,512]{1,0:T(8,128)S(1)}, f32[48,512]{1,0:T(8,128)S(1)}, u32[]{:S(2)}, u32[]{:S(2)}) collective-permute-start(f32[48,512]{1,0:T(8,128)S(1)} %get-tuple-element.37), channel_id=1, source_target_pairs={{8,0},{12,4},{0,8},{4,12},{9,1},{13,5},{1,9},{5,13},{10,2},{14,6},... | collective-permute-start | bytes 294920 | tf_op jit(solution)/shard_map/ppermute | solution.py:25
  7.0 18.3 %copy-start = (s32[8,3]{0,1:T(4,128)S(1)}, s32[8,3]{0,1:T(4,128)}, u32[]{:S(2)}) copy-start(s32[8,3]{0,1:T(4,128)} %param.15) | copy-start | bytes 292
  7.0 14.0 %collective-permute-start.4 = (f32[48,512]{1,0:T(8,128)S(1)}, f32[48,512]{1,0:T(8,128)S(1)}, u32[]{:S(2)}, u32[]{:S(2)}) collective-permute-start(f32[48,512]{1,0:T(8,128)S(1)} %get-tuple-element.41), channel_id=1, source_target_pairs={{8,0},{12,4},{0,8},{4,12},{9,1},{13,5},{1,9},{5,13},{10,2},{14,6},... | collective-permute-start | bytes 294920 | tf_op jit(solution)/shard_map/ppermute | solution.py:25
  7.1 3.9 %collective-permute-start = (f32[48,128]{1,0:T(8,128)S(1)}, f32[48,128]{1,0:T(8,128)S(1)}, u32[]{:S(2)}, u32[]{:S(2)}) collective-permute-start(f32[48,128]{1,0:T(8,128)S(1)} %get-tuple-element.30), channel_id=1, source_target_pairs={{3,0},{0,1},{1,2},{2,3},{7,4},{4,5},{5,6},{6,7},{11,8},{8,9},{9,10... | collective-permute-start | bytes 73736 | tf_op jit(solution)/shard_map/ppermute | solution.py:25
  7.1 18.2 %collective-permute-start.6 = (f32[96,256]{1,0:T(8,128)S(1)}, f32[96,256]{1,0:T(8,128)S(1)}, u32[]{:S(2)}, u32[]{:S(2)}) collective-permute-start(f32[96,256]{1,0:T(8,128)S(1)} %get-tuple-element.47), channel_id=1, source_target_pairs={{12,0},{0,4},{4,8},{8,12},{13,1},{1,5},{5,9},{9,13},{14,2},{2,6},{... | collective-permute-start | bytes 294920 | tf_op jit(solution)/shard_map/ppermute | solution.py:25
  9.0 16.3 %collective-permute-start.7 = (f32[96,256]{1,0:T(8,128)S(1)}, f32[96,256]{1,0:T(8,128)S(1)}, u32[]{:S(2)}, u32[]{:S(2)}) collective-permute-start(f32[96,256]{1,0:T(8,128)S(1)} %get-tuple-element.48), channel_id=1, source_target_pairs={{4,0},{8,4},{12,8},{0,12},{5,1},{9,5},{13,9},{1,13},{6,2},{10,6},{... | collective-permute-start | bytes 294920 | tf_op jit(solution)/shard_map/ppermute | solution.py:25
  11.6 15.2 %collective-permute-start.1 = (f32[48,512]{1,0:T(8,128)S(1)}, f32[48,512]{1,0:T(8,128)S(1)}, u32[]{:S(2)}, u32[]{:S(2)}) collective-permute-start(f32[48,512]{1,0:T(8,128)S(1)} %get-tuple-element.35), channel_id=1, source_target_pairs={{8,0},{12,4},{0,8},{4,12},{9,1},{13,5},{1,9},{5,13},{10,2},{14,6},... | collective-permute-start | bytes 294920 | tf_op jit(solution)/shard_map/ppermute | solution.py:25
  16.3 10.5 %collective-permute-start.3 = (f32[48,256]{1,0:T(8,128)S(1)}, f32[48,256]{1,0:T(8,128)S(1)}, u32[]{:S(2)}, u32[]{:S(2)}) collective-permute-start(f32[48,256]{1,0:T(8,128)S(1)} %get-tuple-element.38), channel_id=1, source_target_pairs={{12,0},{0,4},{4,8},{8,12},{13,1},{1,5},{5,9},{9,13},{14,2},{2,6},{... | collective-permute-start | bytes 147464 | tf_op jit(solution)/shard_map/ppermute | solution.py:25
  21.0 5.9 %collective-permute-start.5 = (f32[48,256]{1,0:T(8,128)S(1)}, f32[48,256]{1,0:T(8,128)S(1)}, u32[]{:S(2)}, u32[]{:S(2)}) collective-permute-start(f32[48,256]{1,0:T(8,128)S(1)} %get-tuple-element.42), channel_id=1, source_target_pairs={{4,0},{8,4},{12,8},{0,12},{5,1},{9,5},{13,9},{1,13},{6,2},{10,6},{... | collective-permute-start | bytes 147464 | tf_op jit(solution)/shard_map/ppermute | solution.py:25

commit v5 on v4

--- a/solution.py
+++ b/solution.py
@@ -349,13 +349,6 @@
         cost_estimate=cost(4 * rows_of(late) * cells * every, 8 * size * cells),
         name="gather_third",
     )(held, prev, listed)
-    arrived_late = [send_to(sends[0], wide)]
-    sends[1], wide_lead = lax.optimization_barrier((sends[1], wide_lead))
-    arrived_late.append(send_to(sends[1], slot_groups[1]))
-    for number in range(2, len(sends)):
-        sends[number], wide_middle = lax.optimization_barrier((sends[number], wide_middle))
-        arrived_late.append(send_to(sends[number], slot_groups[number]))
-
     base_most, base_late, split_tiles = pl.pallas_call(
         functools.partial(local_kernel, (most, late), cell_blocks),
         out_shape=[
@@ -376,6 +369,13 @@
         name="local_terms",
     )(held, prev, *in_hbm(feed, kill, tiles))
 
+    arrived_late = [send_to(sends[0], wide)]
+    sends[1], wide_lead = lax.optimization_barrier((sends[1], wide_lead))
+    arrived_late.append(send_to(sends[1], slot_groups[1]))
+    for number in range(2, len(sends)):
+        sends[number], wide_middle, split_tiles = lax.optimization_barrier((sends[number], wide_middle, split_tiles))
+        arrived_late.append(send_to(sends[number], slot_groups[number]))
+
     def apply(part, base, parts, transfers, outs):
         inputs = [cols, split_tiles, base, parts, *[array for array, _, _ in transfers]]
         received = [(slots, row) for _, slots, row in transfers]

time: 28.2 us -> 27.1 us (0.961)
  waiting for transfers between devices: 7.11 us -> 4.79 us
  starting transfers between devices: 12.8 us -> 13.9 us
    ppermute x8, waiting for transfers between devices: 7.11 us -> 4.79 us  [shift_along(): lax.ppermute(block, axis, [((i - distance) % size, i) for i in range(size)])]
    ppermute x8, starting transfers between devices: 12.8 us -> 13.9 us  [shift_along(): lax.ppermute(block, axis, [((i - distance) % size, i) for i in range(size)])]
  transfers between devices with their start and end apart: 8 -> 8, of which waited for: 2 -> 4; matrix products, arithmetic and copies ran while one was open for 0% -> 0% of each run, Pallas kernels for 17% -> 17%
where the time goes in v5:
time: 27.1 us; the launch traced here: 26.9 us
  starting transfers between devices  13.9 us (51%)
  Pallas kernels  7.43 us (27%)
  waiting for transfers between devices  4.79 us (18%)
  between operations  0.7 us (3%)
    ppermute x8, starting transfers between devices, shift_along(): lax.ppermute(block, axis, [((i - distance) % size, i) for i in range(size)])  13.9 us
    ppermute x8, waiting for transfers between devices, shift_along(): lax.ppermute(block, axis, [((i - distance) % size, i) for i in range(size)])  4.79 us
    pallas_call x2, Pallas kernels, apply(): pl.pallas_call(functools.partial(apply_kernel, part, received, cell_block...  2.68 us
    pallas_call x1, Pallas kernels, per_device(): pl.pallas_call(functools.partial(local_kernel, (most, late), cell_blocks)...  1.94 us
    pallas_call x1, Pallas kernels, per_device(): pl.pallas_call(functools.partial(first_kernel, lead, wide, cell_blocks),...  1.56 us
    pallas_call x1, Pallas kernels, per_device(): pl.pallas_call(functools.partial(second_kernel, middle, wide, others, cel...  0.68 us
    pallas_call x1, Pallas kernels, per_device(): pl.pallas_call(functools.partial(third_kernel, late, wide, others, cell_b...  0.58 us
  transfers between devices with their start and end apart: 8, of which 4 were waited for; matrix products, arithmetic and copies ran while one was open for 0% of the time, Pallas kernels for 17%

profile of v5, /device:TPU:0, one launch (start us, length us, event | category | flops | bytes accessed | tf_op | source)
XLA Modules:
  0.0 26.9 jit_solution(4313003448010493613)
XLA Ops:
  0.6 1.6 %gather_first.1 = (f32[48,512]{1,0:T(8,128)S(1)}, bf16[8,96,128]{2,1,0:T(8,128)(2,1)S(1)}, f32[3,384,128]{2,1,0:T(8,128)S(1)}, s32[4,256]{1,0:T(4,128)S(1)}, f32[48,128]{1,0:T(8,128)S(1)}) custom-call(f32[384,128]{1,0:T(8,128)} %bitcast.39, f32[384,128]{1,0:T(8,128)} %bitcast.40, f32[384,128]{1,0:T(8,128)} %bitcast.41, s32[4,256]{1,0:T(4,128)} %bitcast.42, ...), custom_call_target="tpu_custom_call" | custom-call | flops 100663296 | bytes 1179648 | tf_op jit(solution)/shard_map/gather_first/pallas_call | solution.py:307
  2.2 4.1 %collective-permute-start.3 = (f32[48,512]{1,0:T(8,128)S(1)}, f32[48,512]{1,0:T(8,128)S(1)}, u32[]{:S(2)}, u32[]{:S(2)}) collective-permute-start(f32[48,512]{1,0:T(8,128)S(1)} %get-tuple-element.42), channel_id=1, source_target_pairs={{8,0},{12,4},{0,8},{4,12},{9,1},{13,5},{1,9},{5,13},{10,2},{14,6},... | collective-permute-start | bytes 294920 | tf_op jit(solution)/shard_map/ppermute | solution.py:25
  6.3 0.7 %gather_second.1 = (f32[48,512]{1,0:T(8,128)S(1)}, f32[96,256]{1,0:T(8,128)S(1)}, f32[96,256]{1,0:T(8,128)S(1)}, bf16[8,192,128]{2,1,0:T(8,128)(2,1)S(1)}) custom-call(f32[3,384,128]{2,1,0:T(8,128)S(1)} %get-tuple-element.30.held, s32[4,256]{1,0:T(4,128)S(1)} %get-tuple-element.32.listed, bf16[8,96,128]{2,1,0:T(8,128)(2,1)S(1)} %get-tuple-element.34.lead_parts), custom_call_target="tpu_custom_call" | custom-call | flops 402653184 | bytes 1179648 | tf_op jit(solution)/shard_map/gather_second/pallas_call | solution.py:329
  7.0 0.0 copy-start
  7.0 0.1 collective-permute-start.1
  7.1 0.1 collective-permute-start
  7.1 1.8 %collective-permute-start.6 = (f32[96,256]{1,0:T(8,128)S(1)}, f32[96,256]{1,0:T(8,128)S(1)}, u32[]{:S(2)}, u32[]{:S(2)}) collective-permute-start(f32[96,256]{1,0:T(8,128)S(1)} %get-tuple-element.49), channel_id=1, source_target_pairs={{12,0},{0,4},{4,8},{8,12},{13,1},{1,5},{5,9},{9,13},{14,2},{2,6},{... | collective-permute-start | bytes 294920 | tf_op jit(solution)/shard_map/ppermute | solution.py:25
  9.0 2.0 %collective-permute-start.7 = (f32[96,256]{1,0:T(8,128)S(1)}, f32[96,256]{1,0:T(8,128)S(1)}, u32[]{:S(2)}, u32[]{:S(2)}) collective-permute-start(f32[96,256]{1,0:T(8,128)S(1)} %get-tuple-element.50), channel_id=1, source_target_pairs={{4,0},{8,4},{12,8},{0,12},{5,1},{9,5},{13,9},{1,13},{6,2},{10,6},{... | collective-permute-start | bytes 294920 | tf_op jit(solution)/shard_map/ppermute | solution.py:25
  11.0 0.0 collective-permute-done.prev
  11.0 0.6 %gather_third.1 = (f32[48,512]{1,0:T(8,128)S(1)}, f32[48,256]{1,0:T(8,128)S(1)}, f32[48,256]{1,0:T(8,128)S(1)}, bf16[8,96,128]{2,1,0:T(8,128)(2,1)S(1)}) custom-call(f32[3,384,128]{2,1,0:T(8,128)S(1)} %get-tuple-element.30.held, f32[48,128]{1,0:T(8,128)S(1)} %collective-permute-done.prev, s32[4,256]{1,0:T(4,128)S(1)} %get-tuple-element.32.listed), custom_call_target="tpu_custom_call" | custom-call | flops 201326592 | bytes 1179648 | tf_op jit(solution)/shard_map/gather_third/pallas_call | solution.py:342
  11.6 2.3 %collective-permute-start.2 = (f32[48,512]{1,0:T(8,128)S(1)}, f32[48,512]{1,0:T(8,128)S(1)}, u32[]{:S(2)}, u32[]{:S(2)}) collective-permute-start(f32[48,512]{1,0:T(8,128)S(1)} %get-tuple-element.40), channel_id=1, source_target_pairs={{8,0},{12,4},{0,8},{4,12},{9,1},{13,5},{1,9},{5,13},{10,2},{14,6},... | collective-permute-start | bytes 294920 | tf_op jit(solution)/shard_map/ppermute | solution.py:25
  13.9 1.9 %local_terms.1 = (f32[8,96,128]{2,1,0:T(8,128)S(1)}, f32[8,48,128]{2,1,0:T(8,128)S(1)}, bf16[8,384,256]{2,1,0:T(8,128)(2,1)S(1)}) custom-call(f32[3,384,128]{2,1,0:T(8,128)S(1)} %get-tuple-element.30.held, f32[48,128]{1,0:T(8,128)S(1)} %collective-permute-done.prev, f32[8,128]{1,0:T(8,128)} %bitcast.43, f32[8,128]{1,0:T(8,128)} %bitcast.44, ...), custom_call_target="tpu_custom_call" | custom-call | flops 8847360 | bytes 3145728 | tf_op jit(solution)/shard_map/local_terms/pallas_call | solution.py:352
  15.8 0.5 %collective-permute-done.3.refs_5_ = f32[48,512]{1,0:T(8,128)S(1)} collective-permute-done((f32[48,512]{1,0:T(8,128)S(1)}, f32[48,512]{1,0:T(8,128)S(1)}, u32[]{:S(2)}, u32[]{:S(2)}) %collective-permute-start.3) | collective-permute-done | bytes 98336 | tf_op jit(solution)/shard_map/ppermute | solution.py:25
  16.3 1.2 %collective-permute-start.4 = (f32[48,256]{1,0:T(8,128)S(1)}, f32[48,256]{1,0:T(8,128)S(1)}, u32[]{:S(2)}, u32[]{:S(2)}) collective-permute-start(f32[48,256]{1,0:T(8,128)S(1)} %get-tuple-element.43), channel_id=1, source_target_pairs={{12,0},{0,4},{4,8},{8,12},{13,1},{1,5},{5,9},{9,13},{14,2},{2,6},{... | collective-permute-start | bytes 147464 | tf_op jit(solution)/shard_map/ppermute | solution.py:25
  17.5 3.5 %collective-permute-done.1.refs_4_ = f32[48,512]{1,0:T(8,128)S(1)} collective-permute-done((f32[48,512]{1,0:T(8,128)S(1)}, f32[48,512]{1,0:T(8,128)S(1)}, u32[]{:S(2)}, u32[]{:S(2)}) %collective-permute-start.1) | collective-permute-done | bytes 98336 | tf_op jit(solution)/shard_map/ppermute | solution.py:25
  21.0 2.4 %collective-permute-start.5 = (f32[48,256]{1,0:T(8,128)S(1)}, f32[48,256]{1,0:T(8,128)S(1)}, u32[]{:S(2)}, u32[]{:S(2)}) collective-permute-start(f32[48,256]{1,0:T(8,128)S(1)} %get-tuple-element.44), channel_id=1, source_target_pairs={{4,0},{8,4},{12,8},{0,12},{5,1},{9,5},{13,9},{1,13},{6,2},{10,6},{... | collective-permute-start | bytes 147464 | tf_op jit(solution)/shard_map/ppermute | solution.py:25
  23.4 0.0 collective-permute-done.6.refs_6_
  23.4 0.0 collective-permute-done.7.refs_7_
  23.4 0.0 copy-done
  23.4 1.5 %apply_tiles.2 = (f32[384,128]{1,0:T(8,128)}, f32[384,128]{1,0:T(8,128)}, f32[384,128]{1,0:T(8,128)}) custom-call(s32[3,8]{1,0:T(4,128)S(1)} %bitcast.34, bf16[8,384,256]{2,1,0:T(8,128)(2,1)S(1)} %get-tuple-element.37.refs_1_, f32[8,96,128]{2,1,0:T(8,128)S(1)} %get-tuple-element.45.refs_2_, bf16[8,192,128]{2,1,0:T(8,128)(2,1)S(1)} %get-tuple-element.46.refs_3_, ...), custom_call_target="tpu_custom_call" | custom-call | flops 301989888 | bytes 1572864 | tf_op jit(solution)/shard_map/apply_tiles/pallas_call | solution.py:382
  24.8 0.6 %collective-permute-done.2.refs_4_ = f32[48,512]{1,0:T(8,128)S(1)} collective-permute-done((f32[48,512]{1,0:T(8,128)S(1)}, f32[48,512]{1,0:T(8,128)S(1)}, u32[]{:S(2)}, u32[]{:S(2)}) %collective-permute-start.2) | collective-permute-done | bytes 98336 | tf_op jit(solution)/shard_map/ppermute | solution.py:25
  25.5 0.0 collective-permute-done.4.refs_5_
  25.5 0.2 collective-permute-done.5.refs_6_
  25.7 1.2 %apply_tiles.3 = (f32[384,128]{1,0:T(8,128)}, f32[384,128]{1,0:T(8,128)}, f32[384,128]{1,0:T(8,128)}) custom-call(s32[3,8]{1,0:T(4,128)S(1)} %bitcast.35, bf16[8,384,256]{2,1,0:T(8,128)(2,1)S(1)} %get-tuple-element.37.refs_1_, f32[8,48,128]{2,1,0:T(8,128)S(1)} %get-tuple-element.38.refs_2_, ...), custom_call_target="tpu_custom_call", output_to_operand_aliasing={{0}: (7, {}), {1}: (8, {}), {2}: (9, {})} | custom-call | flops 150994944 | bytes 786432 | tf_op jit(solution)/shard_map/apply_tiles/pallas_call | solution.py:382
Async XLA Ops:
  2.2 14.1 %collective-permute-start.3 = (f32[48,512]{1,0:T(8,128)S(1)}, f32[48,512]{1,0:T(8,128)S(1)}, u32[]{:S(2)}, u32[]{:S(2)}) collective-permute-start(f32[48,512]{1,0:T(8,128)S(1)} %get-tuple-element.42), channel_id=1, source_target_pairs={{8,0},{12,4},{0,8},{4,12},{9,1},{13,5},{1,9},{5,13},{10,2},{14,6},... | collective-permute-start | bytes 294920 | tf_op jit(solution)/shard_map/ppermute | solution.py:25
  7.0 16.4 %copy-start = (s32[8,3]{0,1:T(4,128)S(1)}, s32[8,3]{0,1:T(4,128)}, u32[]{:S(2)}) copy-start(s32[8,3]{0,1:T(4,128)} %param.15) | copy-start | bytes 292
  7.0 14.0 %collective-permute-start.1 = (f32[48,512]{1,0:T(8,128)S(1)}, f32[48,512]{1,0:T(8,128)S(1)}, u32[]{:S(2)}, u32[]{:S(2)}) collective-permute-start(f32[48,512]{1,0:T(8,128)S(1)} %get-tuple-element.35), channel_id=1, source_target_pairs={{8,0},{12,4},{0,8},{4,12},{9,1},{13,5},{1,9},{5,13},{10,2},{14,6},... | collective-permute-start | bytes 294920 | tf_op jit(solution)/shard_map/ppermute | solution.py:25
  7.1 3.9 %collective-permute-start = (f32[48,128]{1,0:T(8,128)S(1)}, f32[48,128]{1,0:T(8,128)S(1)}, u32[]{:S(2)}, u32[]{:S(2)}) collective-permute-start(f32[48,128]{1,0:T(8,128)S(1)} %get-tuple-element.31), channel_id=1, source_target_pairs={{3,0},{0,1},{1,2},{2,3},{7,4},{4,5},{5,6},{6,7},{11,8},{8,9},{9,10... | collective-permute-start | bytes 73736 | tf_op jit(solution)/shard_map/ppermute | solution.py:25
  7.1 16.2 %collective-permute-start.6 = (f32[96,256]{1,0:T(8,128)S(1)}, f32[96,256]{1,0:T(8,128)S(1)}, u32[]{:S(2)}, u32[]{:S(2)}) collective-permute-start(f32[96,256]{1,0:T(8,128)S(1)} %get-tuple-element.49), channel_id=1, source_target_pairs={{12,0},{0,4},{4,8},{8,12},{13,1},{1,5},{5,9},{9,13},{14,2},{2,6},{... | collective-permute-start | bytes 294920 | tf_op jit(solution)/shard_map/ppermute | solution.py:25
  9.0 14.4 %collective-permute-start.7 = (f32[96,256]{1,0:T(8,128)S(1)}, f32[96,256]{1,0:T(8,128)S(1)}, u32[]{:S(2)}, u32[]{:S(2)}) collective-permute-start(f32[96,256]{1,0:T(8,128)S(1)} %get-tuple-element.50), channel_id=1, source_target_pairs={{4,0},{8,4},{12,8},{0,12},{5,1},{9,5},{13,9},{1,13},{6,2},{10,6},{... | collective-permute-start | bytes 294920 | tf_op jit(solution)/shard_map/ppermute | solution.py:25
  11.6 13.8 %collective-permute-start.2 = (f32[48,512]{1,0:T(8,128)S(1)}, f32[48,512]{1,0:T(8,128)S(1)}, u32[]{:S(2)}, u32[]{:S(2)}) collective-permute-start(f32[48,512]{1,0:T(8,128)S(1)} %get-tuple-element.40), channel_id=1, source_target_pairs={{8,0},{12,4},{0,8},{4,12},{9,1},{13,5},{1,9},{5,13},{10,2},{14,6},... | collective-permute-start | bytes 294920 | tf_op jit(solution)/shard_map/ppermute | solution.py:25
  16.3 9.2 %collective-permute-start.4 = (f32[48,256]{1,0:T(8,128)S(1)}, f32[48,256]{1,0:T(8,128)S(1)}, u32[]{:S(2)}, u32[]{:S(2)}) collective-permute-start(f32[48,256]{1,0:T(8,128)S(1)} %get-tuple-element.43), channel_id=1, source_target_pairs={{12,0},{0,4},{4,8},{8,12},{13,1},{1,5},{5,9},{9,13},{14,2},{2,6},{... | collective-permute-start | bytes 147464 | tf_op jit(solution)/shard_map/ppermute | solution.py:25
  21.0 4.7 %collective-permute-start.5 = (f32[48,256]{1,0:T(8,128)S(1)}, f32[48,256]{1,0:T(8,128)S(1)}, u32[]{:S(2)}, u32[]{:S(2)}) collective-permute-start(f32[48,256]{1,0:T(8,128)S(1)} %get-tuple-element.44), channel_id=1, source_target_pairs={{4,0},{8,4},{12,8},{0,12},{5,1},{9,5},{13,9},{1,13},{6,2},{10,6},{... | collective-permute-start | bytes 147464 | tf_op jit(solution)/shard_map/ppermute | solution.py:25

commit v6 on v5

--- a/solution.py
+++ b/solution.py
@@ -45,17 +45,19 @@
     return high, (values - high.astype(F32)).astype(BF16)
 
 
+def scaled_sum(ref, prev_ref, field, group, cell_block, species, stride):
+    now = steps_at(ref, group, cell_block, species, stride)
+    before = steps_before(ref, prev_ref, field, group, cell_block, species, stride)
+    return (now + before) * (-0.5 * (spread_u, spread_v)[species])
+
+
 def summed_parts(groups, cell_blocks, fields, prev, parts_ref, high_row, low_row):
     stride = 2 * cell_blocks
     for place, group in enumerate(groups):
         for field in range(FIELDS):
             row = (place * FIELDS + field) * 2 * STEPS
             for block in range(cell_blocks):
-                both = []
-                for species, scale in enumerate((-0.5 * spread_u, -0.5 * spread_v)):
-                    now = steps_at(fields[field], group, block, species, stride)
-                    before = steps_before(fields[field], prev, field, group, block, species, stride)
-                    both.append((now + before) * scale)
+                both = [scaled_sum(fields[field], prev, field, group, block, species, stride) for species in range(2)]
                 high, low = split(jnp.concatenate(both, axis=0))
                 parts_ref[block, high_row + row : high_row + row + 2 * STEPS, :] = high
                 parts_ref[block, low_row + row : low_row + row + 2 * STEPS, :] = low
@@ -95,7 +97,7 @@
 def first_kernel(lead, slots, cell_blocks, *refs):
     refs = list(refs)
     sources = [refs.pop(0) for _ in range(FIELDS)]
-    rows_hbm, count_hbm, send, parts_ref, held, listed, last, choose, rows_ref, count_ref, sems = refs
+    rows_hbm, count_hbm, send, held, listed, last, rows_ref, count_ref, sems = refs
     stride = 2 * cell_blocks
     early = (lead[0] * STEPS - 1) * stride
     late = held.shape[1] - early
@@ -120,27 +122,40 @@
         listed[slot : slot + 1, :] = jnp.where(
             lane[slot : slot + 1] < count_ref[:, slot : slot + 1], rows_ref[slot : slot + 1, :], -1
         )
-    choose_rows(slots, listed, choose)
     for copy in needed:
         copy.wait()
-    size = parts_ref.shape[1] // 2
-    summed_parts(lead, cell_blocks, [held.at[f] for f in range(FIELDS)], None, parts_ref, 0, size)
-    take_rows(side_by_side(parts_ref, [(0, 2 * size)]), choose, [send])
+    columns = [
+        listed[slot : slot + 1, start : start + LANES]
+        for slot in slots
+        for start in range(0, listed.shape[1], LANES)
+    ]
+    columns = [jnp.broadcast_to(column, (STEPS, LANES)) for column in columns]
+    for place, group in enumerate(lead):
+        for field in range(FIELDS):
+            for species in range(2):
+                row = ((place * FIELDS + field) * 2 + species) * STEPS
+                sums = [
+                    scaled_sum(held.at[field], None, field, group, block, species, stride) for block in range(cell_blocks)
+                ]
+                for number, column in enumerate(columns):
+                    lanes = column & (LANES - 1)
+                    found = jnp.zeros((STEPS, LANES), F32)
+                    for block in range(cell_blocks):
+                        taken = jnp.take_along_axis(sums[block], lanes, axis=1, mode="promise_in_bounds")
+                        found = jnp.where(column >> 7 == block, taken, found)
+                    send[row : row + STEPS, number * LANES : (number + 1) * LANES] = found
     for field in range(FIELDS):
         last[field * stride : (field + 1) * stride, :] = held[field, -stride:, :]
     for copy in others:
         copy.wait()
 
 
-def second_kernel(middle, wide, others, cell_blocks, held, listed, lead_parts, send, *refs):
+def second_kernel(most, middle, wide, others, cell_blocks, held, listed, send, *refs):
     *sends, parts_ref, choose = refs
     size = parts_ref.shape[1] // 2
-    lead_size = lead_parts.shape[1] // 2
-    middle_size = size - lead_size
+    middle_size = size * len(middle) // len(most)
     choose_rows(wide + others, listed, choose)
-    parts_ref[:, middle_size:size, :] = lead_parts[:, :lead_size, :]
-    parts_ref[:, size + middle_size :, :] = lead_parts[:, lead_size:, :]
-    summed_parts(middle, cell_blocks, [held.at[f] for f in range(FIELDS)], None, parts_ref, 0, size)
+    summed_parts(most, cell_blocks, [held.at[f] for f in range(FIELDS)], None, parts_ref, 0, size)
     width = send.shape[1]
     take_rows(side_by_side(parts_ref, [(0, middle_size), (size, middle_size)]), choose, [send])
     take_rows(side_by_side(parts_ref, [(0, 2 * size)]), choose.at[:, width:], sends)
@@ -304,19 +319,17 @@
     size = rows_of(groups)
     every = len(OFFSETS) * slot_rows
     wide_width = len(wide) * slot_rows
-    send, lead_parts, held, listed, last = pl.pallas_call(
+    send, held, listed, last = pl.pallas_call(
         functools.partial(first_kernel, lead, wide, cell_blocks),
         out_shape=[
             f32(rows_of(lead), wide_width),
-            parts_of(lead),
             f32(FIELDS, steps * stride, LANES),
             jax.ShapeDtypeStruct(rows.shape, jnp.int32),
             f32(FIELDS * stride, LANES),
         ],
         in_specs=[hbm] * (FIELDS + 2),
-        out_specs=[vmem] * 5,
+        out_specs=[vmem] * 4,
         scratch_shapes=[
-            VMEM((cells, wide_width), BF16),
             VMEM(rows.shape, jnp.int32),
             VMEM(counts.shape, jnp.int32),
             pltpu.SemaphoreType.DMA((2 * FIELDS + 2,)),
@@ -327,15 +340,15 @@
     )(*in_hbm(*fields, rows, counts))
     wide_lead = send_to(send, wide)
     send, *sends, most_parts = pl.pallas_call(
-        functools.partial(second_kernel, middle, wide, others, cell_blocks),
+        functools.partial(second_kernel, most, middle, wide, others, cell_blocks),
         out_shape=sends_of(middle, [wide]) + sends_of(most, narrow) + [parts_of(most)],
-        in_specs=[vmem] * 3,
+        in_specs=[vmem] * 2,
         out_specs=[vmem] * (len(narrow) + 2),
         scratch_shapes=[VMEM((cells, every), BF16)],
         compiler_params=params,
         cost_estimate=cost(4 * rows_of(most) * cells * every, 8 * size * cells),
         name="gather_second",
-    )(held, listed, lead_parts)
+    )(held, listed)
     wide_middle = send_to(send, wide)
     prev = shift_along(last, "tm", 1)
     narrow_most = [send_to(part, slots) for part, slots in zip(sends, narrow)]

time: 27.1 us -> 26.9 us (level)
    ppermute x8, waiting for transfers between devices: 4.79 us -> 4.52 us  [shift_along(): lax.ppermute(block, axis, [((i - distance) % size, i) for i in range(size)])]
  transfers between devices with their start and end apart: 8 -> 8, of which waited for: 4 -> 4; matrix products, arithmetic and copies ran while one was open for 0% -> 0% of each run, Pallas kernels for 17% -> 18%
where the time goes in v6:
time: 26.9 us; the launch traced here: 26.8 us
  starting transfers between devices  14.1 us (52%)
  Pallas kernels  7.45 us (28%)
  waiting for transfers between devices  4.52 us (17%)
  between operations  0.7 us (3%)
    ppermute x8, starting transfers between devices, shift_along(): lax.ppermute(block, axis, [((i - distance) % size, i) for i in range(size)])  14.1 us
    ppermute x8, waiting for transfers between devices, shift_along(): lax.ppermute(block, axis, [((i - distance) % size, i) for i in range(size)])  4.52 us
    pallas_call x2, Pallas kernels, apply(): pl.pallas_call(functools.partial(apply_kernel, part, received, cell_block...  2.68 us
    pallas_call x1, Pallas kernels, per_device(): pl.pallas_call(functools.partial(local_kernel, (most, late), cell_blocks)...  1.94 us
    pallas_call x1, Pallas kernels, per_device(): pl.pallas_call(functools.partial(first_kernel, lead, wide, cell_blocks),...  1.44 us
    pallas_call x1, Pallas kernels, per_device(): pl.pallas_call(functools.partial(second_kernel, most, middle, wide, other...  0.81 us
    pallas_call x1, Pallas kernels, per_device(): pl.pallas_call(functools.partial(third_kernel, late, wide, others, cell_b...  0.57 us
  transfers between devices with their start and end apart: 8, of which 4 were waited for; matrix products, arithmetic and copies ran while one was open for 0% of the time, Pallas kernels for 18%

profile of v6, /device:TPU:0, one launch (start us, length us, event | category | flops | bytes accessed | tf_op | source)
XLA Modules:
  0.0 26.8 jit_solution(2696319829685180019)
XLA Ops:
  0.6 1.4 %gather_first.1 = (f32[48,512]{1,0:T(8,128)S(1)}, f32[3,384,128]{2,1,0:T(8,128)S(1)}, s32[4,256]{1,0:T(4,128)S(1)}, f32[48,128]{1,0:T(8,128)S(1)}) custom-call(f32[384,128]{1,0:T(8,128)} %bitcast.39, f32[384,128]{1,0:T(8,128)} %bitcast.40, f32[384,128]{1,0:T(8,128)} %bitcast.41, s32[4,256]{1,0:T(4,128)} %bitcast.42, s32[1,4]{1,0:T(1,128)} %refs_4_.1), custom_call_target="tpu_custom_call" | custom-call | flops 100663296 | bytes 1179648 | tf_op jit(solution)/shard_map/gather_first/pallas_call | solution.py:322
  2.1 4.1 %collective-permute-start.3 = (f32[48,512]{1,0:T(8,128)S(1)}, f32[48,512]{1,0:T(8,128)S(1)}, u32[]{:S(2)}, u32[]{:S(2)}) collective-permute-start(f32[48,512]{1,0:T(8,128)S(1)} %get-tuple-element.40), channel_id=1, source_target_pairs={{8,0},{12,4},{0,8},{4,12},{9,1},{13,5},{1,9},{5,13},{10,2},{14,6},... | collective-permute-start | bytes 294920 | tf_op jit(solution)/shard_map/ppermute | solution.py:25
  6.2 0.8 %gather_second.1 = (f32[48,512]{1,0:T(8,128)S(1)}, f32[96,256]{1,0:T(8,128)S(1)}, f32[96,256]{1,0:T(8,128)S(1)}, bf16[8,192,128]{2,1,0:T(8,128)(2,1)S(1)}) custom-call(f32[3,384,128]{2,1,0:T(8,128)S(1)} %get-tuple-element.29.held, s32[4,256]{1,0:T(4,128)S(1)} %get-tuple-element.31.listed), custom_call_target="tpu_custom_call" | custom-call | flops 402653184 | bytes 1179648 | tf_op jit(solution)/shard_map/gather_second/pallas_call | solution.py:342
  7.0 0.0 copy-start
  7.0 0.1 collective-permute-start.1
  7.1 0.1 collective-permute-start
  7.2 1.8 %collective-permute-start.6 = (f32[96,256]{1,0:T(8,128)S(1)}, f32[96,256]{1,0:T(8,128)S(1)}, u32[]{:S(2)}, u32[]{:S(2)}) collective-permute-start(f32[96,256]{1,0:T(8,128)S(1)} %get-tuple-element.47), channel_id=1, source_target_pairs={{12,0},{0,4},{4,8},{8,12},{13,1},{1,5},{5,9},{9,13},{14,2},{2,6},{... | collective-permute-start | bytes 294920 | tf_op jit(solution)/shard_map/ppermute | solution.py:25
  9.0 2.0 %collective-permute-start.7 = (f32[96,256]{1,0:T(8,128)S(1)}, f32[96,256]{1,0:T(8,128)S(1)}, u32[]{:S(2)}, u32[]{:S(2)}) collective-permute-start(f32[96,256]{1,0:T(8,128)S(1)} %get-tuple-element.48), channel_id=1, source_target_pairs={{4,0},{8,4},{12,8},{0,12},{5,1},{9,5},{13,9},{1,13},{6,2},{10,6},{... | collective-permute-start | bytes 294920 | tf_op jit(solution)/shard_map/ppermute | solution.py:25
  11.0 0.0 collective-permute-done.prev
  11.0 0.6 %gather_third.1 = (f32[48,512]{1,0:T(8,128)S(1)}, f32[48,256]{1,0:T(8,128)S(1)}, f32[48,256]{1,0:T(8,128)S(1)}, bf16[8,96,128]{2,1,0:T(8,128)(2,1)S(1)}) custom-call(f32[3,384,128]{2,1,0:T(8,128)S(1)} %get-tuple-element.29.held, f32[48,128]{1,0:T(8,128)S(1)} %collective-permute-done.prev, s32[4,256]{1,0:T(4,128)S(1)} %get-tuple-element.31.listed), custom_call_target="tpu_custom_call" | custom-call | flops 201326592 | bytes 1179648 | tf_op jit(solution)/shard_map/gather_third/pallas_call | solution.py:355
  11.6 2.3 %collective-permute-start.2 = (f32[48,512]{1,0:T(8,128)S(1)}, f32[48,512]{1,0:T(8,128)S(1)}, u32[]{:S(2)}, u32[]{:S(2)}) collective-permute-start(f32[48,512]{1,0:T(8,128)S(1)} %get-tuple-element.38), channel_id=1, source_target_pairs={{8,0},{12,4},{0,8},{4,12},{9,1},{13,5},{1,9},{5,13},{10,2},{14,6},... | collective-permute-start | bytes 294920 | tf_op jit(solution)/shard_map/ppermute | solution.py:25
  13.9 1.9 %local_terms.1 = (f32[8,96,128]{2,1,0:T(8,128)S(1)}, f32[8,48,128]{2,1,0:T(8,128)S(1)}, bf16[8,384,256]{2,1,0:T(8,128)(2,1)S(1)}) custom-call(f32[3,384,128]{2,1,0:T(8,128)S(1)} %get-tuple-element.29.held, f32[48,128]{1,0:T(8,128)S(1)} %collective-permute-done.prev, f32[8,128]{1,0:T(8,128)} %bitcast.43, f32[8,128]{1,0:T(8,128)} %bitcast.44, ...), custom_call_target="tpu_custom_call" | custom-call | flops 8847360 | bytes 3145728 | tf_op jit(solution)/shard_map/local_terms/pallas_call | solution.py:365
  15.9 0.3 %collective-permute-done.3.refs_5_ = f32[48,512]{1,0:T(8,128)S(1)} collective-permute-done((f32[48,512]{1,0:T(8,128)S(1)}, f32[48,512]{1,0:T(8,128)S(1)}, u32[]{:S(2)}, u32[]{:S(2)}) %collective-permute-start.3) | collective-permute-done | bytes 98336 | tf_op jit(solution)/shard_map/ppermute | solution.py:25
  16.2 1.3 %collective-permute-start.4 = (f32[48,256]{1,0:T(8,128)S(1)}, f32[48,256]{1,0:T(8,128)S(1)}, u32[]{:S(2)}, u32[]{:S(2)}) collective-permute-start(f32[48,256]{1,0:T(8,128)S(1)} %get-tuple-element.41), channel_id=1, source_target_pairs={{12,0},{0,4},{4,8},{8,12},{13,1},{1,5},{5,9},{9,13},{14,2},{2,6},{... | collective-permute-start | bytes 147464 | tf_op jit(solution)/shard_map/ppermute | solution.py:25
  17.5 3.4 %collective-permute-done.1.refs_4_ = f32[48,512]{1,0:T(8,128)S(1)} collective-permute-done((f32[48,512]{1,0:T(8,128)S(1)}, f32[48,512]{1,0:T(8,128)S(1)}, u32[]{:S(2)}, u32[]{:S(2)}) %collective-permute-start.1) | collective-permute-done | bytes 98336 | tf_op jit(solution)/shard_map/ppermute | solution.py:25
  20.9 2.4 %collective-permute-start.5 = (f32[48,256]{1,0:T(8,128)S(1)}, f32[48,256]{1,0:T(8,128)S(1)}, u32[]{:S(2)}, u32[]{:S(2)}) collective-permute-start(f32[48,256]{1,0:T(8,128)S(1)} %get-tuple-element.42), channel_id=1, source_target_pairs={{4,0},{8,4},{12,8},{0,12},{5,1},{9,5},{13,9},{1,13},{6,2},{10,6},{... | collective-permute-start | bytes 147464 | tf_op jit(solution)/shard_map/ppermute | solution.py:25
  23.2 0.0 collective-permute-done.6.refs_6_
  23.2 0.0 collective-permute-done.7.refs_7_
  23.2 0.0 copy-done
  23.2 1.5 %apply_tiles.2 = (f32[384,128]{1,0:T(8,128)}, f32[384,128]{1,0:T(8,128)}, f32[384,128]{1,0:T(8,128)}) custom-call(s32[3,8]{1,0:T(4,128)S(1)} %bitcast.34, bf16[8,384,256]{2,1,0:T(8,128)(2,1)S(1)} %get-tuple-element.35.refs_1_, f32[8,96,128]{2,1,0:T(8,128)S(1)} %get-tuple-element.43.refs_2_, bf16[8,192,128]{2,1,0:T(8,128)(2,1)S(1)} %get-tuple-element.44.refs_3_, ...), custom_call_target="tpu_custom_call" | custom-call | flops 301989888 | bytes 1572864 | tf_op jit(solution)/shard_map/apply_tiles/pallas_call | solution.py:395
  24.7 0.6 %collective-permute-done.2.refs_4_ = f32[48,512]{1,0:T(8,128)S(1)} collective-permute-done((f32[48,512]{1,0:T(8,128)S(1)}, f32[48,512]{1,0:T(8,128)S(1)}, u32[]{:S(2)}, u32[]{:S(2)}) %collective-permute-start.2) | collective-permute-done | bytes 98336 | tf_op jit(solution)/shard_map/ppermute | solution.py:25
  25.3 0.0 collective-permute-done.4.refs_5_
  25.3 0.2 collective-permute-done.5.refs_6_
  25.5 1.2 %apply_tiles.3 = (f32[384,128]{1,0:T(8,128)}, f32[384,128]{1,0:T(8,128)}, f32[384,128]{1,0:T(8,128)}) custom-call(s32[3,8]{1,0:T(4,128)S(1)} %bitcast.35, bf16[8,384,256]{2,1,0:T(8,128)(2,1)S(1)} %get-tuple-element.35.refs_1_, f32[8,48,128]{2,1,0:T(8,128)S(1)} %get-tuple-element.36.refs_2_, ...), custom_call_target="tpu_custom_call", output_to_operand_aliasing={{0}: (7, {}), {1}: (8, {}), {2}: (9, {})} | custom-call | flops 150994944 | bytes 786432 | tf_op jit(solution)/shard_map/apply_tiles/pallas_call | solution.py:395
Async XLA Ops:
  2.1 14.1 %collective-permute-start.3 = (f32[48,512]{1,0:T(8,128)S(1)}, f32[48,512]{1,0:T(8,128)S(1)}, u32[]{:S(2)}, u32[]{:S(2)}) collective-permute-start(f32[48,512]{1,0:T(8,128)S(1)} %get-tuple-element.40), channel_id=1, source_target_pairs={{8,0},{12,4},{0,8},{4,12},{9,1},{13,5},{1,9},{5,13},{10,2},{14,6},... | collective-permute-start | bytes 294920 | tf_op jit(solution)/shard_map/ppermute | solution.py:25
  7.0 16.2 %copy-start = (s32[8,3]{0,1:T(4,128)S(1)}, s32[8,3]{0,1:T(4,128)}, u32[]{:S(2)}) copy-start(s32[8,3]{0,1:T(4,128)} %param.15) | copy-start | bytes 292
  7.0 13.9 %collective-permute-start.1 = (f32[48,512]{1,0:T(8,128)S(1)}, f32[48,512]{1,0:T(8,128)S(1)}, u32[]{:S(2)}, u32[]{:S(2)}) collective-permute-start(f32[48,512]{1,0:T(8,128)S(1)} %get-tuple-element.33), channel_id=1, source_target_pairs={{8,0},{12,4},{0,8},{4,12},{9,1},{13,5},{1,9},{5,13},{10,2},{14,6},... | collective-permute-start | bytes 294920 | tf_op jit(solution)/shard_map/ppermute | solution.py:25
  7.1 3.9 %collective-permute-start = (f32[48,128]{1,0:T(8,128)S(1)}, f32[48,128]{1,0:T(8,128)S(1)}, u32[]{:S(2)}, u32[]{:S(2)}) collective-permute-start(f32[48,128]{1,0:T(8,128)S(1)} %get-tuple-element.30), channel_id=1, source_target_pairs={{3,0},{0,1},{1,2},{2,3},{7,4},{4,5},{5,6},{6,7},{11,8},{8,9},{9,10... | collective-permute-start | bytes 73736 | tf_op jit(solution)/shard_map/ppermute | solution.py:25
  7.2 16.1 %collective-permute-start.6 = (f32[96,256]{1,0:T(8,128)S(1)}, f32[96,256]{1,0:T(8,128)S(1)}, u32[]{:S(2)}, u32[]{:S(2)}) collective-permute-start(f32[96,256]{1,0:T(8,128)S(1)} %get-tuple-element.47), channel_id=1, source_target_pairs={{12,0},{0,4},{4,8},{8,12},{13,1},{1,5},{5,9},{9,13},{14,2},{2,6},{... | collective-permute-start | bytes 294920 | tf_op jit(solution)/shard_map/ppermute | solution.py:25
  9.0 14.2 %collective-permute-start.7 = (f32[96,256]{1,0:T(8,128)S(1)}, f32[96,256]{1,0:T(8,128)S(1)}, u32[]{:S(2)}, u32[]{:S(2)}) collective-permute-start(f32[96,256]{1,0:T(8,128)S(1)} %get-tuple-element.48), channel_id=1, source_target_pairs={{4,0},{8,4},{12,8},{0,12},{5,1},{9,5},{13,9},{1,13},{6,2},{10,6},{... | collective-permute-start | bytes 294920 | tf_op jit(solution)/shard_map/ppermute | solution.py:25
  11.6 13.7 %collective-permute-start.2 = (f32[48,512]{1,0:T(8,128)S(1)}, f32[48,512]{1,0:T(8,128)S(1)}, u32[]{:S(2)}, u32[]{:S(2)}) collective-permute-start(f32[48,512]{1,0:T(8,128)S(1)} %get-tuple-element.38), channel_id=1, source_target_pairs={{8,0},{12,4},{0,8},{4,12},{9,1},{13,5},{1,9},{5,13},{10,2},{14,6},... | collective-permute-start | bytes 294920 | tf_op jit(solution)/shard_map/ppermute | solution.py:25
  16.2 9.2 %collective-permute-start.4 = (f32[48,256]{1,0:T(8,128)S(1)}, f32[48,256]{1,0:T(8,128)S(1)}, u32[]{:S(2)}, u32[]{:S(2)}) collective-permute-start(f32[48,256]{1,0:T(8,128)S(1)} %get-tuple-element.41), channel_id=1, source_target_pairs={{12,0},{0,4},{4,8},{8,12},{13,1},{1,5},{5,9},{9,13},{14,2},{2,6},{... | collective-permute-start | bytes 147464 | tf_op jit(solution)/shard_map/ppermute | solution.py:25
  20.9 4.7 %collective-permute-start.5 = (f32[48,256]{1,0:T(8,128)S(1)}, f32[48,256]{1,0:T(8,128)S(1)}, u32[]{:S(2)}, u32[]{:S(2)}) collective-permute-start(f32[48,256]{1,0:T(8,128)S(1)} %get-tuple-element.42), channel_id=1, source_target_pairs={{4,0},{8,4},{12,8},{0,12},{5,1},{9,5},{13,9},{1,13},{6,2},{10,6},{... | collective-permute-start | bytes 147464 | tf_op jit(solution)/shard_map/ppermute | solution.py:25

commit v7 on v6

--- a/solution.py
+++ b/solution.py
@@ -13,6 +13,7 @@
 spread_v = 0.5
 LANES = 128
 STEPS = 8
+HALF = 4
 FIELDS = 3
 VMEM = pltpu.VMEM
 SMEM = pltpu.SMEM
@@ -97,68 +98,70 @@
 def first_kernel(lead, slots, cell_blocks, *refs):
     refs = list(refs)
     sources = [refs.pop(0) for _ in range(FIELDS)]
-    rows_hbm, count_hbm, send, held, listed, last, rows_ref, count_ref, sems = refs
-    stride = 2 * cell_blocks
-    early = (lead[0] * STEPS - 1) * stride
-    late = held.shape[1] - early
+    rows_hbm, count_hbm, send, listed, near, rows_ref, count_ref, sems = refs
+    stride = 2 * cell_blocks
+    first = (lead[0] * STEPS - 1) * stride
     small = [
-        pltpu.make_async_copy(rows_hbm, rows_ref, sems.at[2 * FIELDS]),
-        pltpu.make_async_copy(count_hbm, count_ref, sems.at[2 * FIELDS + 1]),
+        pltpu.make_async_copy(rows_hbm, rows_ref, sems.at[FIELDS]),
+        pltpu.make_async_copy(count_hbm, count_ref, sems.at[FIELDS + 1]),
     ]
     needed = [
-        pltpu.make_async_copy(sources[f].at[pl.ds(early, late), :], held.at[f, pl.ds(early, late), :], sems.at[f])
+        pltpu.make_async_copy(sources[f].at[pl.ds(first, near.shape[1]), :], near.at[f], sems.at[f])
         for f in range(FIELDS)
     ]
-    others = [
-        pltpu.make_async_copy(sources[f].at[pl.ds(0, early), :], held.at[f, pl.ds(0, early), :], sems.at[FIELDS + f])
-        for f in range(FIELDS)
-    ]
-    for copy in small + needed + others:
+    for copy in small + needed:
         copy.start()
     for copy in small:
         copy.wait()
     lane = lax.broadcasted_iota(jnp.int32, rows_ref.shape, 1)
+    columns = {}
     for slot in range(rows_ref.shape[0]):
-        listed[slot : slot + 1, :] = jnp.where(
-            lane[slot : slot + 1] < count_ref[:, slot : slot + 1], rows_ref[slot : slot + 1, :], -1
-        )
+        live = lane[slot : slot + 1] < count_ref[:, slot : slot + 1]
+        row = jnp.where(live, rows_ref[slot : slot + 1, :], -1)
+        listed[slot : slot + 1, :] = row
+        columns[slot] = [row[:, start : start + LANES] for start in range(0, row.shape[1], LANES)]
+    columns = [jnp.broadcast_to(column, (STEPS, LANES)) for slot in slots for column in columns[slot]]
+    lanes = [column & (LANES - 1) for column in columns]
+    blocks = [column >> 7 for column in columns]
     for copy in needed:
         copy.wait()
-    columns = [
-        listed[slot : slot + 1, start : start + LANES]
-        for slot in slots
-        for start in range(0, listed.shape[1], LANES)
-    ]
-    columns = [jnp.broadcast_to(column, (STEPS, LANES)) for column in columns]
-    for place, group in enumerate(lead):
+    for place in range(len(lead)):
         for field in range(FIELDS):
-            for species in range(2):
+            for species, spread in enumerate((spread_u, spread_v)):
                 row = ((place * FIELDS + field) * 2 + species) * STEPS
-                sums = [
-                    scaled_sum(held.at[field], None, field, group, block, species, stride) for block in range(cell_blocks)
-                ]
-                for number, column in enumerate(columns):
-                    lanes = column & (LANES - 1)
+                sums = []
+                for block in range(cell_blocks):
+                    at = place * STEPS * stride + block * 2 + species
+                    before = near[field, pl.ds(at, STEPS, stride=stride), :]
+                    now = near[field, pl.ds(at + stride, STEPS, stride=stride), :]
+                    sums.append((now + before) * (-0.5 * spread))
+                for number in range(len(columns)):
                     found = jnp.zeros((STEPS, LANES), F32)
                     for block in range(cell_blocks):
-                        taken = jnp.take_along_axis(sums[block], lanes, axis=1, mode="promise_in_bounds")
-                        found = jnp.where(column >> 7 == block, taken, found)
+                        taken = jnp.take_along_axis(sums[block], lanes[number], axis=1, mode="promise_in_bounds")
+                        found = jnp.where(blocks[number] == block, taken, found)
                     send[row : row + STEPS, number * LANES : (number + 1) * LANES] = found
-    for field in range(FIELDS):
-        last[field * stride : (field + 1) * stride, :] = held[field, -stride:, :]
-    for copy in others:
+
+
+def second_kernel(most, middle, wide, others, cell_blocks, *refs):
+    refs = list(refs)
+    sources = [refs.pop(0) for _ in range(FIELDS)]
+    listed, send, *sends, parts_ref, held, last, choose, sems = refs
+    copies = [pltpu.make_async_copy(sources[f], held.at[f], sems.at[f]) for f in range(FIELDS)]
+    for copy in copies:
+        copy.start()
+    choose_rows(wide + others, listed, choose)
+    for copy in copies:
         copy.wait()
-
-
-def second_kernel(most, middle, wide, others, cell_blocks, held, listed, send, *refs):
-    *sends, parts_ref, choose = refs
+    stride = 2 * cell_blocks
     size = parts_ref.shape[1] // 2
     middle_size = size * len(middle) // len(most)
-    choose_rows(wide + others, listed, choose)
     summed_parts(most, cell_blocks, [held.at[f] for f in range(FIELDS)], None, parts_ref, 0, size)
     width = send.shape[1]
     take_rows(side_by_side(parts_ref, [(0, middle_size), (size, middle_size)]), choose, [send])
     take_rows(side_by_side(parts_ref, [(0, 2 * size)]), choose.at[:, width:], sends)
+    for field in range(FIELDS):
+        last[field * stride : (field + 1) * stride, :] = held[field, -stride:, :]
 
 
 def third_kernel(late, wide, others, cell_blocks, held, prev, listed, *refs):
@@ -238,6 +241,8 @@
                 high, low = split(ref[:, lane : lane + LANES])
                 extended[cell_blocks + slot * per_slot + b, row : row + count, :] = high
                 extended[cell_blocks + slot * per_slot + b, size + row : size + row + count, :] = low
+    steps = len(groups) * STEPS
+    copies = []
     for block in range(blocks):
         chosen = jnp.concatenate([extended[cols[k, block]] for k in range(per_row)], axis=1)
         product = jnp.dot(chosen, split_tiles[block], preferred_element_type=F32)
@@ -247,10 +252,16 @@
             group, field, species = index // (2 * FIELDS), index // 2 % FIELDS, index % 2
             at = group * STEPS * stride + block * 2 + species
             made[field, pl.ds(at, STEPS, stride=stride), :] = result[index * STEPS : (index + 1) * STEPS, :]
-    span = pl.ds(groups[0] * STEPS * stride, len(groups) * STEPS * stride)
-    copies = [pltpu.make_async_copy(made.at[f], outs[f].at[span, :], sems.at[f]) for f in range(FIELDS)]
-    for copy in copies:
-        copy.start()
+        if (block + 1) % HALF == 0:
+            span = pl.ds((block + 1 - HALF) * 2, 2 * HALF)
+            for field in range(FIELDS):
+                copy = pltpu.make_async_copy(
+                    made.at[field].reshape(steps, stride, LANES).at[:, span, :],
+                    outs[field].at[pl.ds(groups[0] * STEPS, steps), span, :],
+                    sems.at[field, block // HALF],
+                )
+                copy.start()
+                copies.append(copy)
     for copy in copies:
         copy.wait()
 
@@ -319,36 +330,35 @@
     size = rows_of(groups)
     every = len(OFFSETS) * slot_rows
     wide_width = len(wide) * slot_rows
-    send, held, listed, last = pl.pallas_call(
+    first_fields = in_hbm(*fields)
+    send, listed = pl.pallas_call(
         functools.partial(first_kernel, lead, wide, cell_blocks),
-        out_shape=[
-            f32(rows_of(lead), wide_width),
-            f32(FIELDS, steps * stride, LANES),
-            jax.ShapeDtypeStruct(rows.shape, jnp.int32),
-            f32(FIELDS * stride, LANES),
-        ],
+        out_shape=[f32(rows_of(lead), wide_width), jax.ShapeDtypeStruct(rows.shape, jnp.int32)],
         in_specs=[hbm] * (FIELDS + 2),
-        out_specs=[vmem] * 4,
+        out_specs=[vmem] * 2,
         scratch_shapes=[
+            VMEM((FIELDS, (len(lead) * STEPS + 1) * stride, LANES), F32),
             VMEM(rows.shape, jnp.int32),
             VMEM(counts.shape, jnp.int32),
-            pltpu.SemaphoreType.DMA((2 * FIELDS + 2,)),
+            pltpu.SemaphoreType.DMA((FIELDS + 2,)),
         ],
         compiler_params=params,
         cost_estimate=cost(4 * rows_of(lead) * cells * wide_width, 8 * size * cells),
         name="gather_first",
-    )(*in_hbm(*fields, rows, counts))
+    )(*first_fields, *in_hbm(rows, counts))
     wide_lead = send_to(send, wide)
-    send, *sends, most_parts = pl.pallas_call(
+    send, *sends, most_parts, held, last = pl.pallas_call(
         functools.partial(second_kernel, most, middle, wide, others, cell_blocks),
-        out_shape=sends_of(middle, [wide]) + sends_of(most, narrow) + [parts_of(most)],
-        in_specs=[vmem] * 2,
-        out_specs=[vmem] * (len(narrow) + 2),
-        scratch_shapes=[VMEM((cells, every), BF16)],
+        out_shape=sends_of(middle, [wide])
+        + sends_of(most, narrow)
+        + [parts_of(most), f32(FIELDS, steps * stride, LANES), f32(FIELDS * stride, LANES)],
+        in_specs=[hbm] * FIELDS + [vmem],
+        out_specs=[vmem] * (len(narrow) + 4),
+        scratch_shapes=[VMEM((cells, every), BF16), pltpu.SemaphoreType.DMA((FIELDS,))],
         compiler_params=params,
         cost_estimate=cost(4 * rows_of(most) * cells * every, 8 * size * cells),
         name="gather_second",
-    )(held, listed)
+    )(*first_fields, listed)
     wide_middle = send_to(send, wide)
     prev = shift_along(last, "tm", 1)
     narrow_most = [send_to(part, slots) for part, slots in zip(sends, narrow)]
@@ -394,14 +404,14 @@
         received = [(slots, row) for _, slots, row in transfers]
         return pl.pallas_call(
             functools.partial(apply_kernel, part, received, cell_blocks, blocks, per_row, len(outs)),
-            out_shape=[f32(steps * stride, LANES)] * FIELDS,
+            out_shape=[f32(steps, stride, LANES)] * FIELDS,
             in_specs=[vmem] * len(inputs) + [anywhere] * len(outs),
             out_specs=[anywhere] * FIELDS,
             input_output_aliases={len(inputs) + f: f for f in range(len(outs))},
             scratch_shapes=[
                 VMEM((cell_blocks + every // LANES, 2 * rows_of(part), LANES), BF16),
                 VMEM((FIELDS, len(part) * STEPS * stride, LANES), F32),
-                pltpu.SemaphoreType.DMA((FIELDS,)),
+                pltpu.SemaphoreType.DMA((FIELDS, blocks // HALF)),
             ],
             compiler_params=params,
             cost_estimate=cost(8 * rows_of(part) * blocks * per_row * LANES * LANES, 16 * rows_of(part) * cells),

time: 26.9 us -> 26.8 us (level)
  waiting for transfers between devices: 4.52 us -> 0.77 us
  starting transfers between devices: 14.1 us -> 16.7 us
  Pallas kernels: 7.45 us -> 8.46 us
    ppermute x8, waiting for transfers between devices: 4.52 us -> 0.77 us  [shift_along(): lax.ppermute(block, axis, [((i - distance) % size, i) for i in range(size)])]
    ppermute x8, starting transfers between devices: 14.1 us -> 16.7 us  [shift_along(): lax.ppermute(block, axis, [((i - distance) % size, i) for i in range(size)])]
    pallas_call x1, Pallas kernels: 0.81 us -> 1.91 us  [per_device(): pl.pallas_call(functools.partial(second_kernel, most, middle, wide, other...]
  transfers between devices with their start and end apart: 8 -> 8, of which waited for: 4 -> 1; matrix products, arithmetic and copies ran while one was open for 0% -> 0% of each run, Pallas kernels for 18% -> 22%
where the time goes in v7:
time: 26.8 us; the launch traced here: 26.6 us
  starting transfers between devices  16.7 us (62%)
  Pallas kernels  8.46 us (32%)
  waiting for transfers between devices  0.77 us (3%)
  between operations  0.71 us (3%)
    ppermute x8, starting transfers between devices, shift_along(): lax.ppermute(block, axis, [((i - distance) % size, i) for i in range(size)])  16.7 us
    pallas_call x2, Pallas kernels, apply(): pl.pallas_call(functools.partial(apply_kernel, part, received, cell_block...  2.63 us
    pallas_call x1, Pallas kernels, per_device(): pl.pallas_call(functools.partial(local_kernel, (most, late), cell_blocks)...  1.94 us
    pallas_call x1, Pallas kernels, per_device(): pl.pallas_call(functools.partial(second_kernel, most, middle, wide, other...  1.91 us
    pallas_call x1, Pallas kernels, per_device(): pl.pallas_call(functools.partial(first_kernel, lead, wide, cell_blocks),...  1.41 us
    ppermute x8, waiting for transfers between devices, shift_along(): lax.ppermute(block, axis, [((i - distance) % size, i) for i in range(size)])  0.77 us
    pallas_call x1, Pallas kernels, per_device(): pl.pallas_call(functools.partial(third_kernel, late, wide, others, cell_b...  0.57 us
  transfers between devices with their start and end apart: 8, of which 1 were waited for; matrix products, arithmetic and copies ran while one was open for 0% of the time, Pallas kernels for 22%

profile of v7, /device:TPU:0, one launch (start us, length us, event | category | flops | bytes accessed | tf_op | source)
XLA Modules:
  0.0 26.6 jit_solution(9121335950859182711)
XLA Ops:
  0.6 1.4 %gather_first.1 = (f32[48,512]{1,0:T(8,128)S(1)}, s32[4,256]{1,0:T(4,128)S(1)}) custom-call(f32[384,128]{1,0:T(8,128)} %bitcast.39, f32[384,128]{1,0:T(8,128)} %bitcast.41, f32[384,128]{1,0:T(8,128)} %bitcast.43, s32[4,256]{1,0:T(4,128)} %bitcast.45, s32[1,4]{1,0:T(1,128)} %refs_4_.1), custom_call_target="tpu_custom_call" | custom-call | flops 100663296 | bytes 1179648 | tf_op jit(solution)/shard_map/gather_first/pallas_call | solution.py:334
  2.0 4.1 %collective-permute-start.3 = (f32[48,512]{1,0:T(8,128)S(1)}, f32[48,512]{1,0:T(8,128)S(1)}, u32[]{:S(2)}, u32[]{:S(2)}) collective-permute-start(f32[48,512]{1,0:T(8,128)S(1)} %get-tuple-element.40), channel_id=1, source_target_pairs={{8,0},{12,4},{0,8},{4,12},{9,1},{13,5},{1,9},{5,13},{10,2},{14,6},... | collective-permute-start | bytes 294920 | tf_op jit(solution)/shard_map/ppermute | solution.py:26
  6.1 1.9 %gather_second.1 = (f32[48,512]{1,0:T(8,128)S(1)}, f32[96,256]{1,0:T(8,128)S(1)}, f32[96,256]{1,0:T(8,128)S(1)}, bf16[8,192,128]{2,1,0:T(8,128)(2,1)S(1)}, f32[3...) custom-call(f32[384,128]{1,0:T(8,128)} %bitcast.40, f32[384,128]{1,0:T(8,128)} %bitcast.42, f32[384,128]{1,0:T(8,128)} %bitcast.44, ...), custom_call_target="tpu_custom_call" | custom-call | flops 402653184 | bytes 1179648 | tf_op jit(solution)/shard_map/gather_second/pallas_call | solution.py:350
  8.1 0.0 copy-start
  8.1 0.1 collective-permute-start.1
  8.2 0.1 collective-permute-start
  8.2 1.8 %collective-permute-start.6 = (f32[96,256]{1,0:T(8,128)S(1)}, f32[96,256]{1,0:T(8,128)S(1)}, u32[]{:S(2)}, u32[]{:S(2)}) collective-permute-start(f32[96,256]{1,0:T(8,128)S(1)} %get-tuple-element.47), channel_id=1, source_target_pairs={{12,0},{0,4},{4,8},{8,12},{13,1},{1,5},{5,9},{9,13},{14,2},{2,6},{... | collective-permute-start | bytes 294920 | tf_op jit(solution)/shard_map/ppermute | solution.py:26
  10.1 2.0 %collective-permute-start.7 = (f32[96,256]{1,0:T(8,128)S(1)}, f32[96,256]{1,0:T(8,128)S(1)}, u32[]{:S(2)}, u32[]{:S(2)}) collective-permute-start(f32[96,256]{1,0:T(8,128)S(1)} %get-tuple-element.48), channel_id=1, source_target_pairs={{4,0},{8,4},{12,8},{0,12},{5,1},{9,5},{13,9},{1,13},{6,2},{10,6},{... | collective-permute-start | bytes 294920 | tf_op jit(solution)/shard_map/ppermute | solution.py:26
  12.1 0.0 collective-permute-done.prev
  12.1 0.6 %gather_third.1 = (f32[48,512]{1,0:T(8,128)S(1)}, f32[48,256]{1,0:T(8,128)S(1)}, f32[48,256]{1,0:T(8,128)S(1)}, bf16[8,96,128]{2,1,0:T(8,128)(2,1)S(1)}) custom-call(f32[3,384,128]{2,1,0:T(8,128)S(1)} %get-tuple-element.30.held, f32[48,128]{1,0:T(8,128)S(1)} %collective-permute-done.prev, s32[4,256]{1,0:T(4,128)S(1)} %get-tuple-element.29.refs_3_.listed), custom_call_target="tpu_custom_call" | custom-call | flops 201326592 | bytes 1179648 | tf_op jit(solution)/shard_map/gather_third/pallas_call | solution.py:365
  12.7 2.3 %collective-permute-start.2 = (f32[48,512]{1,0:T(8,128)S(1)}, f32[48,512]{1,0:T(8,128)S(1)}, u32[]{:S(2)}, u32[]{:S(2)}) collective-permute-start(f32[48,512]{1,0:T(8,128)S(1)} %get-tuple-element.38), channel_id=1, source_target_pairs={{8,0},{12,4},{0,8},{4,12},{9,1},{13,5},{1,9},{5,13},{10,2},{14,6},... | collective-permute-start | bytes 294920 | tf_op jit(solution)/shard_map/ppermute | solution.py:26
  15.0 1.9 %local_terms.1 = (f32[8,96,128]{2,1,0:T(8,128)S(1)}, f32[8,48,128]{2,1,0:T(8,128)S(1)}, bf16[8,384,256]{2,1,0:T(8,128)(2,1)S(1)}) custom-call(f32[3,384,128]{2,1,0:T(8,128)S(1)} %get-tuple-element.30.held, f32[48,128]{1,0:T(8,128)S(1)} %collective-permute-done.prev, f32[8,128]{1,0:T(8,128)} %bitcast.46, f32[8,128]{1,0:T(8,128)} %bitcast.47, ...), custom_call_target="tpu_custom_call" | custom-call | flops 8847360 | bytes 3145728 | tf_op jit(solution)/shard_map/local_terms/pallas_call | solution.py:375
  16.9 0.0 collective-permute-done.3.refs_5_
  16.9 1.6 %collective-permute-start.4 = (f32[48,256]{1,0:T(8,128)S(1)}, f32[48,256]{1,0:T(8,128)S(1)}, u32[]{:S(2)}, u32[]{:S(2)}) collective-permute-start(f32[48,256]{1,0:T(8,128)S(1)} %get-tuple-element.41), channel_id=1, source_target_pairs={{12,0},{0,4},{4,8},{8,12},{13,1},{1,5},{5,9},{9,13},{14,2},{2,6},{... | collective-permute-start | bytes 147464 | tf_op jit(solution)/shard_map/ppermute | solution.py:26
  18.6 0.0 collective-permute-done.1.refs_4_
  18.6 4.6 %collective-permute-start.5 = (f32[48,256]{1,0:T(8,128)S(1)}, f32[48,256]{1,0:T(8,128)S(1)}, u32[]{:S(2)}, u32[]{:S(2)}) collective-permute-start(f32[48,256]{1,0:T(8,128)S(1)} %get-tuple-element.42), channel_id=1, source_target_pairs={{4,0},{8,4},{12,8},{0,12},{5,1},{9,5},{13,9},{1,13},{6,2},{10,6},{... | collective-permute-start | bytes 147464 | tf_op jit(solution)/shard_map/ppermute | solution.py:26
  23.2 0.0 collective-permute-done.6.refs_6_
  23.2 0.0 collective-permute-done.7.refs_7_
  23.2 0.0 copy-done
  23.2 1.4 %apply_tiles.2 = (f32[24,16,128]{2,1,0:T(8,128)}, f32[24,16,128]{2,1,0:T(8,128)}, f32[24,16,128]{2,1,0:T(8,128)}) custom-call(s32[3,8]{1,0:T(4,128)S(1)} %bitcast.34, bf16[8,384,256]{2,1,0:T(8,128)(2,1)S(1)} %get-tuple-element.35.refs_1_, f32[8,96,128]{2,1,0:T(8,128)S(1)} %get-tuple-element.43.refs_2_, bf16[8,192,128]{2,1,0:T(8,128)(2,1)S(1)} %get-tuple-element.44.refs_3_, ...), custom_call_target="tpu_custom_call" | custom-call | flops 301989888 | bytes 1572864 | tf_op jit(solution)/shard_map/apply_tiles/pallas_call | solution.py:405
  24.7 0.8 %collective-permute-done.2.refs_4_ = f32[48,512]{1,0:T(8,128)S(1)} collective-permute-done((f32[48,512]{1,0:T(8,128)S(1)}, f32[48,512]{1,0:T(8,128)S(1)}, u32[]{:S(2)}, u32[]{:S(2)}) %collective-permute-start.2) | collective-permute-done | bytes 98336 | tf_op jit(solution)/shard_map/ppermute | solution.py:26
  25.4 0.0 collective-permute-done.4.refs_5_
  25.4 0.0 collective-permute-done.5.refs_6_
  25.4 1.2 %apply_tiles.3 = (f32[24,16,128]{2,1,0:T(8,128)}, f32[24,16,128]{2,1,0:T(8,128)}, f32[24,16,128]{2,1,0:T(8,128)}) custom-call(s32[3,8]{1,0:T(4,128)S(1)} %bitcast.35, bf16[8,384,256]{2,1,0:T(8,128)(2,1)S(1)} %get-tuple-element.35.refs_1_, f32[8,48,128]{2,1,0:T(8,128)S(1)} %get-tuple-element.36.refs_2_, ...), custom_call_target="tpu_custom_call", output_to_operand_aliasing={{0}: (7, {}), {1}: (8, {}), {2}: (9, {})} | custom-call | flops 150994944 | bytes 786432 | tf_op jit(solution)/shard_map/apply_tiles/pallas_call | solution.py:405
Async XLA Ops:
  2.0 14.9 %collective-permute-start.3 = (f32[48,512]{1,0:T(8,128)S(1)}, f32[48,512]{1,0:T(8,128)S(1)}, u32[]{:S(2)}, u32[]{:S(2)}) collective-permute-start(f32[48,512]{1,0:T(8,128)S(1)} %get-tuple-element.40), channel_id=1, source_target_pairs={{8,0},{12,4},{0,8},{4,12},{9,1},{13,5},{1,9},{5,13},{10,2},{14,6},... | collective-permute-start | bytes 294920 | tf_op jit(solution)/shard_map/ppermute | solution.py:26
  8.1 15.1 %copy-start = (s32[8,3]{0,1:T(4,128)S(1)}, s32[8,3]{0,1:T(4,128)}, u32[]{:S(2)}) copy-start(s32[8,3]{0,1:T(4,128)} %param.15) | copy-start | bytes 292
  8.1 10.5 %collective-permute-start.1 = (f32[48,512]{1,0:T(8,128)S(1)}, f32[48,512]{1,0:T(8,128)S(1)}, u32[]{:S(2)}, u32[]{:S(2)}) collective-permute-start(f32[48,512]{1,0:T(8,128)S(1)} %get-tuple-element.33), channel_id=1, source_target_pairs={{8,0},{12,4},{0,8},{4,12},{9,1},{13,5},{1,9},{5,13},{10,2},{14,6},... | collective-permute-start | bytes 294920 | tf_op jit(solution)/shard_map/ppermute | solution.py:26
  8.2 3.9 %collective-permute-start = (f32[48,128]{1,0:T(8,128)S(1)}, f32[48,128]{1,0:T(8,128)S(1)}, u32[]{:S(2)}, u32[]{:S(2)}) collective-permute-start(f32[48,128]{1,0:T(8,128)S(1)} %get-tuple-element.31), channel_id=1, source_target_pairs={{3,0},{0,1},{1,2},{2,3},{7,4},{4,5},{5,6},{6,7},{11,8},{8,9},{9,10... | collective-permute-start | bytes 73736 | tf_op jit(solution)/shard_map/ppermute | solution.py:26
  8.2 15.0 %collective-permute-start.6 = (f32[96,256]{1,0:T(8,128)S(1)}, f32[96,256]{1,0:T(8,128)S(1)}, u32[]{:S(2)}, u32[]{:S(2)}) collective-permute-start(f32[96,256]{1,0:T(8,128)S(1)} %get-tuple-element.47), channel_id=1, source_target_pairs={{12,0},{0,4},{4,8},{8,12},{13,1},{1,5},{5,9},{9,13},{14,2},{2,6},{... | collective-permute-start | bytes 294920 | tf_op jit(solution)/shard_map/ppermute | solution.py:26
  10.1 13.1 %collective-permute-start.7 = (f32[96,256]{1,0:T(8,128)S(1)}, f32[96,256]{1,0:T(8,128)S(1)}, u32[]{:S(2)}, u32[]{:S(2)}) collective-permute-start(f32[96,256]{1,0:T(8,128)S(1)} %get-tuple-element.48), channel_id=1, source_target_pairs={{4,0},{8,4},{12,8},{0,12},{5,1},{9,5},{13,9},{1,13},{6,2},{10,6},{... | collective-permute-start | bytes 294920 | tf_op jit(solution)/shard_map/ppermute | solution.py:26
  12.7 12.7 %collective-permute-start.2 = (f32[48,512]{1,0:T(8,128)S(1)}, f32[48,512]{1,0:T(8,128)S(1)}, u32[]{:S(2)}, u32[]{:S(2)}) collective-permute-start(f32[48,512]{1,0:T(8,128)S(1)} %get-tuple-element.38), channel_id=1, source_target_pairs={{8,0},{12,4},{0,8},{4,12},{9,1},{13,5},{1,9},{5,13},{10,2},{14,6},... | collective-permute-start | bytes 294920 | tf_op jit(solution)/shard_map/ppermute | solution.py:26
  16.9 8.5 %collective-permute-start.4 = (f32[48,256]{1,0:T(8,128)S(1)}, f32[48,256]{1,0:T(8,128)S(1)}, u32[]{:S(2)}, u32[]{:S(2)}) collective-permute-start(f32[48,256]{1,0:T(8,128)S(1)} %get-tuple-element.41), channel_id=1, source_target_pairs={{12,0},{0,4},{4,8},{8,12},{13,1},{1,5},{5,9},{9,13},{14,2},{2,6},{... | collective-permute-start | bytes 147464 | tf_op jit(solution)/shard_map/ppermute | solution.py:26
  18.6 6.9 %collective-permute-start.5 = (f32[48,256]{1,0:T(8,128)S(1)}, f32[48,256]{1,0:T(8,128)S(1)}, u32[]{:S(2)}, u32[]{:S(2)}) collective-permute-start(f32[48,256]{1,0:T(8,128)S(1)} %get-tuple-element.42), channel_id=1, source_target_pairs={{4,0},{8,4},{12,8},{0,12},{5,1},{9,5},{13,9},{1,13},{6,2},{10,6},{... | collective-permute-start | bytes 147464 | tf_op jit(solution)/shard_map/ppermute | solution.py:26

commit v8 on v6

--- a/solution.py
+++ b/solution.py
@@ -386,7 +386,7 @@
     sends[1], wide_lead = lax.optimization_barrier((sends[1], wide_lead))
     arrived_late.append(send_to(sends[1], slot_groups[1]))
     for number in range(2, len(sends)):
-        sends[number], wide_middle, split_tiles = lax.optimization_barrier((sends[number], wide_middle, split_tiles))
+        sends[number], narrow_most[0], split_tiles = lax.optimization_barrier((sends[number], narrow_most[0], split_tiles))
         arrived_late.append(send_to(sends[number], slot_groups[number]))
 
     def apply(part, base, parts, transfers, outs):

time: 26.9 us -> 26.4 us (0.981)
  starting transfers between devices: 14.1 us -> 13.2 us
  waiting for transfers between devices: 4.52 us -> 4.9 us
    ppermute x8, starting transfers between devices: 14.1 us -> 13.2 us  [shift_along(): lax.ppermute(block, axis, [((i - distance) % size, i) for i in range(size)])]
    ppermute x8, waiting for transfers between devices: 4.52 us -> 4.9 us  [shift_along(): lax.ppermute(block, axis, [((i - distance) % size, i) for i in range(size)])]
  transfers between devices with their start and end apart: 8 -> 8, of which waited for: 4 -> 2; matrix products, arithmetic and copies ran while one was open for 0% -> 0% of each run, Pallas kernels for 18% -> 18%
where the time goes in v8:
time: 26.4 us; the launch traced here: 26.3 us
  starting transfers between devices  13.2 us (50%)
  Pallas kernels  7.45 us (28%)
  waiting for transfers between devices  4.9 us (19%)
  between operations  0.7 us (3%)
    ppermute x8, starting transfers between devices, shift_along(): lax.ppermute(block, axis, [((i - distance) % size, i) for i in range(size)])  13.2 us
    ppermute x8, waiting for transfers between devices, shift_along(): lax.ppermute(block, axis, [((i - distance) % size, i) for i in range(size)])  4.9 us
    pallas_call x2, Pallas kernels, apply(): pl.pallas_call(functools.partial(apply_kernel, part, received, cell_block...  2.68 us
    pallas_call x1, Pallas kernels, per_device(): pl.pallas_call(functools.partial(local_kernel, (most, late), cell_blocks)...  1.94 us
    pallas_call x1, Pallas kernels, per_device(): pl.pallas_call(functools.partial(first_kernel, lead, wide, cell_blocks),...  1.44 us
    pallas_call x1, Pallas kernels, per_device(): pl.pallas_call(functools.partial(second_kernel, most, middle, wide, other...  0.81 us
    pallas_call x1, Pallas kernels, per_device(): pl.pallas_call(functools.partial(third_kernel, late, wide, others, cell_b...  0.57 us
  transfers between devices with their start and end apart: 8, of which 2 were waited for; matrix products, arithmetic and copies ran while one was open for 0% of the time, Pallas kernels for 18%

profile of v8, /device:TPU:0, one launch (start us, length us, event | category | flops | bytes accessed | tf_op | source)
XLA Modules:
  0.0 26.3 jit_solution(7951586988934342663)
XLA Ops:
  0.6 1.4 %gather_first.1 = (f32[48,512]{1,0:T(8,128)S(1)}, f32[3,384,128]{2,1,0:T(8,128)S(1)}, s32[4,256]{1,0:T(4,128)S(1)}, f32[48,128]{1,0:T(8,128)S(1)}) custom-call(f32[384,128]{1,0:T(8,128)} %bitcast.39, f32[384,128]{1,0:T(8,128)} %bitcast.40, f32[384,128]{1,0:T(8,128)} %bitcast.41, s32[4,256]{1,0:T(4,128)} %bitcast.42, s32[1,4]{1,0:T(1,128)} %refs_4_.1), custom_call_target="tpu_custom_call" | custom-call | flops 100663296 | bytes 1179648 | tf_op jit(solution)/shard_map/gather_first/pallas_call | solution.py:322
  2.1 4.1 %collective-permute-start.3 = (f32[48,512]{1,0:T(8,128)S(1)}, f32[48,512]{1,0:T(8,128)S(1)}, u32[]{:S(2)}, u32[]{:S(2)}) collective-permute-start(f32[48,512]{1,0:T(8,128)S(1)} %get-tuple-element.40), channel_id=1, source_target_pairs={{8,0},{12,4},{0,8},{4,12},{9,1},{13,5},{1,9},{5,13},{10,2},{14,6},... | collective-permute-start | bytes 294920 | tf_op jit(solution)/shard_map/ppermute | solution.py:25
  6.2 0.8 %gather_second.1 = (f32[48,512]{1,0:T(8,128)S(1)}, f32[96,256]{1,0:T(8,128)S(1)}, f32[96,256]{1,0:T(8,128)S(1)}, bf16[8,192,128]{2,1,0:T(8,128)(2,1)S(1)}) custom-call(f32[3,384,128]{2,1,0:T(8,128)S(1)} %get-tuple-element.29.held, s32[4,256]{1,0:T(4,128)S(1)} %get-tuple-element.31.listed), custom_call_target="tpu_custom_call" | custom-call | flops 402653184 | bytes 1179648 | tf_op jit(solution)/shard_map/gather_second/pallas_call | solution.py:342
  7.0 0.0 copy-start
  7.0 1.6 %collective-permute-start.1 = (f32[96,256]{1,0:T(8,128)S(1)}, f32[96,256]{1,0:T(8,128)S(1)}, u32[]{:S(2)}, u32[]{:S(2)}) collective-permute-start(f32[96,256]{1,0:T(8,128)S(1)} %get-tuple-element.33), channel_id=1, source_target_pairs={{12,0},{0,4},{4,8},{8,12},{13,1},{1,5},{5,9},{9,13},{14,2},{2,6},{... | collective-permute-start | bytes 294920 | tf_op jit(solution)/shard_map/ppermute | solution.py:25
  8.6 0.0 collective-permute-start
  8.6 0.3 %collective-permute-start.6 = (f32[48,512]{1,0:T(8,128)S(1)}, f32[48,512]{1,0:T(8,128)S(1)}, u32[]{:S(2)}, u32[]{:S(2)}) collective-permute-start(f32[48,512]{1,0:T(8,128)S(1)} %get-tuple-element.45), channel_id=1, source_target_pairs={{8,0},{12,4},{0,8},{4,12},{9,1},{13,5},{1,9},{5,13},{10,2},{14,6},... | collective-permute-start | bytes 294920 | tf_op jit(solution)/shard_map/ppermute | solution.py:25
  9.0 2.2 %collective-permute-start.7 = (f32[96,256]{1,0:T(8,128)S(1)}, f32[96,256]{1,0:T(8,128)S(1)}, u32[]{:S(2)}, u32[]{:S(2)}) collective-permute-start(f32[96,256]{1,0:T(8,128)S(1)} %get-tuple-element.48), channel_id=1, source_target_pairs={{4,0},{8,4},{12,8},{0,12},{5,1},{9,5},{13,9},{1,13},{6,2},{10,6},{... | collective-permute-start | bytes 294920 | tf_op jit(solution)/shard_map/ppermute | solution.py:25
  11.2 0.7 %collective-permute-done.prev = f32[48,128]{1,0:T(8,128)S(1)} collective-permute-done((f32[48,128]{1,0:T(8,128)S(1)}, f32[48,128]{1,0:T(8,128)S(1)}, u32[]{:S(2)}, u32[]{:S(2)}) %collective-permute-start) | collective-permute-done | bytes 24608 | tf_op jit(solution)/shard_map/ppermute | solution.py:25
  11.9 0.6 %gather_third.1 = (f32[48,512]{1,0:T(8,128)S(1)}, f32[48,256]{1,0:T(8,128)S(1)}, f32[48,256]{1,0:T(8,128)S(1)}, bf16[8,96,128]{2,1,0:T(8,128)(2,1)S(1)}) custom-call(f32[3,384,128]{2,1,0:T(8,128)S(1)} %get-tuple-element.29.held, f32[48,128]{1,0:T(8,128)S(1)} %collective-permute-done.prev, s32[4,256]{1,0:T(4,128)S(1)} %get-tuple-element.31.listed), custom_call_target="tpu_custom_call" | custom-call | flops 201326592 | bytes 1179648 | tf_op jit(solution)/shard_map/gather_third/pallas_call | solution.py:355
  12.5 1.1 %collective-permute-start.2 = (f32[48,512]{1,0:T(8,128)S(1)}, f32[48,512]{1,0:T(8,128)S(1)}, u32[]{:S(2)}, u32[]{:S(2)}) collective-permute-start(f32[48,512]{1,0:T(8,128)S(1)} %get-tuple-element.38), channel_id=1, source_target_pairs={{8,0},{12,4},{0,8},{4,12},{9,1},{13,5},{1,9},{5,13},{10,2},{14,6},... | collective-permute-start | bytes 294920 | tf_op jit(solution)/shard_map/ppermute | solution.py:25
  13.6 1.9 %local_terms.1 = (f32[8,96,128]{2,1,0:T(8,128)S(1)}, f32[8,48,128]{2,1,0:T(8,128)S(1)}, bf16[8,384,256]{2,1,0:T(8,128)(2,1)S(1)}) custom-call(f32[3,384,128]{2,1,0:T(8,128)S(1)} %get-tuple-element.29.held, f32[48,128]{1,0:T(8,128)S(1)} %collective-permute-done.prev, f32[8,128]{1,0:T(8,128)} %bitcast.43, f32[8,128]{1,0:T(8,128)} %bitcast.44, ...), custom_call_target="tpu_custom_call" | custom-call | flops 8847360 | bytes 3145728 | tf_op jit(solution)/shard_map/local_terms/pallas_call | solution.py:365
  15.5 0.0 collective-permute-done.3.refs_5_
  15.5 1.8 %collective-permute-start.4 = (f32[48,256]{1,0:T(8,128)S(1)}, f32[48,256]{1,0:T(8,128)S(1)}, u32[]{:S(2)}, u32[]{:S(2)}) collective-permute-start(f32[48,256]{1,0:T(8,128)S(1)} %get-tuple-element.41), channel_id=1, source_target_pairs={{12,0},{0,4},{4,8},{8,12},{13,1},{1,5},{5,9},{9,13},{14,2},{2,6},{... | collective-permute-start | bytes 147464 | tf_op jit(solution)/shard_map/ppermute | solution.py:25
  17.4 0.0 collective-permute-done.1.refs_6_
  17.4 2.0 %collective-permute-start.5 = (f32[48,256]{1,0:T(8,128)S(1)}, f32[48,256]{1,0:T(8,128)S(1)}, u32[]{:S(2)}, u32[]{:S(2)}) collective-permute-start(f32[48,256]{1,0:T(8,128)S(1)} %get-tuple-element.42), channel_id=1, source_target_pairs={{4,0},{8,4},{12,8},{0,12},{5,1},{9,5},{13,9},{1,13},{6,2},{10,6},{... | collective-permute-start | bytes 147464 | tf_op jit(solution)/shard_map/ppermute | solution.py:25
  19.4 0.0 collective-permute-done.6.refs_4_
  19.4 0.0 collective-permute-done.7.refs_7_
  19.4 0.0 copy-done
  19.4 1.5 %apply_tiles.2 = (f32[384,128]{1,0:T(8,128)}, f32[384,128]{1,0:T(8,128)}, f32[384,128]{1,0:T(8,128)}) custom-call(s32[3,8]{1,0:T(4,128)S(1)} %bitcast.34, bf16[8,384,256]{2,1,0:T(8,128)(2,1)S(1)} %get-tuple-element.35.refs_1_, f32[8,96,128]{2,1,0:T(8,128)S(1)} %get-tuple-element.43.refs_2_, bf16[8,192,128]{2,1,0:T(8,128)(2,1)S(1)} %get-tuple-element.44.refs_3_, ...), custom_call_target="tpu_custom_call" | custom-call | flops 301989888 | bytes 1572864 | tf_op jit(solution)/shard_map/apply_tiles/pallas_call | solution.py:395
  20.9 4.1 %collective-permute-done.2.refs_4_ = f32[48,512]{1,0:T(8,128)S(1)} collective-permute-done((f32[48,512]{1,0:T(8,128)S(1)}, f32[48,512]{1,0:T(8,128)S(1)}, u32[]{:S(2)}, u32[]{:S(2)}) %collective-permute-start.2) | collective-permute-done | bytes 98336 | tf_op jit(solution)/shard_map/ppermute | solution.py:25
  25.0 0.0 collective-permute-done.4.refs_5_
  25.0 0.0 collective-permute-done.5.refs_6_
  25.1 1.2 %apply_tiles.3 = (f32[384,128]{1,0:T(8,128)}, f32[384,128]{1,0:T(8,128)}, f32[384,128]{1,0:T(8,128)}) custom-call(s32[3,8]{1,0:T(4,128)S(1)} %bitcast.35, bf16[8,384,256]{2,1,0:T(8,128)(2,1)S(1)} %get-tuple-element.35.refs_1_, f32[8,48,128]{2,1,0:T(8,128)S(1)} %get-tuple-element.36.refs_2_, ...), custom_call_target="tpu_custom_call", output_to_operand_aliasing={{0}: (7, {}), {1}: (8, {}), {2}: (9, {})} | custom-call | flops 150994944 | bytes 786432 | tf_op jit(solution)/shard_map/apply_tiles/pallas_call | solution.py:395
Async XLA Ops:
  2.1 13.4 %collective-permute-start.3 = (f32[48,512]{1,0:T(8,128)S(1)}, f32[48,512]{1,0:T(8,128)S(1)}, u32[]{:S(2)}, u32[]{:S(2)}) collective-permute-start(f32[48,512]{1,0:T(8,128)S(1)} %get-tuple-element.40), channel_id=1, source_target_pairs={{8,0},{12,4},{0,8},{4,12},{9,1},{13,5},{1,9},{5,13},{10,2},{14,6},... | collective-permute-start | bytes 294920 | tf_op jit(solution)/shard_map/ppermute | solution.py:25
  7.0 12.4 %copy-start = (s32[8,3]{0,1:T(4,128)S(1)}, s32[8,3]{0,1:T(4,128)}, u32[]{:S(2)}) copy-start(s32[8,3]{0,1:T(4,128)} %param.15) | copy-start | bytes 292
  7.0 10.4 %collective-permute-start.1 = (f32[96,256]{1,0:T(8,128)S(1)}, f32[96,256]{1,0:T(8,128)S(1)}, u32[]{:S(2)}, u32[]{:S(2)}) collective-permute-start(f32[96,256]{1,0:T(8,128)S(1)} %get-tuple-element.33), channel_id=1, source_target_pairs={{12,0},{0,4},{4,8},{8,12},{13,1},{1,5},{5,9},{9,13},{14,2},{2,6},{... | collective-permute-start | bytes 294920 | tf_op jit(solution)/shard_map/ppermute | solution.py:25
  8.6 3.3 %collective-permute-start = (f32[48,128]{1,0:T(8,128)S(1)}, f32[48,128]{1,0:T(8,128)S(1)}, u32[]{:S(2)}, u32[]{:S(2)}) collective-permute-start(f32[48,128]{1,0:T(8,128)S(1)} %get-tuple-element.30), channel_id=1, source_target_pairs={{3,0},{0,1},{1,2},{2,3},{7,4},{4,5},{5,6},{6,7},{11,8},{8,9},{9,10... | collective-permute-start | bytes 73736 | tf_op jit(solution)/shard_map/ppermute | solution.py:25
  8.6 10.8 %collective-permute-start.6 = (f32[48,512]{1,0:T(8,128)S(1)}, f32[48,512]{1,0:T(8,128)S(1)}, u32[]{:S(2)}, u32[]{:S(2)}) collective-permute-start(f32[48,512]{1,0:T(8,128)S(1)} %get-tuple-element.45), channel_id=1, source_target_pairs={{8,0},{12,4},{0,8},{4,12},{9,1},{13,5},{1,9},{5,13},{10,2},{14,6},... | collective-permute-start | bytes 294920 | tf_op jit(solution)/shard_map/ppermute | solution.py:25
  9.0 10.4 %collective-permute-start.7 = (f32[96,256]{1,0:T(8,128)S(1)}, f32[96,256]{1,0:T(8,128)S(1)}, u32[]{:S(2)}, u32[]{:S(2)}) collective-permute-start(f32[96,256]{1,0:T(8,128)S(1)} %get-tuple-element.48), channel_id=1, source_target_pairs={{4,0},{8,4},{12,8},{0,12},{5,1},{9,5},{13,9},{1,13},{6,2},{10,6},{... | collective-permute-start | bytes 294920 | tf_op jit(solution)/shard_map/ppermute | solution.py:25
  12.5 12.6 %collective-permute-start.2 = (f32[48,512]{1,0:T(8,128)S(1)}, f32[48,512]{1,0:T(8,128)S(1)}, u32[]{:S(2)}, u32[]{:S(2)}) collective-permute-start(f32[48,512]{1,0:T(8,128)S(1)} %get-tuple-element.38), channel_id=1, source_target_pairs={{8,0},{12,4},{0,8},{4,12},{9,1},{13,5},{1,9},{5,13},{10,2},{14,6},... | collective-permute-start | bytes 294920 | tf_op jit(solution)/shard_map/ppermute | solution.py:25
  15.5 9.5 %collective-permute-start.4 = (f32[48,256]{1,0:T(8,128)S(1)}, f32[48,256]{1,0:T(8,128)S(1)}, u32[]{:S(2)}, u32[]{:S(2)}) collective-permute-start(f32[48,256]{1,0:T(8,128)S(1)} %get-tuple-element.41), channel_id=1, source_target_pairs={{12,0},{0,4},{4,8},{8,12},{13,1},{1,5},{5,9},{9,13},{14,2},{2,6},{... | collective-permute-start | bytes 147464 | tf_op jit(solution)/shard_map/ppermute | solution.py:25
  17.4 7.7 %collective-permute-start.5 = (f32[48,256]{1,0:T(8,128)S(1)}, f32[48,256]{1,0:T(8,128)S(1)}, u32[]{:S(2)}, u32[]{:S(2)}) collective-permute-start(f32[48,256]{1,0:T(8,128)S(1)} %get-tuple-element.42), channel_id=1, source_target_pairs={{4,0},{8,4},{12,8},{0,12},{5,1},{9,5},{13,9},{1,13},{6,2},{10,6},{... | collective-permute-start | bytes 147464 | tf_op jit(solution)/shard_map/ppermute | solution.py:25

commit v9 on v8

--- a/solution.py
+++ b/solution.py
@@ -386,7 +386,7 @@
     sends[1], wide_lead = lax.optimization_barrier((sends[1], wide_lead))
     arrived_late.append(send_to(sends[1], slot_groups[1]))
     for number in range(2, len(sends)):
-        sends[number], narrow_most[0], split_tiles = lax.optimization_barrier((sends[number], narrow_most[0], split_tiles))
+        sends[number], narrow_most[0] = lax.optimization_barrier((sends[number], narrow_most[0]))
         arrived_late.append(send_to(sends[number], slot_groups[number]))
 
     def apply(part, base, parts, transfers, outs):

time: 26.4 us -> 26.9 us (1.019)
  waiting for transfers between devices: 4.9 us -> 5.43 us
    ppermute x8, waiting for transfers between devices: 4.9 us -> 5.43 us  [shift_along(): lax.ppermute(block, axis, [((i - distance) % size, i) for i in range(size)])]
  transfers between devices with their start and end apart: 8 -> 8, of which waited for: 2 -> 3; matrix products, arithmetic and copies ran while one was open for 0% -> 0% of each run, Pallas kernels for 18% -> 18%
where the time goes in v9:
time: 26.9 us; the launch traced here: 26.7 us
  starting transfers between devices  13.2 us (49%)
  Pallas kernels  7.45 us (28%)
  waiting for transfers between devices  5.43 us (20%)
  between operations  0.71 us (3%)
    ppermute x8, starting transfers between devices, shift_along(): lax.ppermute(block, axis, [((i - distance) % size, i) for i in range(size)])  13.2 us
    ppermute x8, waiting for transfers between devices, shift_along(): lax.ppermute(block, axis, [((i - distance) % size, i) for i in range(size)])  5.43 us
    pallas_call x2, Pallas kernels, apply(): pl.pallas_call(functools.partial(apply_kernel, part, received, cell_block...  2.68 us
    pallas_call x1, Pallas kernels, per_device(): pl.pallas_call(functools.partial(local_kernel, (most, late), cell_blocks)...  1.94 us
    pallas_call x1, Pallas kernels, per_device(): pl.pallas_call(functools.partial(first_kernel, lead, wide, cell_blocks),...  1.44 us
    pallas_call x1, Pallas kernels, per_device(): pl.pallas_call(functools.partial(second_kernel, most, middle, wide, other...  0.81 us
    pallas_call x1, Pallas kernels, per_device(): pl.pallas_call(functools.partial(third_kernel, late, wide, others, cell_b...  0.57 us
  transfers between devices with their start and end apart: 8, of which 3 were waited for; matrix products, arithmetic and copies ran while one was open for 0% of the time, Pallas kernels for 18%

profile of v9, /device:TPU:0, one launch (start us, length us, event | category | flops | bytes accessed | tf_op | source)
XLA Modules:
  0.0 26.7 jit_solution(2449450598273179507)
XLA Ops:
  0.6 1.4 %gather_first.1 = (f32[48,512]{1,0:T(8,128)S(1)}, f32[3,384,128]{2,1,0:T(8,128)S(1)}, s32[4,256]{1,0:T(4,128)S(1)}, f32[48,128]{1,0:T(8,128)S(1)}) custom-call(f32[384,128]{1,0:T(8,128)} %bitcast.39, f32[384,128]{1,0:T(8,128)} %bitcast.40, f32[384,128]{1,0:T(8,128)} %bitcast.41, s32[4,256]{1,0:T(4,128)} %bitcast.42, s32[1,4]{1,0:T(1,128)} %refs_4_.1), custom_call_target="tpu_custom_call" | custom-call | flops 100663296 | bytes 1179648 | tf_op jit(solution)/shard_map/gather_first/pallas_call | solution.py:322
  2.1 4.1 %collective-permute-start.2 = (f32[48,512]{1,0:T(8,128)S(1)}, f32[48,512]{1,0:T(8,128)S(1)}, u32[]{:S(2)}, u32[]{:S(2)}) collective-permute-start(f32[48,512]{1,0:T(8,128)S(1)} %get-tuple-element.36), channel_id=1, source_target_pairs={{8,0},{12,4},{0,8},{4,12},{9,1},{13,5},{1,9},{5,13},{10,2},{14,6},... | collective-permute-start | bytes 294920 | tf_op jit(solution)/shard_map/ppermute | solution.py:25
  6.2 0.8 %gather_second.1 = (f32[48,512]{1,0:T(8,128)S(1)}, f32[96,256]{1,0:T(8,128)S(1)}, f32[96,256]{1,0:T(8,128)S(1)}, bf16[8,192,128]{2,1,0:T(8,128)(2,1)S(1)}) custom-call(f32[3,384,128]{2,1,0:T(8,128)S(1)} %get-tuple-element.28.held, s32[4,256]{1,0:T(4,128)S(1)} %get-tuple-element.32.listed), custom_call_target="tpu_custom_call" | custom-call | flops 402653184 | bytes 1179648 | tf_op jit(solution)/shard_map/gather_second/pallas_call | solution.py:342
  7.0 0.0 copy-start
  7.0 1.6 %collective-permute-start.4 = (f32[96,256]{1,0:T(8,128)S(1)}, f32[96,256]{1,0:T(8,128)S(1)}, u32[]{:S(2)}, u32[]{:S(2)}) collective-permute-start(f32[96,256]{1,0:T(8,128)S(1)} %get-tuple-element.39), channel_id=1, source_target_pairs={{12,0},{0,4},{4,8},{8,12},{13,1},{1,5},{5,9},{9,13},{14,2},{2,6},{... | collective-permute-start | bytes 294920 | tf_op jit(solution)/shard_map/ppermute | solution.py:25
  8.6 0.0 collective-permute-start
  8.6 0.3 %collective-permute-start.6 = (f32[48,512]{1,0:T(8,128)S(1)}, f32[48,512]{1,0:T(8,128)S(1)}, u32[]{:S(2)}, u32[]{:S(2)}) collective-permute-start(f32[48,512]{1,0:T(8,128)S(1)} %get-tuple-element.43), channel_id=1, source_target_pairs={{8,0},{12,4},{0,8},{4,12},{9,1},{13,5},{1,9},{5,13},{10,2},{14,6},... | collective-permute-start | bytes 294920 | tf_op jit(solution)/shard_map/ppermute | solution.py:25
  9.0 2.2 %collective-permute-start.7 = (f32[96,256]{1,0:T(8,128)S(1)}, f32[96,256]{1,0:T(8,128)S(1)}, u32[]{:S(2)}, u32[]{:S(2)}) collective-permute-start(f32[96,256]{1,0:T(8,128)S(1)} %get-tuple-element.46), channel_id=1, source_target_pairs={{4,0},{8,4},{12,8},{0,12},{5,1},{9,5},{13,9},{1,13},{6,2},{10,6},{... | collective-permute-start | bytes 294920 | tf_op jit(solution)/shard_map/ppermute | solution.py:25
  11.2 0.7 %collective-permute-done.prev = f32[48,128]{1,0:T(8,128)S(1)} collective-permute-done((f32[48,128]{1,0:T(8,128)S(1)}, f32[48,128]{1,0:T(8,128)S(1)}, u32[]{:S(2)}, u32[]{:S(2)}) %collective-permute-start) | collective-permute-done | bytes 24608 | tf_op jit(solution)/shard_map/ppermute | solution.py:25
  11.9 0.6 %gather_third.1 = (f32[48,512]{1,0:T(8,128)S(1)}, f32[48,256]{1,0:T(8,128)S(1)}, f32[48,256]{1,0:T(8,128)S(1)}, bf16[8,96,128]{2,1,0:T(8,128)(2,1)S(1)}) custom-call(f32[3,384,128]{2,1,0:T(8,128)S(1)} %get-tuple-element.28.held, f32[48,128]{1,0:T(8,128)S(1)} %collective-permute-done.prev, s32[4,256]{1,0:T(4,128)S(1)} %get-tuple-element.32.listed), custom_call_target="tpu_custom_call" | custom-call | flops 201326592 | bytes 1179648 | tf_op jit(solution)/shard_map/gather_third/pallas_call | solution.py:355
  12.5 1.1 %collective-permute-start.1 = (f32[48,512]{1,0:T(8,128)S(1)}, f32[48,512]{1,0:T(8,128)S(1)}, u32[]{:S(2)}, u32[]{:S(2)}) collective-permute-start(f32[48,512]{1,0:T(8,128)S(1)} %get-tuple-element.34), channel_id=1, source_target_pairs={{8,0},{12,4},{0,8},{4,12},{9,1},{13,5},{1,9},{5,13},{10,2},{14,6},... | collective-permute-start | bytes 294920 | tf_op jit(solution)/shard_map/ppermute | solution.py:25
  13.6 0.0 collective-permute-done.2.refs_5_
  13.6 1.8 %collective-permute-start.3 = (f32[48,256]{1,0:T(8,128)S(1)}, f32[48,256]{1,0:T(8,128)S(1)}, u32[]{:S(2)}, u32[]{:S(2)}) collective-permute-start(f32[48,256]{1,0:T(8,128)S(1)} %get-tuple-element.37), channel_id=1, source_target_pairs={{12,0},{0,4},{4,8},{8,12},{13,1},{1,5},{5,9},{9,13},{14,2},{2,6},{... | collective-permute-start | bytes 147464 | tf_op jit(solution)/shard_map/ppermute | solution.py:25
  15.4 0.0 collective-permute-done.4.refs_6_
  15.4 2.0 %collective-permute-start.5 = (f32[48,256]{1,0:T(8,128)S(1)}, f32[48,256]{1,0:T(8,128)S(1)}, u32[]{:S(2)}, u32[]{:S(2)}) collective-permute-start(f32[48,256]{1,0:T(8,128)S(1)} %get-tuple-element.40), channel_id=1, source_target_pairs={{4,0},{8,4},{12,8},{0,12},{5,1},{9,5},{13,9},{1,13},{6,2},{10,6},{... | collective-permute-start | bytes 147464 | tf_op jit(solution)/shard_map/ppermute | solution.py:25
  17.4 1.9 %local_terms.1 = (f32[8,96,128]{2,1,0:T(8,128)S(1)}, f32[8,48,128]{2,1,0:T(8,128)S(1)}, bf16[8,384,256]{2,1,0:T(8,128)(2,1)S(1)}) custom-call(f32[3,384,128]{2,1,0:T(8,128)S(1)} %get-tuple-element.28.held, f32[48,128]{1,0:T(8,128)S(1)} %collective-permute-done.prev, f32[8,128]{1,0:T(8,128)} %bitcast.43, f32[8,128]{1,0:T(8,128)} %bitcast.44, ...), custom_call_target="tpu_custom_call" | custom-call | flops 8847360 | bytes 3145728 | tf_op jit(solution)/shard_map/local_terms/pallas_call | solution.py:365
  19.4 0.0 collective-permute-done.6.refs_4_
  19.4 0.0 collective-permute-done.7.refs_7_
  19.4 0.0 copy-done
  19.4 1.5 %apply_tiles.2 = (f32[384,128]{1,0:T(8,128)}, f32[384,128]{1,0:T(8,128)}, f32[384,128]{1,0:T(8,128)}) custom-call(s32[3,8]{1,0:T(4,128)S(1)} %bitcast.34, bf16[8,384,256]{2,1,0:T(8,128)(2,1)S(1)} %get-tuple-element.30.refs_1_, f32[8,96,128]{2,1,0:T(8,128)S(1)} %get-tuple-element.41.refs_2_, bf16[8,192,128]{2,1,0:T(8,128)(2,1)S(1)} %get-tuple-element.42.refs_3_, ...), custom_call_target="tpu_custom_call" | custom-call | flops 301989888 | bytes 1572864 | tf_op jit(solution)/shard_map/apply_tiles/pallas_call | solution.py:395
  20.9 4.3 %collective-permute-done.1.refs_4_ = f32[48,512]{1,0:T(8,128)S(1)} collective-permute-done((f32[48,512]{1,0:T(8,128)S(1)}, f32[48,512]{1,0:T(8,128)S(1)}, u32[]{:S(2)}, u32[]{:S(2)}) %collective-permute-start.1) | collective-permute-done | bytes 98336 | tf_op jit(solution)/shard_map/ppermute | solution.py:25
  25.1 0.0 collective-permute-done.3.refs_5_
  25.1 0.4 %collective-permute-done.5.refs_6_ = f32[48,256]{1,0:T(8,128)S(1)} collective-permute-done((f32[48,256]{1,0:T(8,128)S(1)}, f32[48,256]{1,0:T(8,128)S(1)}, u32[]{:S(2)}, u32[]{:S(2)}) %collective-permute-start.5) | collective-permute-done | bytes 49184 | tf_op jit(solution)/shard_map/ppermute | solution.py:25
  25.5 1.2 %apply_tiles.3 = (f32[384,128]{1,0:T(8,128)}, f32[384,128]{1,0:T(8,128)}, f32[384,128]{1,0:T(8,128)}) custom-call(s32[3,8]{1,0:T(4,128)S(1)} %bitcast.35, bf16[8,384,256]{2,1,0:T(8,128)(2,1)S(1)} %get-tuple-element.30.refs_1_, f32[8,48,128]{2,1,0:T(8,128)S(1)} %get-tuple-element.31.refs_2_, ...), custom_call_target="tpu_custom_call", output_to_operand_aliasing={{0}: (7, {}), {1}: (8, {}), {2}: (9, {})} | custom-call | flops 150994944 | bytes 786432 | tf_op jit(solution)/shard_map/apply_tiles/pallas_call | solution.py:395
Async XLA Ops:
  2.1 11.5 %collective-permute-start.2 = (f32[48,512]{1,0:T(8,128)S(1)}, f32[48,512]{1,0:T(8,128)S(1)}, u32[]{:S(2)}, u32[]{:S(2)}) collective-permute-start(f32[48,512]{1,0:T(8,128)S(1)} %get-tuple-element.36), channel_id=1, source_target_pairs={{8,0},{12,4},{0,8},{4,12},{9,1},{13,5},{1,9},{5,13},{10,2},{14,6},... | collective-permute-start | bytes 294920 | tf_op jit(solution)/shard_map/ppermute | solution.py:25
  7.0 12.4 %copy-start = (s32[8,3]{0,1:T(4,128)S(1)}, s32[8,3]{0,1:T(4,128)}, u32[]{:S(2)}) copy-start(s32[8,3]{0,1:T(4,128)} %param.15) | copy-start | bytes 292
  7.0 8.3 %collective-permute-start.4 = (f32[96,256]{1,0:T(8,128)S(1)}, f32[96,256]{1,0:T(8,128)S(1)}, u32[]{:S(2)}, u32[]{:S(2)}) collective-permute-start(f32[96,256]{1,0:T(8,128)S(1)} %get-tuple-element.39), channel_id=1, source_target_pairs={{12,0},{0,4},{4,8},{8,12},{13,1},{1,5},{5,9},{9,13},{14,2},{2,6},{... | collective-permute-start | bytes 294920 | tf_op jit(solution)/shard_map/ppermute | solution.py:25
  8.6 3.3 %collective-permute-start = (f32[48,128]{1,0:T(8,128)S(1)}, f32[48,128]{1,0:T(8,128)S(1)}, u32[]{:S(2)}, u32[]{:S(2)}) collective-permute-start(f32[48,128]{1,0:T(8,128)S(1)} %get-tuple-element.29), channel_id=1, source_target_pairs={{3,0},{0,1},{1,2},{2,3},{7,4},{4,5},{5,6},{6,7},{11,8},{8,9},{9,10... | collective-permute-start | bytes 73736 | tf_op jit(solution)/shard_map/ppermute | solution.py:25
  8.6 10.7 %collective-permute-start.6 = (f32[48,512]{1,0:T(8,128)S(1)}, f32[48,512]{1,0:T(8,128)S(1)}, u32[]{:S(2)}, u32[]{:S(2)}) collective-permute-start(f32[48,512]{1,0:T(8,128)S(1)} %get-tuple-element.43), channel_id=1, source_target_pairs={{8,0},{12,4},{0,8},{4,12},{9,1},{13,5},{1,9},{5,13},{10,2},{14,6},... | collective-permute-start | bytes 294920 | tf_op jit(solution)/shard_map/ppermute | solution.py:25
  9.0 10.4 %collective-permute-start.7 = (f32[96,256]{1,0:T(8,128)S(1)}, f32[96,256]{1,0:T(8,128)S(1)}, u32[]{:S(2)}, u32[]{:S(2)}) collective-permute-start(f32[96,256]{1,0:T(8,128)S(1)} %get-tuple-element.46), channel_id=1, source_target_pairs={{4,0},{8,4},{12,8},{0,12},{5,1},{9,5},{13,9},{1,13},{6,2},{10,6},{... | collective-permute-start | bytes 294920 | tf_op jit(solution)/shard_map/ppermute | solution.py:25
  12.5 12.7 %collective-permute-start.1 = (f32[48,512]{1,0:T(8,128)S(1)}, f32[48,512]{1,0:T(8,128)S(1)}, u32[]{:S(2)}, u32[]{:S(2)}) collective-permute-start(f32[48,512]{1,0:T(8,128)S(1)} %get-tuple-element.34), channel_id=1, source_target_pairs={{8,0},{12,4},{0,8},{4,12},{9,1},{13,5},{1,9},{5,13},{10,2},{14,6},... | collective-permute-start | bytes 294920 | tf_op jit(solution)/shard_map/ppermute | solution.py:25
  13.6 11.6 %collective-permute-start.3 = (f32[48,256]{1,0:T(8,128)S(1)}, f32[48,256]{1,0:T(8,128)S(1)}, u32[]{:S(2)}, u32[]{:S(2)}) collective-permute-start(f32[48,256]{1,0:T(8,128)S(1)} %get-tuple-element.37), channel_id=1, source_target_pairs={{12,0},{0,4},{4,8},{8,12},{13,1},{1,5},{5,9},{9,13},{14,2},{2,6},{... | collective-permute-start | bytes 147464 | tf_op jit(solution)/shard_map/ppermute | solution.py:25
  15.4 10.2 %collective-permute-start.5 = (f32[48,256]{1,0:T(8,128)S(1)}, f32[48,256]{1,0:T(8,128)S(1)}, u32[]{:S(2)}, u32[]{:S(2)}) collective-permute-start(f32[48,256]{1,0:T(8,128)S(1)} %get-tuple-element.40), channel_id=1, source_target_pairs={{4,0},{8,4},{12,8},{0,12},{5,1},{9,5},{13,9},{1,13},{6,2},{10,6},{... | collective-permute-start | bytes 147464 | tf_op jit(solution)/shard_map/ppermute | solution.py:25

commit v10 on v9

--- a/solution.py
+++ b/solution.py
@@ -351,7 +351,8 @@
     )(held, listed)
     wide_middle = send_to(send, wide)
     prev = shift_along(last, "tm", 1)
-    narrow_most = [send_to(part, slots) for part, slots in zip(sends, narrow)]
+    narrow_sends = sends
+    narrow_most = [send_to(narrow_sends[0], narrow[0])]
     *sends, late_parts = pl.pallas_call(
         functools.partial(third_kernel, late, wide, others, cell_blocks),
         out_shape=sends_of(late, slot_groups) + [parts_of(late)],
@@ -383,7 +384,10 @@
     )(held, prev, *in_hbm(feed, kill, tiles))
 
     arrived_late = [send_to(sends[0], wide)]
-    sends[1], wide_lead = lax.optimization_barrier((sends[1], wide_lead))
+    for part, slots in zip(narrow_sends[1:], narrow[1:]):
+        part, wide_lead = lax.optimization_barrier((part, wide_lead))
+        narrow_most.append(send_to(part, slots))
+    sends[1], split_tiles = lax.optimization_barrier((sends[1], split_tiles))
     arrived_late.append(send_to(sends[1], slot_groups[1]))
     for number in range(2, len(sends)):
         sends[number], narrow_most[0] = lax.optimization_barrier((sends[number], narrow_most[0]))

time: 26.9 us -> 27 us (level)
  starting transfers between devices: 13.2 us -> 13.7 us
  waiting for transfers between devices: 5.43 us -> 4.98 us
    ppermute x8, starting transfers between devices: 13.2 us -> 13.7 us  [shift_along(): lax.ppermute(block, axis, [((i - distance) % size, i) for i in range(size)])]
    ppermute x8, waiting for transfers between devices: 5.43 us -> 4.98 us  [shift_along(): lax.ppermute(block, axis, [((i - distance) % size, i) for i in range(size)])]
  transfers between devices with their start and end apart: 8 -> 8, of which waited for: 3 -> 4; matrix products, arithmetic and copies ran while one was open for 0% -> 0% of each run, Pallas kernels for 18% -> 18%
where the time goes in v10:
time: 27 us; the launch traced here: 26.8 us
  starting transfers between devices  13.7 us (51%)
  Pallas kernels  7.46 us (28%)
  waiting for transfers between devices  4.98 us (18%)
  between operations  0.7 us (3%)
    ppermute x8, starting transfers between devices, shift_along(): lax.ppermute(block, axis, [((i - distance) % size, i) for i in range(size)])  13.7 us
    ppermute x8, waiting for transfers between devices, shift_along(): lax.ppermute(block, axis, [((i - distance) % size, i) for i in range(size)])  4.98 us
    pallas_call x2, Pallas kernels, apply(): pl.pallas_call(functools.partial(apply_kernel, part, received, cell_block...  2.68 us
    pallas_call x1, Pallas kernels, per_device(): pl.pallas_call(functools.partial(local_kernel, (most, late), cell_blocks)...  1.95 us
    pallas_call x1, Pallas kernels, per_device(): pl.pallas_call(functools.partial(first_kernel, lead, wide, cell_blocks),...  1.44 us
    pallas_call x1, Pallas kernels, per_device(): pl.pallas_call(functools.partial(second_kernel, most, middle, wide, other...  0.81 us
    pallas_call x1, Pallas kernels, per_device(): pl.pallas_call(functools.partial(third_kernel, late, wide, others, cell_b...  0.58 us
  transfers between devices with their start and end apart: 8, of which 4 were waited for; matrix products, arithmetic and copies ran while one was open for 0% of the time, Pallas kernels for 18%

profile of v10, /device:TPU:0, one launch (start us, length us, event | category | flops | bytes accessed | tf_op | source)
XLA Modules:
  0.0 26.8 jit_solution(12957569130489987487)
XLA Ops:
  0.6 1.4 %gather_first.1 = (f32[48,512]{1,0:T(8,128)S(1)}, f32[3,384,128]{2,1,0:T(8,128)S(1)}, s32[4,256]{1,0:T(4,128)S(1)}, f32[48,128]{1,0:T(8,128)S(1)}) custom-call(f32[384,128]{1,0:T(8,128)} %bitcast.39, f32[384,128]{1,0:T(8,128)} %bitcast.40, f32[384,128]{1,0:T(8,128)} %bitcast.41, s32[4,256]{1,0:T(4,128)} %bitcast.42, s32[1,4]{1,0:T(1,128)} %refs_4_.1), custom_call_target="tpu_custom_call" | custom-call | flops 100663296 | bytes 1179648 | tf_op jit(solution)/shard_map/gather_first/pallas_call | solution.py:322
  2.1 4.1 %collective-permute-start.6 = (f32[48,512]{1,0:T(8,128)S(1)}, f32[48,512]{1,0:T(8,128)S(1)}, u32[]{:S(2)}, u32[]{:S(2)}) collective-permute-start(f32[48,512]{1,0:T(8,128)S(1)} %get-tuple-element.47), channel_id=1, source_target_pairs={{8,0},{12,4},{0,8},{4,12},{9,1},{13,5},{1,9},{5,13},{10,2},{14,6},... | collective-permute-start | bytes 294920 | tf_op jit(solution)/shard_map/ppermute | solution.py:25
  6.2 0.8 %gather_second.1 = (f32[48,512]{1,0:T(8,128)S(1)}, f32[96,256]{1,0:T(8,128)S(1)}, f32[96,256]{1,0:T(8,128)S(1)}, bf16[8,192,128]{2,1,0:T(8,128)(2,1)S(1)}) custom-call(f32[3,384,128]{2,1,0:T(8,128)S(1)} %get-tuple-element.30.held, s32[4,256]{1,0:T(4,128)S(1)} %get-tuple-element.32.listed), custom_call_target="tpu_custom_call" | custom-call | flops 402653184 | bytes 1179648 | tf_op jit(solution)/shard_map/gather_second/pallas_call | solution.py:342
  7.0 0.0 copy-start
  7.0 1.6 %collective-permute-start.3 = (f32[96,256]{1,0:T(8,128)S(1)}, f32[96,256]{1,0:T(8,128)S(1)}, u32[]{:S(2)}, u32[]{:S(2)}) collective-permute-start(f32[96,256]{1,0:T(8,128)S(1)} %get-tuple-element.41), channel_id=1, source_target_pairs={{12,0},{0,4},{4,8},{8,12},{13,1},{1,5},{5,9},{9,13},{14,2},{2,6},{... | collective-permute-start | bytes 294920 | tf_op jit(solution)/shard_map/ppermute | solution.py:25
  8.6 0.0 collective-permute-start
  8.6 0.3 %collective-permute-start.5 = (f32[48,512]{1,0:T(8,128)S(1)}, f32[48,512]{1,0:T(8,128)S(1)}, u32[]{:S(2)}, u32[]{:S(2)}) collective-permute-start(f32[48,512]{1,0:T(8,128)S(1)} %get-tuple-element.45), channel_id=1, source_target_pairs={{8,0},{12,4},{0,8},{4,12},{9,1},{13,5},{1,9},{5,13},{10,2},{14,6},... | collective-permute-start | bytes 294920 | tf_op jit(solution)/shard_map/ppermute | solution.py:25
  9.0 2.1 %collective-permute-done.6.refs_5_ = f32[48,512]{1,0:T(8,128)S(1)} collective-permute-done((f32[48,512]{1,0:T(8,128)S(1)}, f32[48,512]{1,0:T(8,128)S(1)}, u32[]{:S(2)}, u32[]{:S(2)}) %collective-permute-start.6) | collective-permute-done | bytes 98336 | tf_op jit(solution)/shard_map/ppermute | solution.py:25
  11.1 3.7 %collective-permute-start.7 = (f32[96,256]{1,0:T(8,128)S(1)}, f32[96,256]{1,0:T(8,128)S(1)}, u32[]{:S(2)}, u32[]{:S(2)}) collective-permute-start(f32[96,256]{1,0:T(8,128)S(1)} %get-tuple-element.50), channel_id=1, source_target_pairs={{4,0},{8,4},{12,8},{0,12},{5,1},{9,5},{13,9},{1,13},{6,2},{10,6},{... | collective-permute-start | bytes 294920 | tf_op jit(solution)/shard_map/ppermute | solution.py:25
  14.8 0.0 collective-permute-done.prev
  14.8 0.6 %gather_third.1 = (f32[48,512]{1,0:T(8,128)S(1)}, f32[48,256]{1,0:T(8,128)S(1)}, f32[48,256]{1,0:T(8,128)S(1)}, bf16[8,96,128]{2,1,0:T(8,128)(2,1)S(1)}) custom-call(f32[3,384,128]{2,1,0:T(8,128)S(1)} %get-tuple-element.30.held, f32[48,128]{1,0:T(8,128)S(1)} %collective-permute-done.prev, s32[4,256]{1,0:T(4,128)S(1)} %get-tuple-element.32.listed), custom_call_target="tpu_custom_call" | custom-call | flops 201326592 | bytes 1179648 | tf_op jit(solution)/shard_map/gather_third/pallas_call | solution.py:356
  15.4 0.1 collective-permute-start.1
  15.4 1.9 %local_terms.1 = (f32[8,96,128]{2,1,0:T(8,128)S(1)}, f32[8,48,128]{2,1,0:T(8,128)S(1)}, bf16[8,384,256]{2,1,0:T(8,128)(2,1)S(1)}) custom-call(f32[3,384,128]{2,1,0:T(8,128)S(1)} %get-tuple-element.30.held, f32[48,128]{1,0:T(8,128)S(1)} %collective-permute-done.prev, f32[8,128]{1,0:T(8,128)} %bitcast.43, f32[8,128]{1,0:T(8,128)} %bitcast.44, ...), custom_call_target="tpu_custom_call" | custom-call | flops 8847360 | bytes 3145728 | tf_op jit(solution)/shard_map/local_terms/pallas_call | solution.py:366
  17.4 0.6 %collective-permute-start.2 = (f32[48,256]{1,0:T(8,128)S(1)}, f32[48,256]{1,0:T(8,128)S(1)}, u32[]{:S(2)}, u32[]{:S(2)}) collective-permute-start(f32[48,256]{1,0:T(8,128)S(1)} %get-tuple-element.39), channel_id=1, source_target_pairs={{12,0},{0,4},{4,8},{8,12},{13,1},{1,5},{5,9},{9,13},{14,2},{2,6},{... | collective-permute-start | bytes 147464 | tf_op jit(solution)/shard_map/ppermute | solution.py:25
  18.0 0.0 collective-permute-done.3.refs_6_
  18.0 3.3 %collective-permute-start.4 = (f32[48,256]{1,0:T(8,128)S(1)}, f32[48,256]{1,0:T(8,128)S(1)}, u32[]{:S(2)}, u32[]{:S(2)}) collective-permute-start(f32[48,256]{1,0:T(8,128)S(1)} %get-tuple-element.42), channel_id=1, source_target_pairs={{4,0},{8,4},{12,8},{0,12},{5,1},{9,5},{13,9},{1,13},{6,2},{10,6},{... | collective-permute-start | bytes 147464 | tf_op jit(solution)/shard_map/ppermute | solution.py:25
  21.3 0.0 collective-permute-done.5.refs_4_
  21.3 0.0 collective-permute-done.7.refs_7_
  21.3 0.0 copy-done
  21.3 1.5 %apply_tiles.2 = (f32[384,128]{1,0:T(8,128)}, f32[384,128]{1,0:T(8,128)}, f32[384,128]{1,0:T(8,128)}) custom-call(s32[3,8]{1,0:T(4,128)S(1)} %bitcast.34, bf16[8,384,256]{2,1,0:T(8,128)(2,1)S(1)} %get-tuple-element.35.refs_1_, f32[8,96,128]{2,1,0:T(8,128)S(1)} %get-tuple-element.43.refs_2_, bf16[8,192,128]{2,1,0:T(8,128)(2,1)S(1)} %get-tuple-element.44.refs_3_, ...), custom_call_target="tpu_custom_call" | custom-call | flops 301989888 | bytes 1572864 | tf_op jit(solution)/shard_map/apply_tiles/pallas_call | solution.py:399
  22.8 0.8 %collective-permute-done.2.refs_5_ = f32[48,256]{1,0:T(8,128)S(1)} collective-permute-done((f32[48,256]{1,0:T(8,128)S(1)}, f32[48,256]{1,0:T(8,128)S(1)}, u32[]{:S(2)}, u32[]{:S(2)}) %collective-permute-start.2) | collective-permute-done | bytes 49184 | tf_op jit(solution)/shard_map/ppermute | solution.py:25
  23.5 1.7 %collective-permute-done.1.refs_4_ = f32[48,512]{1,0:T(8,128)S(1)} collective-permute-done((f32[48,512]{1,0:T(8,128)S(1)}, f32[48,512]{1,0:T(8,128)S(1)}, u32[]{:S(2)}, u32[]{:S(2)}) %collective-permute-start.1) | collective-permute-done | bytes 98336 | tf_op jit(solution)/shard_map/ppermute | solution.py:25
  25.2 0.4 %collective-permute-done.4.refs_6_ = f32[48,256]{1,0:T(8,128)S(1)} collective-permute-done((f32[48,256]{1,0:T(8,128)S(1)}, f32[48,256]{1,0:T(8,128)S(1)}, u32[]{:S(2)}, u32[]{:S(2)}) %collective-permute-start.4) | collective-permute-done | bytes 49184 | tf_op jit(solution)/shard_map/ppermute | solution.py:25
  25.6 1.2 %apply_tiles.3 = (f32[384,128]{1,0:T(8,128)}, f32[384,128]{1,0:T(8,128)}, f32[384,128]{1,0:T(8,128)}) custom-call(s32[3,8]{1,0:T(4,128)S(1)} %bitcast.35, bf16[8,384,256]{2,1,0:T(8,128)(2,1)S(1)} %get-tuple-element.35.refs_1_, f32[8,48,128]{2,1,0:T(8,128)S(1)} %get-tuple-element.36.refs_2_, ...), custom_call_target="tpu_custom_call", output_to_operand_aliasing={{0}: (7, {}), {1}: (8, {}), {2}: (9, {})} | custom-call | flops 150994944 | bytes 786432 | tf_op jit(solution)/shard_map/apply_tiles/pallas_call | solution.py:399
Async XLA Ops:
  2.1 9.0 %collective-permute-start.6 = (f32[48,512]{1,0:T(8,128)S(1)}, f32[48,512]{1,0:T(8,128)S(1)}, u32[]{:S(2)}, u32[]{:S(2)}) collective-permute-start(f32[48,512]{1,0:T(8,128)S(1)} %get-tuple-element.47), channel_id=1, source_target_pairs={{8,0},{12,4},{0,8},{4,12},{9,1},{13,5},{1,9},{5,13},{10,2},{14,6},... | collective-permute-start | bytes 294920 | tf_op jit(solution)/shard_map/ppermute | solution.py:25
  7.0 14.3 %copy-start = (s32[8,3]{0,1:T(4,128)S(1)}, s32[8,3]{0,1:T(4,128)}, u32[]{:S(2)}) copy-start(s32[8,3]{0,1:T(4,128)} %param.15) | copy-start | bytes 292
  7.0 11.0 %collective-permute-start.3 = (f32[96,256]{1,0:T(8,128)S(1)}, f32[96,256]{1,0:T(8,128)S(1)}, u32[]{:S(2)}, u32[]{:S(2)}) collective-permute-start(f32[96,256]{1,0:T(8,128)S(1)} %get-tuple-element.41), channel_id=1, source_target_pairs={{12,0},{0,4},{4,8},{8,12},{13,1},{1,5},{5,9},{9,13},{14,2},{2,6},{... | collective-permute-start | bytes 294920 | tf_op jit(solution)/shard_map/ppermute | solution.py:25
  8.6 6.1 %collective-permute-start = (f32[48,128]{1,0:T(8,128)S(1)}, f32[48,128]{1,0:T(8,128)S(1)}, u32[]{:S(2)}, u32[]{:S(2)}) collective-permute-start(f32[48,128]{1,0:T(8,128)S(1)} %get-tuple-element.31), channel_id=1, source_target_pairs={{3,0},{0,1},{1,2},{2,3},{7,4},{4,5},{5,6},{6,7},{11,8},{8,9},{9,10... | collective-permute-start | bytes 73736 | tf_op jit(solution)/shard_map/ppermute | solution.py:25
  8.6 12.6 %collective-permute-start.5 = (f32[48,512]{1,0:T(8,128)S(1)}, f32[48,512]{1,0:T(8,128)S(1)}, u32[]{:S(2)}, u32[]{:S(2)}) collective-permute-start(f32[48,512]{1,0:T(8,128)S(1)} %get-tuple-element.45), channel_id=1, source_target_pairs={{8,0},{12,4},{0,8},{4,12},{9,1},{13,5},{1,9},{5,13},{10,2},{14,6},... | collective-permute-start | bytes 294920 | tf_op jit(solution)/shard_map/ppermute | solution.py:25
  11.1 10.2 %collective-permute-start.7 = (f32[96,256]{1,0:T(8,128)S(1)}, f32[96,256]{1,0:T(8,128)S(1)}, u32[]{:S(2)}, u32[]{:S(2)}) collective-permute-start(f32[96,256]{1,0:T(8,128)S(1)} %get-tuple-element.50), channel_id=1, source_target_pairs={{4,0},{8,4},{12,8},{0,12},{5,1},{9,5},{13,9},{1,13},{6,2},{10,6},{... | collective-permute-start | bytes 294920 | tf_op jit(solution)/shard_map/ppermute | solution.py:25
  15.4 9.8 %collective-permute-start.1 = (f32[48,512]{1,0:T(8,128)S(1)}, f32[48,512]{1,0:T(8,128)S(1)}, u32[]{:S(2)}, u32[]{:S(2)}) collective-permute-start(f32[48,512]{1,0:T(8,128)S(1)} %get-tuple-element.38), channel_id=1, source_target_pairs={{8,0},{12,4},{0,8},{4,12},{9,1},{13,5},{1,9},{5,13},{10,2},{14,6},... | collective-permute-start | bytes 294920 | tf_op jit(solution)/shard_map/ppermute | solution.py:25
  17.4 6.1 %collective-permute-start.2 = (f32[48,256]{1,0:T(8,128)S(1)}, f32[48,256]{1,0:T(8,128)S(1)}, u32[]{:S(2)}, u32[]{:S(2)}) collective-permute-start(f32[48,256]{1,0:T(8,128)S(1)} %get-tuple-element.39), channel_id=1, source_target_pairs={{12,0},{0,4},{4,8},{8,12},{13,1},{1,5},{5,9},{9,13},{14,2},{2,6},{... | collective-permute-start | bytes 147464 | tf_op jit(solution)/shard_map/ppermute | solution.py:25
  18.0 7.6 %collective-permute-start.4 = (f32[48,256]{1,0:T(8,128)S(1)}, f32[48,256]{1,0:T(8,128)S(1)}, u32[]{:S(2)}, u32[]{:S(2)}) collective-permute-start(f32[48,256]{1,0:T(8,128)S(1)} %get-tuple-element.42), channel_id=1, source_target_pairs={{4,0},{8,4},{12,8},{0,12},{5,1},{9,5},{13,9},{1,13},{6,2},{10,6},{... | collective-permute-start | bytes 147464 | tf_op jit(solution)/shard_map/ppermute | solution.py:25

commit v11 on v8

--- a/solution.py
+++ b/solution.py
@@ -118,31 +118,28 @@
     for copy in small:
         copy.wait()
     lane = lax.broadcasted_iota(jnp.int32, rows_ref.shape, 1)
+    columns = {}
     for slot in range(rows_ref.shape[0]):
-        listed[slot : slot + 1, :] = jnp.where(
-            lane[slot : slot + 1] < count_ref[:, slot : slot + 1], rows_ref[slot : slot + 1, :], -1
-        )
-    for copy in needed:
-        copy.wait()
-    columns = [
-        listed[slot : slot + 1, start : start + LANES]
-        for slot in slots
-        for start in range(0, listed.shape[1], LANES)
-    ]
-    columns = [jnp.broadcast_to(column, (STEPS, LANES)) for column in columns]
-    for place, group in enumerate(lead):
-        for field in range(FIELDS):
+        live = lane[slot : slot + 1] < count_ref[:, slot : slot + 1]
+        row = jnp.where(live, rows_ref[slot : slot + 1, :], -1)
+        listed[slot : slot + 1, :] = row
+        columns[slot] = [row[:, start : start + LANES] for start in range(0, row.shape[1], LANES)]
+    columns = [jnp.broadcast_to(column, (STEPS, LANES)) for slot in slots for column in columns[slot]]
+    lanes = [column & (LANES - 1) for column in columns]
+    blocks = [column >> 7 for column in columns]
+    for field in range(FIELDS):
+        needed[field].wait()
+        for place, group in enumerate(lead):
             for species in range(2):
                 row = ((place * FIELDS + field) * 2 + species) * STEPS
                 sums = [
                     scaled_sum(held.at[field], None, field, group, block, species, stride) for block in range(cell_blocks)
                 ]
-                for number, column in enumerate(columns):
-                    lanes = column & (LANES - 1)
+                for number in range(len(columns)):
                     found = jnp.zeros((STEPS, LANES), F32)
                     for block in range(cell_blocks):
-                        taken = jnp.take_along_axis(sums[block], lanes, axis=1, mode="promise_in_bounds")
-                        found = jnp.where(column >> 7 == block, taken, found)
+                        taken = jnp.take_along_axis(sums[block], lanes[number], axis=1, mode="promise_in_bounds")
+                        found = jnp.where(blocks[number] == block, taken, found)
                     send[row : row + STEPS, number * LANES : (number + 1) * LANES] = found
     for field in range(FIELDS):
         last[field * stride : (field + 1) * stride, :] = held[field, -stride:, :]

time: 26.4 us -> 26.5 us (level)
  no operation moved by 1% of the time
where the time goes in v11:
time: 26.5 us; the launch traced here: 26.4 us
  starting transfers between devices  13.2 us (50%)
  Pallas kernels  7.56 us (29%)
  waiting for transfers between devices  4.89 us (18%)
  between operations  0.7 us (3%)
    ppermute x8, starting transfers between devices, shift_along(): lax.ppermute(block, axis, [((i - distance) % size, i) for i in range(size)])  13.2 us
    ppermute x8, waiting for transfers between devices, shift_along(): lax.ppermute(block, axis, [((i - distance) % size, i) for i in range(size)])  4.89 us
    pallas_call x2, Pallas kernels, apply(): pl.pallas_call(functools.partial(apply_kernel, part, received, cell_block...  2.68 us
    pallas_call x1, Pallas kernels, per_device(): pl.pallas_call(functools.partial(local_kernel, (most, late), cell_blocks)...  1.94 us
    pallas_call x1, Pallas kernels, per_device(): pl.pallas_call(functools.partial(first_kernel, lead, wide, cell_blocks),...  1.56 us
    pallas_call x1, Pallas kernels, per_device(): pl.pallas_call(functools.partial(second_kernel, most, middle, wide, other...  0.81 us
    pallas_call x1, Pallas kernels, per_device(): pl.pallas_call(functools.partial(third_kernel, late, wide, others, cell_b...  0.57 us
  transfers between devices with their start and end apart: 8, of which 2 were waited for; matrix products, arithmetic and copies ran while one was open for 0% of the time, Pallas kernels for 18%

profile of v11, /device:TPU:0, one launch (start us, length us, event | category | flops | bytes accessed | tf_op | source)
XLA Modules:
  0.0 26.4 jit_solution(8192897099562322668)
XLA Ops:
  0.6 1.6 %gather_first.1 = (f32[48,512]{1,0:T(8,128)S(1)}, f32[3,384,128]{2,1,0:T(8,128)S(1)}, s32[4,256]{1,0:T(4,128)S(1)}, f32[48,128]{1,0:T(8,128)S(1)}) custom-call(f32[384,128]{1,0:T(8,128)} %bitcast.39, f32[384,128]{1,0:T(8,128)} %bitcast.40, f32[384,128]{1,0:T(8,128)} %bitcast.41, s32[4,256]{1,0:T(4,128)} %bitcast.42, s32[1,4]{1,0:T(1,128)} %refs_4_.1), custom_call_target="tpu_custom_call" | custom-call | flops 100663296 | bytes 1179648 | tf_op jit(solution)/shard_map/gather_first/pallas_call | solution.py:319
  2.2 4.1 %collective-permute-start.3 = (f32[48,512]{1,0:T(8,128)S(1)}, f32[48,512]{1,0:T(8,128)S(1)}, u32[]{:S(2)}, u32[]{:S(2)}) collective-permute-start(f32[48,512]{1,0:T(8,128)S(1)} %get-tuple-element.40), channel_id=1, source_target_pairs={{8,0},{12,4},{0,8},{4,12},{9,1},{13,5},{1,9},{5,13},{10,2},{14,6},... | collective-permute-start | bytes 294920 | tf_op jit(solution)/shard_map/ppermute | solution.py:25
  6.3 0.8 %gather_second.1 = (f32[48,512]{1,0:T(8,128)S(1)}, f32[96,256]{1,0:T(8,128)S(1)}, f32[96,256]{1,0:T(8,128)S(1)}, bf16[8,192,128]{2,1,0:T(8,128)(2,1)S(1)}) custom-call(f32[3,384,128]{2,1,0:T(8,128)S(1)} %get-tuple-element.29.held, s32[4,256]{1,0:T(4,128)S(1)} %get-tuple-element.31.listed), custom_call_target="tpu_custom_call" | custom-call | flops 402653184 | bytes 1179648 | tf_op jit(solution)/shard_map/gather_second/pallas_call | solution.py:339
  7.1 0.0 copy-start
  7.1 1.6 %collective-permute-start.1 = (f32[96,256]{1,0:T(8,128)S(1)}, f32[96,256]{1,0:T(8,128)S(1)}, u32[]{:S(2)}, u32[]{:S(2)}) collective-permute-start(f32[96,256]{1,0:T(8,128)S(1)} %get-tuple-element.33), channel_id=1, source_target_pairs={{12,0},{0,4},{4,8},{8,12},{13,1},{1,5},{5,9},{9,13},{14,2},{2,6},{... | collective-permute-start | bytes 294920 | tf_op jit(solution)/shard_map/ppermute | solution.py:25
  8.8 0.0 collective-permute-start
  8.8 0.3 %collective-permute-start.6 = (f32[48,512]{1,0:T(8,128)S(1)}, f32[48,512]{1,0:T(8,128)S(1)}, u32[]{:S(2)}, u32[]{:S(2)}) collective-permute-start(f32[48,512]{1,0:T(8,128)S(1)} %get-tuple-element.45), channel_id=1, source_target_pairs={{8,0},{12,4},{0,8},{4,12},{9,1},{13,5},{1,9},{5,13},{10,2},{14,6},... | collective-permute-start | bytes 294920 | tf_op jit(solution)/shard_map/ppermute | solution.py:25
  9.1 2.2 %collective-permute-start.7 = (f32[96,256]{1,0:T(8,128)S(1)}, f32[96,256]{1,0:T(8,128)S(1)}, u32[]{:S(2)}, u32[]{:S(2)}) collective-permute-start(f32[96,256]{1,0:T(8,128)S(1)} %get-tuple-element.48), channel_id=1, source_target_pairs={{4,0},{8,4},{12,8},{0,12},{5,1},{9,5},{13,9},{1,13},{6,2},{10,6},{... | collective-permute-start | bytes 294920 | tf_op jit(solution)/shard_map/ppermute | solution.py:25
  11.3 0.7 %collective-permute-done.prev = f32[48,128]{1,0:T(8,128)S(1)} collective-permute-done((f32[48,128]{1,0:T(8,128)S(1)}, f32[48,128]{1,0:T(8,128)S(1)}, u32[]{:S(2)}, u32[]{:S(2)}) %collective-permute-start) | collective-permute-done | bytes 24608 | tf_op jit(solution)/shard_map/ppermute | solution.py:25
  12.0 0.6 %gather_third.1 = (f32[48,512]{1,0:T(8,128)S(1)}, f32[48,256]{1,0:T(8,128)S(1)}, f32[48,256]{1,0:T(8,128)S(1)}, bf16[8,96,128]{2,1,0:T(8,128)(2,1)S(1)}) custom-call(f32[3,384,128]{2,1,0:T(8,128)S(1)} %get-tuple-element.29.held, f32[48,128]{1,0:T(8,128)S(1)} %collective-permute-done.prev, s32[4,256]{1,0:T(4,128)S(1)} %get-tuple-element.31.listed), custom_call_target="tpu_custom_call" | custom-call | flops 201326592 | bytes 1179648 | tf_op jit(solution)/shard_map/gather_third/pallas_call | solution.py:352
  12.6 1.1 %collective-permute-start.2 = (f32[48,512]{1,0:T(8,128)S(1)}, f32[48,512]{1,0:T(8,128)S(1)}, u32[]{:S(2)}, u32[]{:S(2)}) collective-permute-start(f32[48,512]{1,0:T(8,128)S(1)} %get-tuple-element.38), channel_id=1, source_target_pairs={{8,0},{12,4},{0,8},{4,12},{9,1},{13,5},{1,9},{5,13},{10,2},{14,6},... | collective-permute-start | bytes 294920 | tf_op jit(solution)/shard_map/ppermute | solution.py:25
  13.7 1.9 %local_terms.1 = (f32[8,96,128]{2,1,0:T(8,128)S(1)}, f32[8,48,128]{2,1,0:T(8,128)S(1)}, bf16[8,384,256]{2,1,0:T(8,128)(2,1)S(1)}) custom-call(f32[3,384,128]{2,1,0:T(8,128)S(1)} %get-tuple-element.29.held, f32[48,128]{1,0:T(8,128)S(1)} %collective-permute-done.prev, f32[8,128]{1,0:T(8,128)} %bitcast.43, f32[8,128]{1,0:T(8,128)} %bitcast.44, ...), custom_call_target="tpu_custom_call" | custom-call | flops 8847360 | bytes 3145728 | tf_op jit(solution)/shard_map/local_terms/pallas_call | solution.py:362
  15.6 0.0 collective-permute-done.3.refs_5_
  15.6 1.8 %collective-permute-start.4 = (f32[48,256]{1,0:T(8,128)S(1)}, f32[48,256]{1,0:T(8,128)S(1)}, u32[]{:S(2)}, u32[]{:S(2)}) collective-permute-start(f32[48,256]{1,0:T(8,128)S(1)} %get-tuple-element.41), channel_id=1, source_target_pairs={{12,0},{0,4},{4,8},{8,12},{13,1},{1,5},{5,9},{9,13},{14,2},{2,6},{... | collective-permute-start | bytes 147464 | tf_op jit(solution)/shard_map/ppermute | solution.py:25
  17.5 0.0 collective-permute-done.1.refs_6_
  17.5 2.0 %collective-permute-start.5 = (f32[48,256]{1,0:T(8,128)S(1)}, f32[48,256]{1,0:T(8,128)S(1)}, u32[]{:S(2)}, u32[]{:S(2)}) collective-permute-start(f32[48,256]{1,0:T(8,128)S(1)} %get-tuple-element.42), channel_id=1, source_target_pairs={{4,0},{8,4},{12,8},{0,12},{5,1},{9,5},{13,9},{1,13},{6,2},{10,6},{... | collective-permute-start | bytes 147464 | tf_op jit(solution)/shard_map/ppermute | solution.py:25
  19.5 0.0 collective-permute-done.6.refs_4_
  19.5 0.0 collective-permute-done.7.refs_7_
  19.5 0.0 copy-done
  19.5 1.5 %apply_tiles.2 = (f32[384,128]{1,0:T(8,128)}, f32[384,128]{1,0:T(8,128)}, f32[384,128]{1,0:T(8,128)}) custom-call(s32[3,8]{1,0:T(4,128)S(1)} %bitcast.34, bf16[8,384,256]{2,1,0:T(8,128)(2,1)S(1)} %get-tuple-element.35.refs_1_, f32[8,96,128]{2,1,0:T(8,128)S(1)} %get-tuple-element.43.refs_2_, bf16[8,192,128]{2,1,0:T(8,128)(2,1)S(1)} %get-tuple-element.44.refs_3_, ...), custom_call_target="tpu_custom_call" | custom-call | flops 301989888 | bytes 1572864 | tf_op jit(solution)/shard_map/apply_tiles/pallas_call | solution.py:392
  21.0 4.1 %collective-permute-done.2.refs_4_ = f32[48,512]{1,0:T(8,128)S(1)} collective-permute-done((f32[48,512]{1,0:T(8,128)S(1)}, f32[48,512]{1,0:T(8,128)S(1)}, u32[]{:S(2)}, u32[]{:S(2)}) %collective-permute-start.2) | collective-permute-done | bytes 98336 | tf_op jit(solution)/shard_map/ppermute | solution.py:25
  25.2 0.0 collective-permute-done.4.refs_5_
  25.2 0.0 collective-permute-done.5.refs_6_
  25.2 1.2 %apply_tiles.3 = (f32[384,128]{1,0:T(8,128)}, f32[384,128]{1,0:T(8,128)}, f32[384,128]{1,0:T(8,128)}) custom-call(s32[3,8]{1,0:T(4,128)S(1)} %bitcast.35, bf16[8,384,256]{2,1,0:T(8,128)(2,1)S(1)} %get-tuple-element.35.refs_1_, f32[8,48,128]{2,1,0:T(8,128)S(1)} %get-tuple-element.36.refs_2_, ...), custom_call_target="tpu_custom_call", output_to_operand_aliasing={{0}: (7, {}), {1}: (8, {}), {2}: (9, {})} | custom-call | flops 150994944 | bytes 786432 | tf_op jit(solution)/shard_map/apply_tiles/pallas_call | solution.py:392
Async XLA Ops:
  2.2 13.4 %collective-permute-start.3 = (f32[48,512]{1,0:T(8,128)S(1)}, f32[48,512]{1,0:T(8,128)S(1)}, u32[]{:S(2)}, u32[]{:S(2)}) collective-permute-start(f32[48,512]{1,0:T(8,128)S(1)} %get-tuple-element.40), channel_id=1, source_target_pairs={{8,0},{12,4},{0,8},{4,12},{9,1},{13,5},{1,9},{5,13},{10,2},{14,6},... | collective-permute-start | bytes 294920 | tf_op jit(solution)/shard_map/ppermute | solution.py:25
  7.1 12.4 %copy-start = (s32[8,3]{0,1:T(4,128)S(1)}, s32[8,3]{0,1:T(4,128)}, u32[]{:S(2)}) copy-start(s32[8,3]{0,1:T(4,128)} %param.15) | copy-start | bytes 292
  7.1 10.4 %collective-permute-start.1 = (f32[96,256]{1,0:T(8,128)S(1)}, f32[96,256]{1,0:T(8,128)S(1)}, u32[]{:S(2)}, u32[]{:S(2)}) collective-permute-start(f32[96,256]{1,0:T(8,128)S(1)} %get-tuple-element.33), channel_id=1, source_target_pairs={{12,0},{0,4},{4,8},{8,12},{13,1},{1,5},{5,9},{9,13},{14,2},{2,6},{... | collective-permute-start | bytes 294920 | tf_op jit(solution)/shard_map/ppermute | solution.py:25
  8.8 3.3 %collective-permute-start = (f32[48,128]{1,0:T(8,128)S(1)}, f32[48,128]{1,0:T(8,128)S(1)}, u32[]{:S(2)}, u32[]{:S(2)}) collective-permute-start(f32[48,128]{1,0:T(8,128)S(1)} %get-tuple-element.30), channel_id=1, source_target_pairs={{3,0},{0,1},{1,2},{2,3},{7,4},{4,5},{5,6},{6,7},{11,8},{8,9},{9,10... | collective-permute-start | bytes 73736 | tf_op jit(solution)/shard_map/ppermute | solution.py:25
  8.8 10.8 %collective-permute-start.6 = (f32[48,512]{1,0:T(8,128)S(1)}, f32[48,512]{1,0:T(8,128)S(1)}, u32[]{:S(2)}, u32[]{:S(2)}) collective-permute-start(f32[48,512]{1,0:T(8,128)S(1)} %get-tuple-element.45), channel_id=1, source_target_pairs={{8,0},{12,4},{0,8},{4,12},{9,1},{13,5},{1,9},{5,13},{10,2},{14,6},... | collective-permute-start | bytes 294920 | tf_op jit(solution)/shard_map/ppermute | solution.py:25
  9.1 10.4 %collective-permute-start.7 = (f32[96,256]{1,0:T(8,128)S(1)}, f32[96,256]{1,0:T(8,128)S(1)}, u32[]{:S(2)}, u32[]{:S(2)}) collective-permute-start(f32[96,256]{1,0:T(8,128)S(1)} %get-tuple-element.48), channel_id=1, source_target_pairs={{4,0},{8,4},{12,8},{0,12},{5,1},{9,5},{13,9},{1,13},{6,2},{10,6},{... | collective-permute-start | bytes 294920 | tf_op jit(solution)/shard_map/ppermute | solution.py:25
  12.6 12.6 %collective-permute-start.2 = (f32[48,512]{1,0:T(8,128)S(1)}, f32[48,512]{1,0:T(8,128)S(1)}, u32[]{:S(2)}, u32[]{:S(2)}) collective-permute-start(f32[48,512]{1,0:T(8,128)S(1)} %get-tuple-element.38), channel_id=1, source_target_pairs={{8,0},{12,4},{0,8},{4,12},{9,1},{13,5},{1,9},{5,13},{10,2},{14,6},... | collective-permute-start | bytes 294920 | tf_op jit(solution)/shard_map/ppermute | solution.py:25
  15.6 9.5 %collective-permute-start.4 = (f32[48,256]{1,0:T(8,128)S(1)}, f32[48,256]{1,0:T(8,128)S(1)}, u32[]{:S(2)}, u32[]{:S(2)}) collective-permute-start(f32[48,256]{1,0:T(8,128)S(1)} %get-tuple-element.41), channel_id=1, source_target_pairs={{12,0},{0,4},{4,8},{8,12},{13,1},{1,5},{5,9},{9,13},{14,2},{2,6},{... | collective-permute-start | bytes 147464 | tf_op jit(solution)/shard_map/ppermute | solution.py:25
  17.5 7.7 %collective-permute-start.5 = (f32[48,256]{1,0:T(8,128)S(1)}, f32[48,256]{1,0:T(8,128)S(1)}, u32[]{:S(2)}, u32[]{:S(2)}) collective-permute-start(f32[48,256]{1,0:T(8,128)S(1)} %get-tuple-element.42), channel_id=1, source_target_pairs={{4,0},{8,4},{12,8},{0,12},{5,1},{9,5},{13,9},{1,13},{6,2},{10,6},{... | collective-permute-start | bytes 147464 | tf_op jit(solution)/shard_map/ppermute | solution.py:25

commit v12 on v9

--- a/solution.py
+++ b/solution.py
@@ -386,7 +386,9 @@
     sends[1], wide_lead = lax.optimization_barrier((sends[1], wide_lead))
     arrived_late.append(send_to(sends[1], slot_groups[1]))
     for number in range(2, len(sends)):
-        sends[number], narrow_most[0] = lax.optimization_barrier((sends[number], narrow_most[0]))
+        sends[number], narrow_most[0], wide_middle, split_tiles = lax.optimization_barrier(
+            (sends[number], narrow_most[0], wide_middle, split_tiles)
+        )
         arrived_late.append(send_to(sends[number], slot_groups[number]))
 
     def apply(part, base, parts, transfers, outs):

time: 26.9 us -> 28.5 us (1.059)
  starting transfers between devices: 13.2 us -> 18.8 us
  waiting for transfers between devices: 5.43 us -> 1.4 us
    ppermute x8, starting transfers between devices: 13.2 us -> 18.8 us  [shift_along(): lax.ppermute(block, axis, [((i - distance) % size, i) for i in range(size)])]
    ppermute x8, waiting for transfers between devices: 5.43 us -> 1.4 us  [shift_along(): lax.ppermute(block, axis, [((i - distance) % size, i) for i in range(size)])]
  transfers between devices with their start and end apart: 8 -> 8, of which waited for: 3 -> 2; matrix products, arithmetic and copies ran while one was open for 0% -> 0% of each run, Pallas kernels for 18% -> 17%
where the time goes in v12:
time: 28.5 us; the launch traced here: 28.4 us
  starting transfers between devices  18.8 us (66%)
  Pallas kernels  7.44 us (26%)
  waiting for transfers between devices  1.4 us (5%)
  between operations  0.71 us (2%)
    ppermute x8, starting transfers between devices, shift_along(): lax.ppermute(block, axis, [((i - distance) % size, i) for i in range(size)])  18.8 us
    pallas_call x2, Pallas kernels, apply(): pl.pallas_call(functools.partial(apply_kernel, part, received, cell_block...  2.68 us
    pallas_call x1, Pallas kernels, per_device(): pl.pallas_call(functools.partial(local_kernel, (most, late), cell_blocks)...  1.94 us
    pallas_call x1, Pallas kernels, per_device(): pl.pallas_call(functools.partial(first_kernel, lead, wide, cell_blocks),...  1.44 us
    ppermute x8, waiting for transfers between devices, shift_along(): lax.ppermute(block, axis, [((i - distance) % size, i) for i in range(size)])  1.4 us
    pallas_call x1, Pallas kernels, per_device(): pl.pallas_call(functools.partial(second_kernel, most, middle, wide, other...  0.81 us
    pallas_call x1, Pallas kernels, per_device(): pl.pallas_call(functools.partial(third_kernel, late, wide, others, cell_b...  0.57 us
  transfers between devices with their start and end apart: 8, of which 2 were waited for; matrix products, arithmetic and copies ran while one was open for 0% of the time, Pallas kernels for 17%

profile of v12, /device:TPU:0, one launch (start us, length us, event | category | flops | bytes accessed | tf_op | source)
XLA Modules:
  0.0 28.4 jit_solution(11051594868623114307)
XLA Ops:
  0.6 1.4 %gather_first.1 = (f32[48,512]{1,0:T(8,128)S(1)}, f32[3,384,128]{2,1,0:T(8,128)S(1)}, s32[4,256]{1,0:T(4,128)S(1)}, f32[48,128]{1,0:T(8,128)S(1)}) custom-call(f32[384,128]{1,0:T(8,128)} %bitcast.39, f32[384,128]{1,0:T(8,128)} %bitcast.40, f32[384,128]{1,0:T(8,128)} %bitcast.41, s32[4,256]{1,0:T(4,128)} %bitcast.42, s32[1,4]{1,0:T(1,128)} %refs_4_.1), custom_call_target="tpu_custom_call" | custom-call | flops 100663296 | bytes 1179648 | tf_op jit(solution)/shard_map/gather_first/pallas_call | solution.py:322
  2.1 4.1 %collective-permute-start.4 = (f32[48,512]{1,0:T(8,128)S(1)}, f32[48,512]{1,0:T(8,128)S(1)}, u32[]{:S(2)}, u32[]{:S(2)}) collective-permute-start(f32[48,512]{1,0:T(8,128)S(1)} %get-tuple-element.42), channel_id=1, source_target_pairs={{8,0},{12,4},{0,8},{4,12},{9,1},{13,5},{1,9},{5,13},{10,2},{14,6},... | collective-permute-start | bytes 294920 | tf_op jit(solution)/shard_map/ppermute | solution.py:25
  6.2 0.8 %gather_second.1 = (f32[48,512]{1,0:T(8,128)S(1)}, f32[96,256]{1,0:T(8,128)S(1)}, f32[96,256]{1,0:T(8,128)S(1)}, bf16[8,192,128]{2,1,0:T(8,128)(2,1)S(1)}) custom-call(f32[3,384,128]{2,1,0:T(8,128)S(1)} %get-tuple-element.30.held, s32[4,256]{1,0:T(4,128)S(1)} %get-tuple-element.32.listed), custom_call_target="tpu_custom_call" | custom-call | flops 402653184 | bytes 1179648 | tf_op jit(solution)/shard_map/gather_second/pallas_call | solution.py:342
  7.0 0.0 copy-start
  7.0 1.6 %collective-permute-start.1 = (f32[96,256]{1,0:T(8,128)S(1)}, f32[96,256]{1,0:T(8,128)S(1)}, u32[]{:S(2)}, u32[]{:S(2)}) collective-permute-start(f32[96,256]{1,0:T(8,128)S(1)} %get-tuple-element.34), channel_id=1, source_target_pairs={{12,0},{0,4},{4,8},{8,12},{13,1},{1,5},{5,9},{9,13},{14,2},{2,6},{... | collective-permute-start | bytes 294920 | tf_op jit(solution)/shard_map/ppermute | solution.py:25
  8.6 0.3 %collective-permute-start.2 = (f32[48,512]{1,0:T(8,128)S(1)}, f32[48,512]{1,0:T(8,128)S(1)}, u32[]{:S(2)}, u32[]{:S(2)}) collective-permute-start(f32[48,512]{1,0:T(8,128)S(1)} %get-tuple-element.35), channel_id=1, source_target_pairs={{8,0},{12,4},{0,8},{4,12},{9,1},{13,5},{1,9},{5,13},{10,2},{14,6},... | collective-permute-start | bytes 294920 | tf_op jit(solution)/shard_map/ppermute | solution.py:25
  9.0 0.0 collective-permute-start
  9.0 2.1 %collective-permute-start.7 = (f32[96,256]{1,0:T(8,128)S(1)}, f32[96,256]{1,0:T(8,128)S(1)}, u32[]{:S(2)}, u32[]{:S(2)}) collective-permute-start(f32[96,256]{1,0:T(8,128)S(1)} %get-tuple-element.50), channel_id=1, source_target_pairs={{4,0},{8,4},{12,8},{0,12},{5,1},{9,5},{13,9},{1,13},{6,2},{10,6},{... | collective-permute-start | bytes 294920 | tf_op jit(solution)/shard_map/ppermute | solution.py:25
  11.1 1.1 %collective-permute-done.prev = f32[48,128]{1,0:T(8,128)S(1)} collective-permute-done((f32[48,128]{1,0:T(8,128)S(1)}, f32[48,128]{1,0:T(8,128)S(1)}, u32[]{:S(2)}, u32[]{:S(2)}) %collective-permute-start) | collective-permute-done | bytes 24608 | tf_op jit(solution)/shard_map/ppermute | solution.py:25
  12.2 0.6 %gather_third.1 = (f32[48,512]{1,0:T(8,128)S(1)}, f32[48,256]{1,0:T(8,128)S(1)}, f32[48,256]{1,0:T(8,128)S(1)}, bf16[8,96,128]{2,1,0:T(8,128)(2,1)S(1)}) custom-call(f32[3,384,128]{2,1,0:T(8,128)S(1)} %get-tuple-element.30.held, f32[48,128]{1,0:T(8,128)S(1)} %collective-permute-done.prev, s32[4,256]{1,0:T(4,128)S(1)} %get-tuple-element.32.listed), custom_call_target="tpu_custom_call" | custom-call | flops 201326592 | bytes 1179648 | tf_op jit(solution)/shard_map/gather_third/pallas_call | solution.py:355
  12.8 2.7 %collective-permute-start.3 = (f32[48,512]{1,0:T(8,128)S(1)}, f32[48,512]{1,0:T(8,128)S(1)}, u32[]{:S(2)}, u32[]{:S(2)}) collective-permute-start(f32[48,512]{1,0:T(8,128)S(1)} %get-tuple-element.40), channel_id=1, source_target_pairs={{8,0},{12,4},{0,8},{4,12},{9,1},{13,5},{1,9},{5,13},{10,2},{14,6},... | collective-permute-start | bytes 294920 | tf_op jit(solution)/shard_map/ppermute | solution.py:25
  15.5 1.9 %local_terms.1 = (f32[8,96,128]{2,1,0:T(8,128)S(1)}, f32[8,48,128]{2,1,0:T(8,128)S(1)}, bf16[8,384,256]{2,1,0:T(8,128)(2,1)S(1)}) custom-call(f32[3,384,128]{2,1,0:T(8,128)S(1)} %get-tuple-element.30.held, f32[48,128]{1,0:T(8,128)S(1)} %collective-permute-done.prev, f32[8,128]{1,0:T(8,128)} %bitcast.43, f32[8,128]{1,0:T(8,128)} %bitcast.44, ...), custom_call_target="tpu_custom_call" | custom-call | flops 8847360 | bytes 3145728 | tf_op jit(solution)/shard_map/local_terms/pallas_call | solution.py:365
  17.4 0.0 collective-permute-done.4.refs_5_
  17.4 0.1 collective-permute-start.5
  17.6 0.0 collective-permute-done.1.refs_6_
  17.6 0.0 collective-permute-done.2.refs_4_
  17.6 7.8 %collective-permute-start.6 = (f32[48,256]{1,0:T(8,128)S(1)}, f32[48,256]{1,0:T(8,128)S(1)}, u32[]{:S(2)}, u32[]{:S(2)}) collective-permute-start(f32[48,256]{1,0:T(8,128)S(1)} %get-tuple-element.44), channel_id=1, source_target_pairs={{4,0},{8,4},{12,8},{0,12},{5,1},{9,5},{13,9},{1,13},{6,2},{10,6},{... | collective-permute-start | bytes 147464 | tf_op jit(solution)/shard_map/ppermute | solution.py:25
  25.4 0.0 collective-permute-done.7.refs_7_
  25.4 0.0 copy-done
  25.4 1.5 %apply_tiles.2 = (f32[384,128]{1,0:T(8,128)}, f32[384,128]{1,0:T(8,128)}, f32[384,128]{1,0:T(8,128)}) custom-call(s32[3,8]{1,0:T(4,128)S(1)} %bitcast.34, bf16[8,384,256]{2,1,0:T(8,128)(2,1)S(1)} %get-tuple-element.37.refs_1_, f32[8,96,128]{2,1,0:T(8,128)S(1)} %get-tuple-element.45.refs_2_, bf16[8,192,128]{2,1,0:T(8,128)(2,1)S(1)} %get-tuple-element.46.refs_3_, ...), custom_call_target="tpu_custom_call" | custom-call | flops 301989888 | bytes 1572864 | tf_op jit(solution)/shard_map/apply_tiles/pallas_call | solution.py:397
  26.9 0.0 collective-permute-done.3.refs_4_
  26.9 0.0 collective-permute-done.5.refs_5_
  26.9 0.2 collective-permute-done.6.refs_6_
  27.1 1.2 %apply_tiles.3 = (f32[384,128]{1,0:T(8,128)}, f32[384,128]{1,0:T(8,128)}, f32[384,128]{1,0:T(8,128)}) custom-call(s32[3,8]{1,0:T(4,128)S(1)} %bitcast.35, bf16[8,384,256]{2,1,0:T(8,128)(2,1)S(1)} %get-tuple-element.37.refs_1_, f32[8,48,128]{2,1,0:T(8,128)S(1)} %get-tuple-element.38.refs_2_, ...), custom_call_target="tpu_custom_call", output_to_operand_aliasing={{0}: (7, {}), {1}: (8, {}), {2}: (9, {})} | custom-call | flops 150994944 | bytes 786432 | tf_op jit(solution)/shard_map/apply_tiles/pallas_call | solution.py:397
Async XLA Ops:
  2.1 15.3 %collective-permute-start.4 = (f32[48,512]{1,0:T(8,128)S(1)}, f32[48,512]{1,0:T(8,128)S(1)}, u32[]{:S(2)}, u32[]{:S(2)}) collective-permute-start(f32[48,512]{1,0:T(8,128)S(1)} %get-tuple-element.42), channel_id=1, source_target_pairs={{8,0},{12,4},{0,8},{4,12},{9,1},{13,5},{1,9},{5,13},{10,2},{14,6},... | collective-permute-start | bytes 294920 | tf_op jit(solution)/shard_map/ppermute | solution.py:25
  7.0 18.4 %copy-start = (s32[8,3]{0,1:T(4,128)S(1)}, s32[8,3]{0,1:T(4,128)}, u32[]{:S(2)}) copy-start(s32[8,3]{0,1:T(4,128)} %param.15) | copy-start | bytes 292
  7.0 10.6 %collective-permute-start.1 = (f32[96,256]{1,0:T(8,128)S(1)}, f32[96,256]{1,0:T(8,128)S(1)}, u32[]{:S(2)}, u32[]{:S(2)}) collective-permute-start(f32[96,256]{1,0:T(8,128)S(1)} %get-tuple-element.34), channel_id=1, source_target_pairs={{12,0},{0,4},{4,8},{8,12},{13,1},{1,5},{5,9},{9,13},{14,2},{2,6},{... | collective-permute-start | bytes 294920 | tf_op jit(solution)/shard_map/ppermute | solution.py:25
  8.6 8.9 %collective-permute-start.2 = (f32[48,512]{1,0:T(8,128)S(1)}, f32[48,512]{1,0:T(8,128)S(1)}, u32[]{:S(2)}, u32[]{:S(2)}) collective-permute-start(f32[48,512]{1,0:T(8,128)S(1)} %get-tuple-element.35), channel_id=1, source_target_pairs={{8,0},{12,4},{0,8},{4,12},{9,1},{13,5},{1,9},{5,13},{10,2},{14,6},... | collective-permute-start | bytes 294920 | tf_op jit(solution)/shard_map/ppermute | solution.py:25
  9.0 3.3 %collective-permute-start = (f32[48,128]{1,0:T(8,128)S(1)}, f32[48,128]{1,0:T(8,128)S(1)}, u32[]{:S(2)}, u32[]{:S(2)}) collective-permute-start(f32[48,128]{1,0:T(8,128)S(1)} %get-tuple-element.31), channel_id=1, source_target_pairs={{3,0},{0,1},{1,2},{2,3},{7,4},{4,5},{5,6},{6,7},{11,8},{8,9},{9,10... | collective-permute-start | bytes 73736 | tf_op jit(solution)/shard_map/ppermute | solution.py:25
  9.0 16.4 %collective-permute-start.7 = (f32[96,256]{1,0:T(8,128)S(1)}, f32[96,256]{1,0:T(8,128)S(1)}, u32[]{:S(2)}, u32[]{:S(2)}) collective-permute-start(f32[96,256]{1,0:T(8,128)S(1)} %get-tuple-element.50), channel_id=1, source_target_pairs={{4,0},{8,4},{12,8},{0,12},{5,1},{9,5},{13,9},{1,13},{6,2},{10,6},{... | collective-permute-start | bytes 294920 | tf_op jit(solution)/shard_map/ppermute | solution.py:25
  12.8 14.1 %collective-permute-start.3 = (f32[48,512]{1,0:T(8,128)S(1)}, f32[48,512]{1,0:T(8,128)S(1)}, u32[]{:S(2)}, u32[]{:S(2)}) collective-permute-start(f32[48,512]{1,0:T(8,128)S(1)} %get-tuple-element.40), channel_id=1, source_target_pairs={{8,0},{12,4},{0,8},{4,12},{9,1},{13,5},{1,9},{5,13},{10,2},{14,6},... | collective-permute-start | bytes 294920 | tf_op jit(solution)/shard_map/ppermute | solution.py:25
  17.4 9.5 %collective-permute-start.5 = (f32[48,256]{1,0:T(8,128)S(1)}, f32[48,256]{1,0:T(8,128)S(1)}, u32[]{:S(2)}, u32[]{:S(2)}) collective-permute-start(f32[48,256]{1,0:T(8,128)S(1)} %get-tuple-element.43), channel_id=1, source_target_pairs={{12,0},{0,4},{4,8},{8,12},{13,1},{1,5},{5,9},{9,13},{14,2},{2,6},{... | collective-permute-start | bytes 147464 | tf_op jit(solution)/shard_map/ppermute | solution.py:25
  17.6 9.6 %collective-permute-start.6 = (f32[48,256]{1,0:T(8,128)S(1)}, f32[48,256]{1,0:T(8,128)S(1)}, u32[]{:S(2)}, u32[]{:S(2)}) collective-permute-start(f32[48,256]{1,0:T(8,128)S(1)} %get-tuple-element.44), channel_id=1, source_target_pairs={{4,0},{8,4},{12,8},{0,12},{5,1},{9,5},{13,9},{1,13},{6,2},{10,6},{... | collective-permute-start | bytes 147464 | tf_op jit(solution)/shard_map/ppermute | solution.py:25

commit v13 on v11

--- a/solution.py
+++ b/solution.py
@@ -127,8 +127,9 @@
     columns = [jnp.broadcast_to(column, (STEPS, LANES)) for slot in slots for column in columns[slot]]
     lanes = [column & (LANES - 1) for column in columns]
     blocks = [column >> 7 for column in columns]
+    for copy in needed:
+        copy.wait()
     for field in range(FIELDS):
-        needed[field].wait()
         for place, group in enumerate(lead):
             for species in range(2):
                 row = ((place * FIELDS + field) * 2 + species) * STEPS

time: 26.5 us -> 26.4 us (level)
  no operation moved by 1% of the time
where the time goes in v13:
time: 26.4 us; the launch traced here: 26.3 us
  starting transfers between devices  13.2 us (50%)
  Pallas kernels  7.45 us (28%)
  waiting for transfers between devices  4.89 us (19%)
  between operations  0.7 us (3%)
    ppermute x8, starting transfers between devices, shift_along(): lax.ppermute(block, axis, [((i - distance) % size, i) for i in range(size)])  13.2 us
    ppermute x8, waiting for transfers between devices, shift_along(): lax.ppermute(block, axis, [((i - distance) % size, i) for i in range(size)])  4.89 us
    pallas_call x2, Pallas kernels, apply(): pl.pallas_call(functools.partial(apply_kernel, part, received, cell_block...  2.68 us
    pallas_call x1, Pallas kernels, per_device(): pl.pallas_call(functools.partial(local_kernel, (most, late), cell_blocks)...  1.94 us
    pallas_call x1, Pallas kernels, per_device(): pl.pallas_call(functools.partial(first_kernel, lead, wide, cell_blocks),...  1.44 us
    pallas_call x1, Pallas kernels, per_device(): pl.pallas_call(functools.partial(second_kernel, most, middle, wide, other...  0.81 us
    pallas_call x1, Pallas kernels, per_device(): pl.pallas_call(functools.partial(third_kernel, late, wide, others, cell_b...  0.57 us
  transfers between devices with their start and end apart: 8, of which 2 were waited for; matrix products, arithmetic and copies ran while one was open for 0% of the time, Pallas kernels for 18%

profile of v13, /device:TPU:0, one launch (start us, length us, event | category | flops | bytes accessed | tf_op | source)
XLA Modules:
  0.0 26.3 jit_solution(5851981036802354869)
XLA Ops:
  0.6 1.4 %gather_first.1 = (f32[48,512]{1,0:T(8,128)S(1)}, f32[3,384,128]{2,1,0:T(8,128)S(1)}, s32[4,256]{1,0:T(4,128)S(1)}, f32[48,128]{1,0:T(8,128)S(1)}) custom-call(f32[384,128]{1,0:T(8,128)} %bitcast.39, f32[384,128]{1,0:T(8,128)} %bitcast.40, f32[384,128]{1,0:T(8,128)} %bitcast.41, s32[4,256]{1,0:T(4,128)} %bitcast.42, s32[1,4]{1,0:T(1,128)} %refs_4_.1), custom_call_target="tpu_custom_call" | custom-call | flops 100663296 | bytes 1179648 | tf_op jit(solution)/shard_map/gather_first/pallas_call | solution.py:320
  2.1 4.1 %collective-permute-start.3 = (f32[48,512]{1,0:T(8,128)S(1)}, f32[48,512]{1,0:T(8,128)S(1)}, u32[]{:S(2)}, u32[]{:S(2)}) collective-permute-start(f32[48,512]{1,0:T(8,128)S(1)} %get-tuple-element.40), channel_id=1, source_target_pairs={{8,0},{12,4},{0,8},{4,12},{9,1},{13,5},{1,9},{5,13},{10,2},{14,6},... | collective-permute-start | bytes 294920 | tf_op jit(solution)/shard_map/ppermute | solution.py:25
  6.2 0.8 %gather_second.1 = (f32[48,512]{1,0:T(8,128)S(1)}, f32[96,256]{1,0:T(8,128)S(1)}, f32[96,256]{1,0:T(8,128)S(1)}, bf16[8,192,128]{2,1,0:T(8,128)(2,1)S(1)}) custom-call(f32[3,384,128]{2,1,0:T(8,128)S(1)} %get-tuple-element.29.held, s32[4,256]{1,0:T(4,128)S(1)} %get-tuple-element.31.listed), custom_call_target="tpu_custom_call" | custom-call | flops 402653184 | bytes 1179648 | tf_op jit(solution)/shard_map/gather_second/pallas_call | solution.py:340
  7.0 0.0 copy-start
  7.0 1.6 %collective-permute-start.1 = (f32[96,256]{1,0:T(8,128)S(1)}, f32[96,256]{1,0:T(8,128)S(1)}, u32[]{:S(2)}, u32[]{:S(2)}) collective-permute-start(f32[96,256]{1,0:T(8,128)S(1)} %get-tuple-element.33), channel_id=1, source_target_pairs={{12,0},{0,4},{4,8},{8,12},{13,1},{1,5},{5,9},{9,13},{14,2},{2,6},{... | collective-permute-start | bytes 294920 | tf_op jit(solution)/shard_map/ppermute | solution.py:25
  8.6 0.0 collective-permute-start
  8.6 0.3 %collective-permute-start.6 = (f32[48,512]{1,0:T(8,128)S(1)}, f32[48,512]{1,0:T(8,128)S(1)}, u32[]{:S(2)}, u32[]{:S(2)}) collective-permute-start(f32[48,512]{1,0:T(8,128)S(1)} %get-tuple-element.45), channel_id=1, source_target_pairs={{8,0},{12,4},{0,8},{4,12},{9,1},{13,5},{1,9},{5,13},{10,2},{14,6},... | collective-permute-start | bytes 294920 | tf_op jit(solution)/shard_map/ppermute | solution.py:25
  9.0 2.2 %collective-permute-start.7 = (f32[96,256]{1,0:T(8,128)S(1)}, f32[96,256]{1,0:T(8,128)S(1)}, u32[]{:S(2)}, u32[]{:S(2)}) collective-permute-start(f32[96,256]{1,0:T(8,128)S(1)} %get-tuple-element.48), channel_id=1, source_target_pairs={{4,0},{8,4},{12,8},{0,12},{5,1},{9,5},{13,9},{1,13},{6,2},{10,6},{... | collective-permute-start | bytes 294920 | tf_op jit(solution)/shard_map/ppermute | solution.py:25
  11.2 0.7 %collective-permute-done.prev = f32[48,128]{1,0:T(8,128)S(1)} collective-permute-done((f32[48,128]{1,0:T(8,128)S(1)}, f32[48,128]{1,0:T(8,128)S(1)}, u32[]{:S(2)}, u32[]{:S(2)}) %collective-permute-start) | collective-permute-done | bytes 24608 | tf_op jit(solution)/shard_map/ppermute | solution.py:25
  11.9 0.6 %gather_third.1 = (f32[48,512]{1,0:T(8,128)S(1)}, f32[48,256]{1,0:T(8,128)S(1)}, f32[48,256]{1,0:T(8,128)S(1)}, bf16[8,96,128]{2,1,0:T(8,128)(2,1)S(1)}) custom-call(f32[3,384,128]{2,1,0:T(8,128)S(1)} %get-tuple-element.29.held, f32[48,128]{1,0:T(8,128)S(1)} %collective-permute-done.prev, s32[4,256]{1,0:T(4,128)S(1)} %get-tuple-element.31.listed), custom_call_target="tpu_custom_call" | custom-call | flops 201326592 | bytes 1179648 | tf_op jit(solution)/shard_map/gather_third/pallas_call | solution.py:353
  12.5 1.1 %collective-permute-start.2 = (f32[48,512]{1,0:T(8,128)S(1)}, f32[48,512]{1,0:T(8,128)S(1)}, u32[]{:S(2)}, u32[]{:S(2)}) collective-permute-start(f32[48,512]{1,0:T(8,128)S(1)} %get-tuple-element.38), channel_id=1, source_target_pairs={{8,0},{12,4},{0,8},{4,12},{9,1},{13,5},{1,9},{5,13},{10,2},{14,6},... | collective-permute-start | bytes 294920 | tf_op jit(solution)/shard_map/ppermute | solution.py:25
  13.6 1.9 %local_terms.1 = (f32[8,96,128]{2,1,0:T(8,128)S(1)}, f32[8,48,128]{2,1,0:T(8,128)S(1)}, bf16[8,384,256]{2,1,0:T(8,128)(2,1)S(1)}) custom-call(f32[3,384,128]{2,1,0:T(8,128)S(1)} %get-tuple-element.29.held, f32[48,128]{1,0:T(8,128)S(1)} %collective-permute-done.prev, f32[8,128]{1,0:T(8,128)} %bitcast.43, f32[8,128]{1,0:T(8,128)} %bitcast.44, ...), custom_call_target="tpu_custom_call" | custom-call | flops 8847360 | bytes 3145728 | tf_op jit(solution)/shard_map/local_terms/pallas_call | solution.py:363
  15.5 0.0 collective-permute-done.3.refs_5_
  15.5 1.8 %collective-permute-start.4 = (f32[48,256]{1,0:T(8,128)S(1)}, f32[48,256]{1,0:T(8,128)S(1)}, u32[]{:S(2)}, u32[]{:S(2)}) collective-permute-start(f32[48,256]{1,0:T(8,128)S(1)} %get-tuple-element.41), channel_id=1, source_target_pairs={{12,0},{0,4},{4,8},{8,12},{13,1},{1,5},{5,9},{9,13},{14,2},{2,6},{... | collective-permute-start | bytes 147464 | tf_op jit(solution)/shard_map/ppermute | solution.py:25
  17.4 0.0 collective-permute-done.1.refs_6_
  17.4 2.0 %collective-permute-start.5 = (f32[48,256]{1,0:T(8,128)S(1)}, f32[48,256]{1,0:T(8,128)S(1)}, u32[]{:S(2)}, u32[]{:S(2)}) collective-permute-start(f32[48,256]{1,0:T(8,128)S(1)} %get-tuple-element.42), channel_id=1, source_target_pairs={{4,0},{8,4},{12,8},{0,12},{5,1},{9,5},{13,9},{1,13},{6,2},{10,6},{... | collective-permute-start | bytes 147464 | tf_op jit(solution)/shard_map/ppermute | solution.py:25
  19.4 0.0 collective-permute-done.6.refs_4_
  19.4 0.0 collective-permute-done.7.refs_7_
  19.4 0.0 copy-done
  19.4 1.5 %apply_tiles.2 = (f32[384,128]{1,0:T(8,128)}, f32[384,128]{1,0:T(8,128)}, f32[384,128]{1,0:T(8,128)}) custom-call(s32[3,8]{1,0:T(4,128)S(1)} %bitcast.34, bf16[8,384,256]{2,1,0:T(8,128)(2,1)S(1)} %get-tuple-element.35.refs_1_, f32[8,96,128]{2,1,0:T(8,128)S(1)} %get-tuple-element.43.refs_2_, bf16[8,192,128]{2,1,0:T(8,128)(2,1)S(1)} %get-tuple-element.44.refs_3_, ...), custom_call_target="tpu_custom_call" | custom-call | flops 301989888 | bytes 1572864 | tf_op jit(solution)/shard_map/apply_tiles/pallas_call | solution.py:393
  20.9 4.1 %collective-permute-done.2.refs_4_ = f32[48,512]{1,0:T(8,128)S(1)} collective-permute-done((f32[48,512]{1,0:T(8,128)S(1)}, f32[48,512]{1,0:T(8,128)S(1)}, u32[]{:S(2)}, u32[]{:S(2)}) %collective-permute-start.2) | collective-permute-done | bytes 98336 | tf_op jit(solution)/shard_map/ppermute | solution.py:25
  25.0 0.0 collective-permute-done.4.refs_5_
  25.0 0.0 collective-permute-done.5.refs_6_
  25.0 1.2 %apply_tiles.3 = (f32[384,128]{1,0:T(8,128)}, f32[384,128]{1,0:T(8,128)}, f32[384,128]{1,0:T(8,128)}) custom-call(s32[3,8]{1,0:T(4,128)S(1)} %bitcast.35, bf16[8,384,256]{2,1,0:T(8,128)(2,1)S(1)} %get-tuple-element.35.refs_1_, f32[8,48,128]{2,1,0:T(8,128)S(1)} %get-tuple-element.36.refs_2_, ...), custom_call_target="tpu_custom_call", output_to_operand_aliasing={{0}: (7, {}), {1}: (8, {}), {2}: (9, {})} | custom-call | flops 150994944 | bytes 786432 | tf_op jit(solution)/shard_map/apply_tiles/pallas_call | solution.py:393
Async XLA Ops:
  2.1 13.4 %collective-permute-start.3 = (f32[48,512]{1,0:T(8,128)S(1)}, f32[48,512]{1,0:T(8,128)S(1)}, u32[]{:S(2)}, u32[]{:S(2)}) collective-permute-start(f32[48,512]{1,0:T(8,128)S(1)} %get-tuple-element.40), channel_id=1, source_target_pairs={{8,0},{12,4},{0,8},{4,12},{9,1},{13,5},{1,9},{5,13},{10,2},{14,6},... | collective-permute-start | bytes 294920 | tf_op jit(solution)/shard_map/ppermute | solution.py:25
  7.0 12.4 %copy-start = (s32[8,3]{0,1:T(4,128)S(1)}, s32[8,3]{0,1:T(4,128)}, u32[]{:S(2)}) copy-start(s32[8,3]{0,1:T(4,128)} %param.15) | copy-start | bytes 292
  7.0 10.4 %collective-permute-start.1 = (f32[96,256]{1,0:T(8,128)S(1)}, f32[96,256]{1,0:T(8,128)S(1)}, u32[]{:S(2)}, u32[]{:S(2)}) collective-permute-start(f32[96,256]{1,0:T(8,128)S(1)} %get-tuple-element.33), channel_id=1, source_target_pairs={{12,0},{0,4},{4,8},{8,12},{13,1},{1,5},{5,9},{9,13},{14,2},{2,6},{... | collective-permute-start | bytes 294920 | tf_op jit(solution)/shard_map/ppermute | solution.py:25
  8.6 3.3 %collective-permute-start = (f32[48,128]{1,0:T(8,128)S(1)}, f32[48,128]{1,0:T(8,128)S(1)}, u32[]{:S(2)}, u32[]{:S(2)}) collective-permute-start(f32[48,128]{1,0:T(8,128)S(1)} %get-tuple-element.30), channel_id=1, source_target_pairs={{3,0},{0,1},{1,2},{2,3},{7,4},{4,5},{5,6},{6,7},{11,8},{8,9},{9,10... | collective-permute-start | bytes 73736 | tf_op jit(solution)/shard_map/ppermute | solution.py:25
  8.6 10.8 %collective-permute-start.6 = (f32[48,512]{1,0:T(8,128)S(1)}, f32[48,512]{1,0:T(8,128)S(1)}, u32[]{:S(2)}, u32[]{:S(2)}) collective-permute-start(f32[48,512]{1,0:T(8,128)S(1)} %get-tuple-element.45), channel_id=1, source_target_pairs={{8,0},{12,4},{0,8},{4,12},{9,1},{13,5},{1,9},{5,13},{10,2},{14,6},... | collective-permute-start | bytes 294920 | tf_op jit(solution)/shard_map/ppermute | solution.py:25
  9.0 10.4 %collective-permute-start.7 = (f32[96,256]{1,0:T(8,128)S(1)}, f32[96,256]{1,0:T(8,128)S(1)}, u32[]{:S(2)}, u32[]{:S(2)}) collective-permute-start(f32[96,256]{1,0:T(8,128)S(1)} %get-tuple-element.48), channel_id=1, source_target_pairs={{4,0},{8,4},{12,8},{0,12},{5,1},{9,5},{13,9},{1,13},{6,2},{10,6},{... | collective-permute-start | bytes 294920 | tf_op jit(solution)/shard_map/ppermute | solution.py:25
  12.5 12.6 %collective-permute-start.2 = (f32[48,512]{1,0:T(8,128)S(1)}, f32[48,512]{1,0:T(8,128)S(1)}, u32[]{:S(2)}, u32[]{:S(2)}) collective-permute-start(f32[48,512]{1,0:T(8,128)S(1)} %get-tuple-element.38), channel_id=1, source_target_pairs={{8,0},{12,4},{0,8},{4,12},{9,1},{13,5},{1,9},{5,13},{10,2},{14,6},... | collective-permute-start | bytes 294920 | tf_op jit(solution)/shard_map/ppermute | solution.py:25
  15.5 9.5 %collective-permute-start.4 = (f32[48,256]{1,0:T(8,128)S(1)}, f32[48,256]{1,0:T(8,128)S(1)}, u32[]{:S(2)}, u32[]{:S(2)}) collective-permute-start(f32[48,256]{1,0:T(8,128)S(1)} %get-tuple-element.41), channel_id=1, source_target_pairs={{12,0},{0,4},{4,8},{8,12},{13,1},{1,5},{5,9},{9,13},{14,2},{2,6},{... | collective-permute-start | bytes 147464 | tf_op jit(solution)/shard_map/ppermute | solution.py:25
  17.4 7.7 %collective-permute-start.5 = (f32[48,256]{1,0:T(8,128)S(1)}, f32[48,256]{1,0:T(8,128)S(1)}, u32[]{:S(2)}, u32[]{:S(2)}) collective-permute-start(f32[48,256]{1,0:T(8,128)S(1)} %get-tuple-element.42), channel_id=1, source_target_pairs={{4,0},{8,4},{12,8},{0,12},{5,1},{9,5},{13,9},{1,13},{6,2},{10,6},{... | collective-permute-start | bytes 147464 | tf_op jit(solution)/shard_map/ppermute | solution.py:25

commit v14 on v13

--- a/solution.py
+++ b/solution.py
@@ -113,10 +113,12 @@
         pltpu.make_async_copy(sources[f].at[pl.ds(0, early), :], held.at[f, pl.ds(0, early), :], sems.at[FIELDS + f])
         for f in range(FIELDS)
     ]
-    for copy in small + needed + others:
+    for copy in needed + small:
         copy.start()
     for copy in small:
         copy.wait()
+    for copy in others:
+        copy.start()
     lane = lax.broadcasted_iota(jnp.int32, rows_ref.shape, 1)
     columns = {}
     for slot in range(rows_ref.shape[0]):

time: 26.4 us -> 26.9 us (1.019)
  Pallas kernels: 7.45 us -> 7.92 us
    pallas_call x1, Pallas kernels: 1.44 us -> 1.91 us  [per_device(): pl.pallas_call(functools.partial(first_kernel, lead, wide, cell_blocks),...]
where the time goes in v14:
time: 26.9 us; the launch traced here: 26.7 us
  starting transfers between devices  13.2 us (49%)
  Pallas kernels  7.92 us (29%)
  waiting for transfers between devices  4.89 us (18%)
  between operations  0.7 us (3%)
    ppermute x8, starting transfers between devices, shift_along(): lax.ppermute(block, axis, [((i - distance) % size, i) for i in range(size)])  13.2 us
    ppermute x8, waiting for transfers between devices, shift_along(): lax.ppermute(block, axis, [((i - distance) % size, i) for i in range(size)])  4.89 us
    pallas_call x2, Pallas kernels, apply(): pl.pallas_call(functools.partial(apply_kernel, part, received, cell_block...  2.68 us
    pallas_call x1, Pallas kernels, per_device(): pl.pallas_call(functools.partial(local_kernel, (most, late), cell_blocks)...  1.94 us
    pallas_call x1, Pallas kernels, per_device(): pl.pallas_call(functools.partial(first_kernel, lead, wide, cell_blocks),...  1.91 us
    pallas_call x1, Pallas kernels, per_device(): pl.pallas_call(functools.partial(second_kernel, most, middle, wide, other...  0.81 us
    pallas_call x1, Pallas kernels, per_device(): pl.pallas_call(functools.partial(third_kernel, late, wide, others, cell_b...  0.57 us
  transfers between devices with their start and end apart: 8, of which 2 were waited for; matrix products, arithmetic and copies ran while one was open for 0% of the time, Pallas kernels for 18%

profile of v14, /device:TPU:0, one launch (start us, length us, event | category | flops | bytes accessed | tf_op | source)
XLA Modules:
  0.0 26.7 jit_solution(2779059747860579012)
XLA Ops:
  0.6 1.9 %gather_first.1 = (f32[48,512]{1,0:T(8,128)S(1)}, f32[3,384,128]{2,1,0:T(8,128)S(1)}, s32[4,256]{1,0:T(4,128)S(1)}, f32[48,128]{1,0:T(8,128)S(1)}) custom-call(f32[384,128]{1,0:T(8,128)} %bitcast.39, f32[384,128]{1,0:T(8,128)} %bitcast.40, f32[384,128]{1,0:T(8,128)} %bitcast.41, s32[4,256]{1,0:T(4,128)} %bitcast.42, s32[1,4]{1,0:T(1,128)} %refs_4_.1), custom_call_target="tpu_custom_call" | custom-call | flops 100663296 | bytes 1179648 | tf_op jit(solution)/shard_map/gather_first/pallas_call | solution.py:322
  2.6 4.1 %collective-permute-start.3 = (f32[48,512]{1,0:T(8,128)S(1)}, f32[48,512]{1,0:T(8,128)S(1)}, u32[]{:S(2)}, u32[]{:S(2)}) collective-permute-start(f32[48,512]{1,0:T(8,128)S(1)} %get-tuple-element.40), channel_id=1, source_target_pairs={{8,0},{12,4},{0,8},{4,12},{9,1},{13,5},{1,9},{5,13},{10,2},{14,6},... | collective-permute-start | bytes 294920 | tf_op jit(solution)/shard_map/ppermute | solution.py:25
  6.7 0.8 %gather_second.1 = (f32[48,512]{1,0:T(8,128)S(1)}, f32[96,256]{1,0:T(8,128)S(1)}, f32[96,256]{1,0:T(8,128)S(1)}, bf16[8,192,128]{2,1,0:T(8,128)(2,1)S(1)}) custom-call(f32[3,384,128]{2,1,0:T(8,128)S(1)} %get-tuple-element.29.held, s32[4,256]{1,0:T(4,128)S(1)} %get-tuple-element.31.listed), custom_call_target="tpu_custom_call" | custom-call | flops 402653184 | bytes 1179648 | tf_op jit(solution)/shard_map/gather_second/pallas_call | solution.py:342
  7.5 0.0 copy-start
  7.5 1.6 %collective-permute-start.1 = (f32[96,256]{1,0:T(8,128)S(1)}, f32[96,256]{1,0:T(8,128)S(1)}, u32[]{:S(2)}, u32[]{:S(2)}) collective-permute-start(f32[96,256]{1,0:T(8,128)S(1)} %get-tuple-element.33), channel_id=1, source_target_pairs={{12,0},{0,4},{4,8},{8,12},{13,1},{1,5},{5,9},{9,13},{14,2},{2,6},{... | collective-permute-start | bytes 294920 | tf_op jit(solution)/shard_map/ppermute | solution.py:25
  9.1 0.0 collective-permute-start
  9.1 0.3 %collective-permute-start.6 = (f32[48,512]{1,0:T(8,128)S(1)}, f32[48,512]{1,0:T(8,128)S(1)}, u32[]{:S(2)}, u32[]{:S(2)}) collective-permute-start(f32[48,512]{1,0:T(8,128)S(1)} %get-tuple-element.45), channel_id=1, source_target_pairs={{8,0},{12,4},{0,8},{4,12},{9,1},{13,5},{1,9},{5,13},{10,2},{14,6},... | collective-permute-start | bytes 294920 | tf_op jit(solution)/shard_map/ppermute | solution.py:25
  9.5 2.2 %collective-permute-start.7 = (f32[96,256]{1,0:T(8,128)S(1)}, f32[96,256]{1,0:T(8,128)S(1)}, u32[]{:S(2)}, u32[]{:S(2)}) collective-permute-start(f32[96,256]{1,0:T(8,128)S(1)} %get-tuple-element.48), channel_id=1, source_target_pairs={{4,0},{8,4},{12,8},{0,12},{5,1},{9,5},{13,9},{1,13},{6,2},{10,6},{... | collective-permute-start | bytes 294920 | tf_op jit(solution)/shard_map/ppermute | solution.py:25
  11.6 0.7 %collective-permute-done.prev = f32[48,128]{1,0:T(8,128)S(1)} collective-permute-done((f32[48,128]{1,0:T(8,128)S(1)}, f32[48,128]{1,0:T(8,128)S(1)}, u32[]{:S(2)}, u32[]{:S(2)}) %collective-permute-start) | collective-permute-done | bytes 24608 | tf_op jit(solution)/shard_map/ppermute | solution.py:25
  12.4 0.6 %gather_third.1 = (f32[48,512]{1,0:T(8,128)S(1)}, f32[48,256]{1,0:T(8,128)S(1)}, f32[48,256]{1,0:T(8,128)S(1)}, bf16[8,96,128]{2,1,0:T(8,128)(2,1)S(1)}) custom-call(f32[3,384,128]{2,1,0:T(8,128)S(1)} %get-tuple-element.29.held, f32[48,128]{1,0:T(8,128)S(1)} %collective-permute-done.prev, s32[4,256]{1,0:T(4,128)S(1)} %get-tuple-element.31.listed), custom_call_target="tpu_custom_call" | custom-call | flops 201326592 | bytes 1179648 | tf_op jit(solution)/shard_map/gather_third/pallas_call | solution.py:355
  12.9 1.1 %collective-permute-start.2 = (f32[48,512]{1,0:T(8,128)S(1)}, f32[48,512]{1,0:T(8,128)S(1)}, u32[]{:S(2)}, u32[]{:S(2)}) collective-permute-start(f32[48,512]{1,0:T(8,128)S(1)} %get-tuple-element.38), channel_id=1, source_target_pairs={{8,0},{12,4},{0,8},{4,12},{9,1},{13,5},{1,9},{5,13},{10,2},{14,6},... | collective-permute-start | bytes 294920 | tf_op jit(solution)/shard_map/ppermute | solution.py:25
  14.0 1.9 %local_terms.1 = (f32[8,96,128]{2,1,0:T(8,128)S(1)}, f32[8,48,128]{2,1,0:T(8,128)S(1)}, bf16[8,384,256]{2,1,0:T(8,128)(2,1)S(1)}) custom-call(f32[3,384,128]{2,1,0:T(8,128)S(1)} %get-tuple-element.29.held, f32[48,128]{1,0:T(8,128)S(1)} %collective-permute-done.prev, f32[8,128]{1,0:T(8,128)} %bitcast.43, f32[8,128]{1,0:T(8,128)} %bitcast.44, ...), custom_call_target="tpu_custom_call" | custom-call | flops 8847360 | bytes 3145728 | tf_op jit(solution)/shard_map/local_terms/pallas_call | solution.py:365
  16.0 0.0 collective-permute-done.3.refs_5_
  16.0 1.8 %collective-permute-start.4 = (f32[48,256]{1,0:T(8,128)S(1)}, f32[48,256]{1,0:T(8,128)S(1)}, u32[]{:S(2)}, u32[]{:S(2)}) collective-permute-start(f32[48,256]{1,0:T(8,128)S(1)} %get-tuple-element.41), channel_id=1, source_target_pairs={{12,0},{0,4},{4,8},{8,12},{13,1},{1,5},{5,9},{9,13},{14,2},{2,6},{... | collective-permute-start | bytes 147464 | tf_op jit(solution)/shard_map/ppermute | solution.py:25
  17.8 0.0 collective-permute-done.1.refs_6_
  17.8 2.0 %collective-permute-start.5 = (f32[48,256]{1,0:T(8,128)S(1)}, f32[48,256]{1,0:T(8,128)S(1)}, u32[]{:S(2)}, u32[]{:S(2)}) collective-permute-start(f32[48,256]{1,0:T(8,128)S(1)} %get-tuple-element.42), channel_id=1, source_target_pairs={{4,0},{8,4},{12,8},{0,12},{5,1},{9,5},{13,9},{1,13},{6,2},{10,6},{... | collective-permute-start | bytes 147464 | tf_op jit(solution)/shard_map/ppermute | solution.py:25
  19.9 0.0 collective-permute-done.6.refs_4_
  19.9 0.0 collective-permute-done.7.refs_7_
  19.9 0.0 copy-done
  19.9 1.5 %apply_tiles.2 = (f32[384,128]{1,0:T(8,128)}, f32[384,128]{1,0:T(8,128)}, f32[384,128]{1,0:T(8,128)}) custom-call(s32[3,8]{1,0:T(4,128)S(1)} %bitcast.34, bf16[8,384,256]{2,1,0:T(8,128)(2,1)S(1)} %get-tuple-element.35.refs_1_, f32[8,96,128]{2,1,0:T(8,128)S(1)} %get-tuple-element.43.refs_2_, bf16[8,192,128]{2,1,0:T(8,128)(2,1)S(1)} %get-tuple-element.44.refs_3_, ...), custom_call_target="tpu_custom_call" | custom-call | flops 301989888 | bytes 1572864 | tf_op jit(solution)/shard_map/apply_tiles/pallas_call | solution.py:395
  21.4 4.1 %collective-permute-done.2.refs_4_ = f32[48,512]{1,0:T(8,128)S(1)} collective-permute-done((f32[48,512]{1,0:T(8,128)S(1)}, f32[48,512]{1,0:T(8,128)S(1)}, u32[]{:S(2)}, u32[]{:S(2)}) %collective-permute-start.2) | collective-permute-done | bytes 98336 | tf_op jit(solution)/shard_map/ppermute | solution.py:25
  25.5 0.0 collective-permute-done.4.refs_5_
  25.5 0.0 collective-permute-done.5.refs_6_
  25.5 1.2 %apply_tiles.3 = (f32[384,128]{1,0:T(8,128)}, f32[384,128]{1,0:T(8,128)}, f32[384,128]{1,0:T(8,128)}) custom-call(s32[3,8]{1,0:T(4,128)S(1)} %bitcast.35, bf16[8,384,256]{2,1,0:T(8,128)(2,1)S(1)} %get-tuple-element.35.refs_1_, f32[8,48,128]{2,1,0:T(8,128)S(1)} %get-tuple-element.36.refs_2_, ...), custom_call_target="tpu_custom_call", output_to_operand_aliasing={{0}: (7, {}), {1}: (8, {}), {2}: (9, {})} | custom-call | flops 150994944 | bytes 786432 | tf_op jit(solution)/shard_map/apply_tiles/pallas_call | solution.py:395
Async XLA Ops:
  2.6 13.4 %collective-permute-start.3 = (f32[48,512]{1,0:T(8,128)S(1)}, f32[48,512]{1,0:T(8,128)S(1)}, u32[]{:S(2)}, u32[]{:S(2)}) collective-permute-start(f32[48,512]{1,0:T(8,128)S(1)} %get-tuple-element.40), channel_id=1, source_target_pairs={{8,0},{12,4},{0,8},{4,12},{9,1},{13,5},{1,9},{5,13},{10,2},{14,6},... | collective-permute-start | bytes 294920 | tf_op jit(solution)/shard_map/ppermute | solution.py:25
  7.5 12.4 %copy-start = (s32[8,3]{0,1:T(4,128)S(1)}, s32[8,3]{0,1:T(4,128)}, u32[]{:S(2)}) copy-start(s32[8,3]{0,1:T(4,128)} %param.15) | copy-start | bytes 292
  7.5 10.4 %collective-permute-start.1 = (f32[96,256]{1,0:T(8,128)S(1)}, f32[96,256]{1,0:T(8,128)S(1)}, u32[]{:S(2)}, u32[]{:S(2)}) collective-permute-start(f32[96,256]{1,0:T(8,128)S(1)} %get-tuple-element.33), channel_id=1, source_target_pairs={{12,0},{0,4},{4,8},{8,12},{13,1},{1,5},{5,9},{9,13},{14,2},{2,6},{... | collective-permute-start | bytes 294920 | tf_op jit(solution)/shard_map/ppermute | solution.py:25
  9.1 3.3 %collective-permute-start = (f32[48,128]{1,0:T(8,128)S(1)}, f32[48,128]{1,0:T(8,128)S(1)}, u32[]{:S(2)}, u32[]{:S(2)}) collective-permute-start(f32[48,128]{1,0:T(8,128)S(1)} %get-tuple-element.30), channel_id=1, source_target_pairs={{3,0},{0,1},{1,2},{2,3},{7,4},{4,5},{5,6},{6,7},{11,8},{8,9},{9,10... | collective-permute-start | bytes 73736 | tf_op jit(solution)/shard_map/ppermute | solution.py:25
  9.1 10.8 %collective-permute-start.6 = (f32[48,512]{1,0:T(8,128)S(1)}, f32[48,512]{1,0:T(8,128)S(1)}, u32[]{:S(2)}, u32[]{:S(2)}) collective-permute-start(f32[48,512]{1,0:T(8,128)S(1)} %get-tuple-element.45), channel_id=1, source_target_pairs={{8,0},{12,4},{0,8},{4,12},{9,1},{13,5},{1,9},{5,13},{10,2},{14,6},... | collective-permute-start | bytes 294920 | tf_op jit(solution)/shard_map/ppermute | solution.py:25
  9.5 10.4 %collective-permute-start.7 = (f32[96,256]{1,0:T(8,128)S(1)}, f32[96,256]{1,0:T(8,128)S(1)}, u32[]{:S(2)}, u32[]{:S(2)}) collective-permute-start(f32[96,256]{1,0:T(8,128)S(1)} %get-tuple-element.48), channel_id=1, source_target_pairs={{4,0},{8,4},{12,8},{0,12},{5,1},{9,5},{13,9},{1,13},{6,2},{10,6},{... | collective-permute-start | bytes 294920 | tf_op jit(solution)/shard_map/ppermute | solution.py:25
  12.9 12.6 %collective-permute-start.2 = (f32[48,512]{1,0:T(8,128)S(1)}, f32[48,512]{1,0:T(8,128)S(1)}, u32[]{:S(2)}, u32[]{:S(2)}) collective-permute-start(f32[48,512]{1,0:T(8,128)S(1)} %get-tuple-element.38), channel_id=1, source_target_pairs={{8,0},{12,4},{0,8},{4,12},{9,1},{13,5},{1,9},{5,13},{10,2},{14,6},... | collective-permute-start | bytes 294920 | tf_op jit(solution)/shard_map/ppermute | solution.py:25
  16.0 9.5 %collective-permute-start.4 = (f32[48,256]{1,0:T(8,128)S(1)}, f32[48,256]{1,0:T(8,128)S(1)}, u32[]{:S(2)}, u32[]{:S(2)}) collective-permute-start(f32[48,256]{1,0:T(8,128)S(1)} %get-tuple-element.41), channel_id=1, source_target_pairs={{12,0},{0,4},{4,8},{8,12},{13,1},{1,5},{5,9},{9,13},{14,2},{2,6},{... | collective-permute-start | bytes 147464 | tf_op jit(solution)/shard_map/ppermute | solution.py:25
  17.8 7.7 %collective-permute-start.5 = (f32[48,256]{1,0:T(8,128)S(1)}, f32[48,256]{1,0:T(8,128)S(1)}, u32[]{:S(2)}, u32[]{:S(2)}) collective-permute-start(f32[48,256]{1,0:T(8,128)S(1)} %get-tuple-element.42), channel_id=1, source_target_pairs={{4,0},{8,4},{12,8},{0,12},{5,1},{9,5},{13,9},{1,13},{6,2},{10,6},{... | collective-permute-start | bytes 147464 | tf_op jit(solution)/shard_map/ppermute | solution.py:25
